TPU v7x, 32 devices: a whole 2x2x4 slice. The times are simulated.
32 devices in a mesh: cfg: 2 (over x), pr: 16 (over z, y, core).
Axes of the slice: x: 2, y: 2, z: 4, core: 2. Of those that a mesh axis runs over, the one named last changes fastest.
Arguments:
- sep_inv: float32 [4096, 2048], P(('cfg', 'pr')), parts along dimension 0, as said below
- factor: float32 [1024, 65536], P('cfg', 'pr'), parts along dimension 0, may hold values from -0.5 to 0.5
- widths: int32 [16, 8], P('pr'), may hold values from 1 to 8, 32 in all within a row
- patterns: int32 [128, 4], P('pr'), may hold values from 0 to 15, all different within a row; in each aligned block of 8 rows (0 to 7, 8 to 15, ...) at most 2 rows name the same one
- dinv: float32 [131072], P(('cfg', 'pr')), parts along dimension 0, may hold values from 2 to 20
Outputs:
- sel_offdiag: float32 [1024, 65536], P('cfg', 'pr'), parts along dimension 0
- marg_var: float32 [131072], P(('cfg', 'pr')), parts along dimension 0
There are 2 independent parts, one for each index of `cfg`. A program takes and returns all parts, laid end to end along the dimension named above; an argument that names none is the same for every part. Nothing has to cross between parts.
Inputs may be any that keep to these rules, and one draw needn't show every extreme that they name: sep_inv is symmetric. `widths`: each aligned block of 8 entries of one index of pr sums to 32, and its largest is 8. `patterns`: each row names 4 different separator tiles; among the 8 rows of one index of pr no tile is named more than 2 times, and on some index a tile is named exactly 2 times.
All inputs are finite; a program needn't handle non-finite values.
Results may differ from a plain program's by a relative error of at most 0.0003.
Values sent between devices are 32-bit elements; how exact they have to be, the bound alone decides.
No kernel may reach another device: no remote copies, remote signals or barrier semaphores. Data moves between devices by JAX's collectives and lax.ppermute only.
A program may use at most 128 MiB of HBM per device.

v0:
```python
import jax
import jax.numpy as jnp
from jax import lax
from jax.sharding import PartitionSpec as P

TILE = 128
P_SIZE = 4
WMAX = 8
TILES_DEV = 32
NS = 8
PT = 512


def cut_block(whole_inv, tile_row):
    row_tiles = [
        lax.dynamic_slice_in_dim(whole_inv, tile_row[a] * TILE, TILE, 0) for a in range(P_SIZE)
    ]
    rows_part = jnp.concatenate(row_tiles, axis=0)
    col_tiles = [
        lax.dynamic_slice_in_dim(rows_part, tile_row[a] * TILE, TILE, 1) for a in range(P_SIZE)
    ]
    return jnp.concatenate(col_tiles, axis=1)


def shards(sep_inv, factor, widths, patterns, dinv):
    whole_inv = lax.all_gather(sep_inv, "pr", axis=0, tiled=True)

    def pick_block(tile_row):
        return cut_block(whole_inv, tile_row)

    blocks = lax.map(pick_block, patterns)
    node_widths = widths.reshape(NS)
    tile_ends = jnp.cumsum(node_widths)
    tile_starts = tile_ends - node_widths
    window_cols = WMAX * TILE
    window_ids = jnp.arange(WMAX, dtype=jnp.int32)

    def one_node(node, output):
        start = tile_starts[node]
        first = jnp.minimum(start, TILES_DEV - WMAX)
        factor_part = lax.dynamic_slice_in_dim(factor, first * TILE, window_cols, 1)
        block = lax.dynamic_index_in_dim(blocks, node, 0, keepdims=False)
        product = -jnp.dot(
            block, factor_part, precision=lax.Precision.HIGHEST, preferred_element_type=jnp.float32
        )
        tile_pos = first + window_ids
        inside = (tile_pos >= start) & (tile_pos < tile_ends[node])
        old_part = lax.dynamic_slice_in_dim(output, first * TILE, window_cols, 1)
        merged = jnp.where(
            inside[None, :, None], product.reshape(PT, WMAX, TILE), old_part.reshape(PT, WMAX, TILE)
        )
        return lax.dynamic_update_slice_in_dim(
            output, merged.reshape(PT, window_cols), first * TILE, 1
        )

    sel_offdiag = lax.fori_loop(0, NS, one_node, jnp.zeros((PT, TILES_DEV * TILE), jnp.float32))
    variance = dinv - jnp.sum(factor * sel_offdiag, axis=0)
    return (sel_offdiag, variance)


def solution(mesh):
    placed = (
        P(("cfg", "pr"), None),
        P("cfg", "pr"),
        P("pr", None),
        P("pr", None),
        P(("cfg", "pr")),
    )
    return jax.shard_map(
        shards,
        mesh=mesh,
        in_specs=placed,
        out_specs=(P("cfg", "pr"), P(("cfg", "pr"))),
        check_vma=False,
    )
```

profile of v0, /device:TPU:0, one launch (start us, length us, event | category | flops | bytes accessed | tf_op | source)
XLA Modules:
  0.0 308.8 jit_solution(699605395400771136)
XLA Ops:
  9.4 130.4 %all-gather.2.cloned.1.call-done = f32[2048,2048]{1,0:T(8,128)} async-done(((f32[128,2048]{1,0:T(8,128)}), f32[2048,2048]{1,0:T(8,128)}) %all-gather.2.cloned.1.call-update) | async-done | bytes 16777232 | tf_op jit(solution)/shard_map/all_gather | solution.py:26
  139.8 65.9 %while.24 = (s32[]{:T(128)}, f32[8,512,512]{2,1,0:T(8,128)}, s32[8,4]{0,1:T(4,128)}, f32[2048,2048]{1,0:T(8,128)}, s32[]{:T(128)}, /*index=5*/s32[1,1]{0,1:T(1,128)}, s32[]{:T(128)}, s32[]{:T(128)}) while((s32[]{:T(128)}, f32[8,512,512]{2,1,0:T(8,128)}, s32[8,4]{0,1:T(4,128)}, f32[2048,2048]{1,0:T(8,128)}, s32[]{:T(128)}, ...), condition=%wide.region_2.3_spmd, body=%wide.region_1.2_spmd.sunk | while | flops 3932178 | bytes 20972400 | solution.py:31
  143.6 2.7 constant_dynamic-slice_fusion.13
  151.8 2.7 constant_dynamic-slice_fusion.13
  160.1 2.7 constant_dynamic-slice_fusion.13
  168.3 2.7 constant_dynamic-slice_fusion.13
  176.6 2.7 constant_dynamic-slice_fusion.13
  184.8 2.7 constant_dynamic-slice_fusion.13
  193.0 2.7 constant_dynamic-slice_fusion.13
  201.2 2.7 constant_dynamic-slice_fusion.13
  205.6 4.4 %broadcast_in_dim.33 = f32[512,4096]{1,0:T(8,128)} broadcast(f32[]{:T(128)} %constant.70.clone.1), dimensions={} | broadcast | bytes 8388612 | tf_op jit(solution)/shard_map/broadcast_in_dim | solution.py:56
  210.1 84.5 %while.25 = (s32[]{:T(128)}, f32[512,4096]{1,0:T(8,128)}, s32[8]{0:T(128)S(1)}, s32[8]{0:T(128)S(1)}, f32[8,512,512]{2,1,0:T(8,128)}, /*index=5*/f32[512,4096]{1...) while((s32[]{:T(128)}, f32[512,4096]{1,0:T(8,128)}, ...), condition=%wide.region_4.5_spmd.clone, body=%wide.region_3.4_spmd.clone.sunk | while | flops 3222274048 | bytes 7343835 | solution.py:56
  213.2 7.4 %select_dynamic-update-slice_fusion.2 = f32[512,4096]{1,0:T(8,128)} fusion(f32[512,4096]{1,0:T(8,128)} %get-tuple-element.318, s32[]{:T(128)S(6)} %select_n.56, f32[512,4096]{1,0:T(8,128)} %get-tuple-element.333, f32[8,512,512]{2,1,0:T(8,128)} %get-tuple-element.332, s32[]{:T(128)} %get-tuple-element.317, ...), kind=kOutput, calls=%fused_computation.13.clone.1 | convolution fusion | flops 3222274048 | bytes 7342592 | tf_op jit(solution)/shard_map/while/body/eval_jaxpr/dot_general | solution.py:43
  223.8 7.4 %select_dynamic-update-slice_fusion.2 = f32[512,4096]{1,0:T(8,128)} fusion(f32[512,4096]{1,0:T(8,128)} %get-tuple-element.318, s32[]{:T(128)S(6)} %select_n.56, f32[512,4096]{1,0:T(8,128)} %get-tuple-element.333, f32[8,512,512]{2,1,0:T(8,128)} %get-tuple-element.332, s32[]{:T(128)} %get-tuple-element.317, ...), kind=kOutput, calls=%fused_computation.13.clone.1 | convolution fusion | flops 3222274048 | bytes 7342592 | tf_op jit(solution)/shard_map/while/body/eval_jaxpr/dot_general | solution.py:43
  234.3 7.4 %select_dynamic-update-slice_fusion.2 = f32[512,4096]{1,0:T(8,128)} fusion(f32[512,4096]{1,0:T(8,128)} %get-tuple-element.318, s32[]{:T(128)S(6)} %select_n.56, f32[512,4096]{1,0:T(8,128)} %get-tuple-element.333, f32[8,512,512]{2,1,0:T(8,128)} %get-tuple-element.332, s32[]{:T(128)} %get-tuple-element.317, ...), kind=kOutput, calls=%fused_computation.13.clone.1 | convolution fusion | flops 3222274048 | bytes 7342592 | tf_op jit(solution)/shard_map/while/body/eval_jaxpr/dot_general | solution.py:43
  243.6 1.2 compare_and_fusion.2
  244.9 7.4 %select_dynamic-update-slice_fusion.2 = f32[512,4096]{1,0:T(8,128)} fusion(f32[512,4096]{1,0:T(8,128)} %get-tuple-element.318, s32[]{:T(128)S(6)} %select_n.56, f32[512,4096]{1,0:T(8,128)} %get-tuple-element.333, f32[8,512,512]{2,1,0:T(8,128)} %get-tuple-element.332, s32[]{:T(128)} %get-tuple-element.317, ...), kind=kOutput, calls=%fused_computation.13.clone.1 | convolution fusion | flops 3222274048 | bytes 7342592 | tf_op jit(solution)/shard_map/while/body/eval_jaxpr/dot_general | solution.py:43
  254.2 1.2 compare_and_fusion.2
  255.5 7.4 %select_dynamic-update-slice_fusion.2 = f32[512,4096]{1,0:T(8,128)} fusion(f32[512,4096]{1,0:T(8,128)} %get-tuple-element.318, s32[]{:T(128)S(6)} %select_n.56, f32[512,4096]{1,0:T(8,128)} %get-tuple-element.333, f32[8,512,512]{2,1,0:T(8,128)} %get-tuple-element.332, s32[]{:T(128)} %get-tuple-element.317, ...), kind=kOutput, calls=%fused_computation.13.clone.1 | convolution fusion | flops 3222274048 | bytes 7342592 | tf_op jit(solution)/shard_map/while/body/eval_jaxpr/dot_general | solution.py:43
  264.7 1.2 compare_and_fusion.2
  266.1 7.4 %select_dynamic-update-slice_fusion.2 = f32[512,4096]{1,0:T(8,128)} fusion(f32[512,4096]{1,0:T(8,128)} %get-tuple-element.318, s32[]{:T(128)S(6)} %select_n.56, f32[512,4096]{1,0:T(8,128)} %get-tuple-element.333, f32[8,512,512]{2,1,0:T(8,128)} %get-tuple-element.332, s32[]{:T(128)} %get-tuple-element.317, ...), kind=kOutput, calls=%fused_computation.13.clone.1 | convolution fusion | flops 3222274048 | bytes 7342592 | tf_op jit(solution)/shard_map/while/body/eval_jaxpr/dot_general | solution.py:43
  276.6 7.4 %select_dynamic-update-slice_fusion.2 = f32[512,4096]{1,0:T(8,128)} fusion(f32[512,4096]{1,0:T(8,128)} %get-tuple-element.318, s32[]{:T(128)S(6)} %select_n.56, f32[512,4096]{1,0:T(8,128)} %get-tuple-element.333, f32[8,512,512]{2,1,0:T(8,128)} %get-tuple-element.332, s32[]{:T(128)} %get-tuple-element.317, ...), kind=kOutput, calls=%fused_computation.13.clone.1 | convolution fusion | flops 3222274048 | bytes 7342592 | tf_op jit(solution)/shard_map/while/body/eval_jaxpr/dot_general | solution.py:43
  287.2 7.4 %select_dynamic-update-slice_fusion.2 = f32[512,4096]{1,0:T(8,128)} fusion(f32[512,4096]{1,0:T(8,128)} %get-tuple-element.318, s32[]{:T(128)S(6)} %select_n.56, f32[512,4096]{1,0:T(8,128)} %get-tuple-element.333, f32[8,512,512]{2,1,0:T(8,128)} %get-tuple-element.332, s32[]{:T(128)} %get-tuple-element.317, ...), kind=kOutput, calls=%fused_computation.13.clone.1 | convolution fusion | flops 3222274048 | bytes 7342592 | tf_op jit(solution)/shard_map/while/body/eval_jaxpr/dot_general | solution.py:43
  294.6 6.7 %multiply_reduce_fusion = f32[4096]{0:T(1024)S(1)} fusion(f32[512,4096]{1,0:T(8,128)} %get-tuple-element.340, f32[512,4096]{1,0:T(8,128)} %get-tuple-element.146), kind=kLoop, calls=%fused_computation.22 | loop fusion | flops 4190208 | bytes 16793600 | tf_op jit(solution)/shard_map/reduce_sum | solution.py:57
  (77 shorter events, 43.5 us)
Async XLA Ops:
  7.2 132.6 %all-gather.2.cloned.1.call-start = ((), (), s32[]{:S(2)}) async-start(), calls=%async_computation | async-start | bytes 17825792 | tf_op jit(solution)/shard_map/all_gather | solution.py:26
  294.6 6.7 %copy-start = (f32[4096]{0:T(1024)S(1)}, f32[4096]{0:T(1024)}, u32[]{:S(2)}) copy-start(f32[4096]{0:T(1024)} %param.13) | copy-start | bytes 49156
Sparse Core Ops, SparseCore 0:
  10.2 129.5 all-gather.1
where the time goes:
time: 310 us; the launch traced here: 309 us
  waiting for transfers between devices  131 us (42%)
  matrix products  59.4 us (19%)
  local copies, waits for them, and re-layouts  47.9 us (15%)
  other arithmetic  31.1 us (10%)
  loops' own time  25.2 us (8%)
  between operations  14 us (5%)
    all_gather x1, waiting for transfers between devices, shards(): whole_inv = lax.all_gather(sep_inv, 'pr', axis=0, tiled=True)  130 us
    dot_general x8, matrix products, one_node(): jnp.dot(block, factor_part, precision=lax.Precision.HIGHEST, preferred_el...  59.4 us
    dynamic_slice x8, local copies, waits for them, and re-layouts, cut_block(): lax.dynamic_slice_in_dim(whole_inv, tile_row[a] * TILE, TILE, 0)  21.4 us
    another operation x1, loops' own time, shards(): blocks = lax.map(pick_block, patterns)  20.2 us
    and x8, other arithmetic, one_node(): inside = (tile_pos >= start) & (tile_pos < tile_ends[node])  9.83 us
    dynamic_update_slice x8, other arithmetic, shards(): blocks = lax.map(pick_block, patterns)  8.54 us
    reduce_sum x1, other arithmetic, shards(): variance = dinv - jnp.sum(factor * sel_offdiag, axis=0)  6.68 us
  transfers between devices with their start and end apart: 1, of which 1 were waited for; matrix products, arithmetic and copies ran while one was open for 0% of the time, Pallas kernels for 0%

commit v1 on v0

v1 whole, which is shorter than its diff:
```python
import functools

import jax
import jax.numpy as jnp
from jax import lax
from jax.experimental import pallas as pl
from jax.experimental.pallas import tpu as pltpu
from jax.sharding import PartitionSpec as P

TILE = 128
HALF = TILE // 2
MIB = 1024 * 1024


def split(value):
    high = value.astype(jnp.bfloat16)
    low = (value - high.astype(jnp.float32)).astype(jnp.bfloat16)
    return high, low


def pack_kernel(tiles, me_ref, rows_ref, packed_ref):
    me = me_ref[0]
    half = tiles // 2
    for d in range(half):
        col = lax.rem(me + d, tiles) * TILE
        packed_ref[d * TILE : (d + 1) * TILE, :] = rows_ref[:, pl.ds(pl.multiple_of(col, TILE), TILE)]
    col = lax.rem(me + half, tiles) * TILE
    opposite = rows_ref[:, pl.ds(pl.multiple_of(col, TILE), TILE)]

    @pl.when(me < half)
    def _():
        packed_ref[half * TILE :, :] = opposite[:HALF, :]

    @pl.when(me >= half)
    def _():
        packed_ref[half * TILE :, :] = opposite.T[HALF:, :]


def pack(sep_rows, me, tiles):
    return pl.pallas_call(
        functools.partial(pack_kernel, tiles),
        out_shape=jax.ShapeDtypeStruct((tiles * HALF + HALF, TILE), jnp.float32),
        in_specs=[pl.BlockSpec(memory_space=pltpu.SMEM), pl.BlockSpec(memory_space=pltpu.VMEM)],
        out_specs=pl.BlockSpec(memory_space=pltpu.VMEM),
        compiler_params=pltpu.CompilerParams(vmem_limit_bytes=8 * MIB),
        name="pack_share",
    )(me, sep_rows)


def place(high_ref, low_ref, node, a, b, high, low):
    rows = pl.ds(pl.multiple_of(a * TILE, TILE), TILE)
    cols = pl.ds(pl.multiple_of(b * TILE, TILE), TILE)
    high_ref[node, rows, cols] = high
    low_ref[node, rows, cols] = low


def assemble_kernel(tiles, nodes, sides, patterns_ref, packed_ref, high_ref, low_ref):
    half = tiles // 2
    share = tiles * HALF + HALF

    def one(step, _):
        node = step // (sides * sides)
        a = lax.rem(step // sides, sides)
        b = lax.rem(step, sides)
        r = patterns_ref[node, a]
        q = patterns_ref[node, b]
        d = lax.rem(q - r + tiles, tiles)

        @pl.when(d < half)
        def _():
            start = pl.multiple_of(r * share + d * TILE, HALF)
            value = packed_ref[pl.ds(start, TILE), :]
            high, low = split(value)
            place(high_ref, low_ref, node, a, b, high, low)

            @pl.when(d > 0)
            def _():
                high, low = split(value.T)
                place(high_ref, low_ref, node, b, a, high, low)

        @pl.when((d == half) & (r < half))
        def _():
            first = pl.multiple_of(r * share + half * TILE, HALF)
            second = pl.multiple_of(q * share + half * TILE, HALF)
            value = jnp.concatenate([packed_ref[pl.ds(first, HALF), :], packed_ref[pl.ds(second, HALF), :]], axis=0)
            high, low = split(value)
            place(high_ref, low_ref, node, a, b, high, low)
            high, low = split(value.T)
            place(high_ref, low_ref, node, b, a, high, low)

        return 0

    lax.fori_loop(0, nodes * sides * sides, one, 0)


def assemble_full_kernel(nodes, sides, patterns_ref, whole_ref, high_ref, low_ref):
    def one(step, _):
        node = step // (sides * sides)
        a = lax.rem(step // sides, sides)
        b = lax.rem(step, sides)
        rows = pl.ds(pl.multiple_of(patterns_ref[node, a] * TILE, TILE), TILE)
        cols = pl.ds(pl.multiple_of(patterns_ref[node, b] * TILE, TILE), TILE)
        high, low = split(whole_ref[rows, cols])
        place(high_ref, low_ref, node, a, b, high, low)
        return 0

    lax.fori_loop(0, nodes * sides * sides, one, 0)


def assemble(kernel, patterns, source):
    nodes, sides = patterns.shape
    side = sides * TILE
    return pl.pallas_call(
        kernel,
        out_shape=[pltpu.VMEM((nodes, side, side), jnp.bfloat16)] * 2,
        in_specs=[pl.BlockSpec(memory_space=pltpu.SMEM), pl.BlockSpec(memory_space=pltpu.VMEM)],
        out_specs=[pl.BlockSpec(memory_space=pltpu.VMEM)] * 2,
        compiler_params=pltpu.CompilerParams(vmem_limit_bytes=32 * MIB),
        name="assemble_blocks",
    )(patterns, source)


def halves_kernel(factor_ref, high_ref, low_ref):
    high_ref[...], low_ref[...] = split(factor_ref[...])


def factor_halves(factor):
    rows, cols = factor.shape
    step = 512
    spec = pl.BlockSpec((rows, step), lambda i: (0, i))
    return pl.pallas_call(
        halves_kernel,
        grid=(cols // step,),
        out_shape=[jax.ShapeDtypeStruct((rows, cols), jnp.bfloat16)] * 2,
        in_specs=[spec],
        out_specs=[spec] * 2,
        name="factor_halves",
        cost_estimate=pl.CostEstimate(flops=4 * rows * cols, bytes_accessed=8 * rows * cols, transcendentals=0),
    )(factor)


def product_kernel(nodes, widths_ref, high_ref, low_ref, factor_ref, dinv_ref, out_ref, marg_ref):
    pair = pl.program_id(0)

    def node_of(tile):
        node, end = 0, 0
        for j in range(nodes):
            end = end + widths_ref[0, j]
            node = node + (tile >= end).astype(jnp.int32)
        return jnp.minimum(node, nodes - 1)

    first, second = node_of(2 * pair), node_of(2 * pair + 1)

    def columns(node, where):
        factor = factor_ref[:, where]
        f_high, f_low = split(factor)
        high, low = high_ref[node], low_ref[node]
        dot = functools.partial(jnp.dot, preferred_element_type=jnp.float32)
        product = -(dot(high, f_high) + (dot(high, f_low) + dot(low, f_high)))
        out_ref[:, where] = product
        total = jnp.sum(factor * product, axis=0, keepdims=True)
        for k in range(factor.shape[1] // TILE):
            row = pl.ds(2 * pair + where.start // TILE + k, 1)
            marg_ref[row, :] = dinv_ref[row, :] - total[:, k * TILE : (k + 1) * TILE]

    @pl.when(first == second)
    def _():
        columns(first, slice(0, 2 * TILE))

    @pl.when(first != second)
    def _():
        columns(first, slice(0, TILE))
        columns(second, slice(TILE, 2 * TILE))


def products(widths, high, low, factor, dinv):
    rows, cols = factor.shape
    nodes = widths.shape[1]
    whole = pl.BlockSpec(memory_space=pltpu.VMEM)
    spec = pl.BlockSpec((rows, 2 * TILE), lambda i: (0, i))
    out, marg = pl.pallas_call(
        functools.partial(product_kernel, nodes),
        grid=(cols // (2 * TILE),),
        out_shape=[jax.ShapeDtypeStruct((rows, cols), jnp.float32), jax.ShapeDtypeStruct((cols // TILE, TILE), jnp.float32)],
        in_specs=[pl.BlockSpec(memory_space=pltpu.SMEM), whole, whole, spec, whole],
        out_specs=[spec, whole],
        compiler_params=pltpu.CompilerParams(vmem_limit_bytes=40 * MIB),
        name="products",
        cost_estimate=pl.CostEstimate(flops=6 * rows * rows * cols, bytes_accessed=8 * rows * cols, transcendentals=0),
    )(widths, high, low, factor, dinv.reshape(cols // TILE, TILE))
    return out, marg.reshape(cols)


def shards(sep_inv, factor, widths, patterns, dinv):
    own_rows, order = sep_inv.shape
    tiles = order // TILE
    nodes, sides = patterns.shape
    if own_rows == TILE and tiles % 2 == 0:
        me = lax.axis_index("pr").astype(jnp.int32).reshape(1)
        packed = pack(sep_inv, me, tiles)
        gathered = lax.all_gather(packed, "pr", axis=0, tiled=True)
        kernel = functools.partial(assemble_kernel, tiles, nodes, sides)
    else:
        gathered = lax.all_gather(sep_inv, "pr", axis=0, tiled=True)
        kernel = functools.partial(assemble_full_kernel, nodes, sides)
    high, low = assemble(kernel, patterns, gathered)
    return products(widths, high, low, factor, dinv)


def solution(mesh):
    placed = (
        P(("cfg", "pr"), None),
        P("cfg", "pr"),
        P("pr", None),
        P("pr", None),
        P(("cfg", "pr")),
    )
    return jax.shard_map(
        shards,
        mesh=mesh,
        in_specs=placed,
        out_specs=(P("cfg", "pr"), P(("cfg", "pr"))),
        check_vma=False,
    )
```

time: 310 us -> 131 us (0.42)
  matrix products: 59.4 us -> 0 us
  waiting for transfers between devices: 131 us -> 81.7 us
  local copies, waits for them, and re-layouts: 47.9 us -> 5.51 us
  other arithmetic: 31.1 us -> 0 us
  Pallas kernels: 0 us -> 28.4 us
  loops' own time: 25.2 us -> 0 us
    dot_general x8 -> x0, matrix products: 59.4 us -> none  [one_node(): jnp.dot(block, factor_part, precision=lax.Precision.HIGHEST, preferred_el...]
    all_gather x1, waiting for transfers between devices: 130 us -> 81.7 us  [shards(): gathered = lax.all_gather(packed, 'pr', axis=0, tiled=True)]
    dynamic_slice x40 -> x0, local copies, waits for them, and re-layouts: 38.3 us -> none  [the longest x8 21.4 us: cut_block(): lax.dynamic_slice_in_dim(whole_inv, tile_row[a] * TILE, TILE, 0)]
    pallas_call x0 -> x3, Pallas kernels: none -> 28.4 us  [the longest x1 17.4 us: products(): pl.pallas_call(functools.partial(product_kernel, nodes), grid=(cols // (2...]
    another operation x2 -> x0, loops' own time: 25.2 us -> none  [the longest x1 20.2 us: shards(): blocks = lax.map(pick_block, patterns)]
    and x8 -> x0, other arithmetic: 9.83 us -> none  [one_node(): inside = (tile_pos >= start) & (tile_pos < tile_ends[node])]
    dynamic_update_slice x8 -> x0, other arithmetic: 8.54 us -> none  [shards(): blocks = lax.map(pick_block, patterns)]
    reduce_sum x1 -> x0, other arithmetic: 6.68 us -> none  [shards(): variance = dinv - jnp.sum(factor * sel_offdiag, axis=0)]
  transfers between devices with their start and end apart: 1 -> 1, of which waited for: 1 -> 1; matrix products, arithmetic and copies ran while one was open for 0% -> 1% of each run, Pallas kernels for 0% -> 0%
where the time goes in v1:
time: 131 us; the launch traced here: 130 us
  waiting for transfers between devices  81.7 us (62%)
  Pallas kernels  28.4 us (22%)
  between operations  14.1 us (11%)
  local copies, waits for them, and re-layouts  5.51 us (4%)
    all_gather x1, waiting for transfers between devices, shards(): gathered = lax.all_gather(packed, 'pr', axis=0, tiled=True)  81.7 us
    pallas_call x1, Pallas kernels, products(): pl.pallas_call(functools.partial(product_kernel, nodes), grid=(cols // (2...  17.4 us
    pallas_call x1, Pallas kernels, assemble(): pl.pallas_call(kernel, out_shape=[pltpu.VMEM((nodes, side, side), jnp.bfl...  10.2 us
    unnamed x9, local copies, waits for them, and re-layouts  5.51 us
  transfers between devices with their start and end apart: 1, of which 1 were waited for; matrix products, arithmetic and copies ran while one was open for 1% of the time, Pallas kernels for 0%

profile of v1, /device:TPU:0, one launch (start us, length us, event | category | flops | bytes accessed | tf_op | source)
XLA Modules:
  0.0 129.7 jit_solution(3212356275401332025)
XLA Ops:
  7.2 0.0 copy-start.3
  7.2 0.0 all-gather.2.cloned.1.call-start
  7.2 0.0 copy-start.1
  7.2 1.2 copy-done.1
  8.4 0.0 copy-start.2
  8.5 0.9 pack_share.1
  9.3 0.0 all-gather.2.cloned.1.call-update
  9.4 0.8 copy.7.patterns_ref
  10.1 81.7 %all-gather.2.cloned.1.call-done.packed_ref = f32[17408,128]{1,0:T(8,128)} async-done(((f32[1088,128]{1,0:T(8,128)}), f32[17408,128]{1,0:T(8,128)}) %all-gather.2.cloned.1.call-update) | async-done | bytes 8912912 | tf_op jit(solution)/shard_map/all_gather | solution.py:201
  91.8 0.0 copy-start
  91.8 3.5 %copy-done = f32[17408,128]{1,0:T(8,128)S(1)} copy-done((f32[17408,128]{1,0:T(8,128)S(1)}, f32[17408,128]{1,0:T(8,128)}, u32[]{:S(2)}) %copy-start) | copy-done | bytes 8912920
  95.3 10.2 %assemble_blocks.1 = (bf16[8,512,512]{2,1,0:T(8,128)(2,1)S(1)}, bf16[8,512,512]{2,1,0:T(8,128)(2,1)S(1)}) custom-call(s32[8,4]{1,0:T(8,128)S(1)} %copy.7.patterns_ref, f32[17408,128]{1,0:T(8,128)S(1)} %copy-done), custom_call_target="tpu_custom_call" | custom-call | tf_op jit(solution)/shard_map/assemble_blocks/pallas_call | solution.py:113
  105.5 0.0 copy-done.3
  105.5 0.0 copy-done.2
  105.5 17.4 %products.1 = (f32[512,4096]{1,0:T(8,128)}, f32[32,128]{1,0:T(8,128)}) custom-call(s32[1,8]{1,0:T(1,128)S(1)} %copy-done.3, bf16[8,512,512]{2,1,0:T(8,128)(2,1)S(1)} %get-tuple-element.6.high_ref, bf16[8,512,512]{2,1,0:T(8,128)(2,1)S(1)} %get-tuple-element.7.low_ref, f32[512,4096]{1,0:T(8,128)} %factor_ref.1, f32[32,128]{1,0:T(8,128)S(1)} %bitcast.3), custom_call_target="tpu_custom_call" | custom-call | flops 6442450944 | bytes 16777216 | tf_op jit(solution)/shard_map/products/pallas_call | solution.py:181
Async XLA Ops:
  7.2 98.4 %copy-start.3 = (s32[1,8]{1,0:T(1,128)S(1)}, s32[1,8]{1,0:T(1,128)}, u32[]{:S(2)}) copy-start(s32[1,8]{1,0:T(1,128)} %widths_ref.1) | copy-start | bytes 100
  7.2 84.6 %all-gather.2.cloned.1.call-start = ((), (), s32[]{:S(2)}) async-start(), calls=%async_computation | async-start | bytes 9469952 | tf_op jit(solution)/shard_map/all_gather | solution.py:201
  7.2 1.2 copy-start.1
  8.4 97.1 %copy-start.2 = (f32[4096]{0:T(1024)S(1)}, f32[4096]{0:T(1024)}, u32[]{:S(2)}) copy-start(f32[4096]{0:T(1024)} %param.9) | copy-start | bytes 49156
  91.8 3.5 %copy-start = (f32[17408,128]{1,0:T(8,128)S(1)}, f32[17408,128]{1,0:T(8,128)}, u32[]{:S(2)}) copy-start(f32[17408,128]{1,0:T(8,128)} %all-gather.2.cloned.1.call-done.packed_ref) | copy-start | bytes 26738692
Sparse Core Ops, SparseCore 0:
  10.9 80.8 all-gather.1

commit v2 on v1

--- a/solution.py
+++ b/solution.py
@@ -11,6 +11,42 @@
 HALF = TILE // 2
 MIB = 1024 * 1024
 
+ORDER = (0, 2, 1, 3, 4, 6, 5, 7)
+PIECES = {
+    "near": (2, True, (4, 6, 5, 7)),
+    "near_rest": (2, False, (1, 3)),
+    "side": (1, True, (3, 4, 6, 5, 7)),
+    "mid": (4, True, (6,)),
+    "mid_rest": (4, False, (5, 7)),
+    "far": (6, True, ()),
+    "far_rest": (6, False, (5, 7)),
+    "side_near": (3, True, (5, 7, 4, 6)),
+    "side_mid": (5, True, (7,)),
+    "side_far": (7, True, ()),
+}
+SENT = ("side", "near", "mid", "far", "near_rest", "mid_rest", "far_rest")
+PASSED_ON = {"side_near": "near", "side_mid": "mid", "side_far": "far"}
+PHASES = (("rows",), ("near", "side"), ("near_rest", "mid", "far", "side_near"), ("mid_rest", "far_rest", "side_mid", "side_far"))
+KINDS = ("rows",) + tuple(PIECES)
+DEVICES = 16
+CLASSES = DEVICES // 2
+
+
+def piece_rows(name):
+    _, own, classes = PIECES[name]
+    return 2 * TILE * len(classes) + (TILE + HALF if own else 0)
+
+
+def piece_table():
+    table = [0] * (CLASSES * CLASSES)
+    for name, (owner, own, classes) in PIECES.items():
+        kind = KINDS.index(name)
+        for place, column in enumerate(classes):
+            table[owner * CLASSES + column] = kind * 64 + 4 * place + (2 if own else 0)
+        if own:
+            table[owner * CLASSES + owner] = kind * 64 + 4 * len(classes) + 2
+    return jnp.array(table, jnp.int32)
+
 
 def split(value):
     high = value.astype(jnp.bfloat16)
@@ -18,33 +54,90 @@
     return high, low
 
 
-def pack_kernel(tiles, me_ref, rows_ref, packed_ref):
+def pack_kernel(names, me_ref, rows_ref, *packed_refs):
     me = me_ref[0]
-    half = tiles // 2
-    for d in range(half):
-        col = lax.rem(me + d, tiles) * TILE
-        packed_ref[d * TILE : (d + 1) * TILE, :] = rows_ref[:, pl.ds(pl.multiple_of(col, TILE), TILE)]
-    col = lax.rem(me + half, tiles) * TILE
-    opposite = rows_ref[:, pl.ds(pl.multiple_of(col, TILE), TILE)]
-
-    @pl.when(me < half)
-    def _():
-        packed_ref[half * TILE :, :] = opposite[:HALF, :]
-
-    @pl.when(me >= half)
-    def _():
-        packed_ref[half * TILE :, :] = opposite.T[HALF:, :]
-
-
-def pack(sep_rows, me, tiles):
-    return pl.pallas_call(
-        functools.partial(pack_kernel, tiles),
-        out_shape=jax.ShapeDtypeStruct((tiles * HALF + HALF, TILE), jnp.float32),
+
+    def tile(q):
+        return rows_ref[:, pl.ds(pl.multiple_of(q * TILE, TILE), TILE)]
+
+    diagonal, pair = tile(me), tile(me ^ 1)
+    half = jnp.where(me % 2 == 0, pair[:HALF, :], pair.T[HALF:, :])
+    for name, packed_ref in zip(names, packed_refs, strict=True):
+        owner, own, classes = PIECES[name]
+        row = 0
+        if own:
+            packed_ref[:TILE, :] = diagonal
+            row = TILE
+        for column in classes:
+            for core in range(2):
+                q = (me & ~1) ^ (2 * (owner ^ column)) ^ core
+                packed_ref[row : row + TILE, :] = tile(q)
+                row += TILE
+        if own:
+            packed_ref[row : row + HALF, :] = half
+
+
+def pack(names, me, sep_rows):
+    return pl.pallas_call(
+        functools.partial(pack_kernel, names),
+        out_shape=[jax.ShapeDtypeStruct((piece_rows(name), TILE), jnp.float32) for name in names],
         in_specs=[pl.BlockSpec(memory_space=pltpu.SMEM), pl.BlockSpec(memory_space=pltpu.VMEM)],
-        out_specs=pl.BlockSpec(memory_space=pltpu.VMEM),
-        compiler_params=pltpu.CompilerParams(vmem_limit_bytes=8 * MIB),
-        name="pack_share",
+        out_specs=[pl.BlockSpec(memory_space=pltpu.VMEM)] * len(names),
+        compiler_params=pltpu.CompilerParams(vmem_limit_bytes=16 * MIB),
+        name="pack_" + names[0],
     )(me, sep_rows)
+
+
+def jobs_kernel(nodes, sides, me_ref, table_ref, patterns_ref, jobs_ref, count_ref):
+    room = jobs_ref.shape[1]
+    me = me_ref[0]
+    ranks = sum(ORDER.index(c) << (3 * c) for c in range(CLASSES))
+    for s in range(2 * len(KINDS)):
+        count_ref[s] = 0
+
+    def one(step, _):
+        node, a, b = step // (sides * sides), (step // sides) % sides, step % sides
+        r, q = patterns_ref[node, a], patterns_ref[node, b]
+        owner, column = (r ^ me) >> 1, (q ^ me) >> 1
+        core = r & 1
+        rank_r, rank_q = (ranks >> (3 * owner)) & 7, (ranks >> (3 * column)) & 7
+        same = owner == column
+        here = owner == 0
+        entry = table_ref[owner * CLASSES + column]
+        kind = jnp.where(here, 0, entry // 64)
+        first = jnp.where(same, jnp.where(r == q, 0, entry % 64), entry % 64 + 2 * (q & 1))
+        first = jnp.where(here, q, first)
+        halved = same & (r != q) & (owner != 0)
+        sends = jnp.where(same, (r == q) | (owner != 0) | (core == 0), rank_r < rank_q)
+        swap = halved & (core == 1)
+        low_a, low_b = jnp.where(swap, b, a), jnp.where(swap, a, b)
+
+        @pl.when(sends)
+        def _():
+            slot = kind * 2 + ((r ^ me) & 1)
+            at = count_ref[slot]
+            code = ((first * nodes + node) * sides + low_a) * sides + low_b
+            jobs_ref[slot, at] = code * 2 + halved.astype(jnp.int32)
+            count_ref[slot] = at + 1
+
+        return 0
+
+    lax.fori_loop(0, nodes * sides * sides, one, 0)
+
+
+def plan_jobs(me, patterns):
+    nodes, sides = patterns.shape
+    smem = pl.BlockSpec(memory_space=pltpu.SMEM)
+    return pl.pallas_call(
+        functools.partial(jobs_kernel, nodes, sides),
+        out_shape=[
+            jax.ShapeDtypeStruct((2 * len(KINDS), nodes * sides), jnp.int32),
+            jax.ShapeDtypeStruct((2 * len(KINDS),), jnp.int32),
+        ],
+        in_specs=[smem] * 3,
+        out_specs=[smem] * 2,
+        name="plan_jobs",
+    )(me, piece_table(), patterns)
 
 
 def place(high_ref, low_ref, node, a, b, high, low):
@@ -54,43 +147,77 @@
     low_ref[node, rows, cols] = low
 
 
-def assemble_kernel(tiles, nodes, sides, patterns_ref, packed_ref, high_ref, low_ref):
-    half = tiles // 2
-    share = tiles * HALF + HALF
-
-    def one(step, _):
-        node = step // (sides * sides)
-        a = lax.rem(step // sides, sides)
-        b = lax.rem(step, sides)
-        r = patterns_ref[node, a]
-        q = patterns_ref[node, b]
-        d = lax.rem(q - r + tiles, tiles)
-
-        @pl.when(d < half)
-        def _():
-            start = pl.multiple_of(r * share + d * TILE, HALF)
-            value = packed_ref[pl.ds(start, TILE), :]
-            high, low = split(value)
-            place(high_ref, low_ref, node, a, b, high, low)
-
-            @pl.when(d > 0)
+def assemble_kernel(names, nodes, sides, me_ref, jobs_ref, count_ref, *refs):
+    sources, (high_ref, low_ref) = refs[: 2 * len(names)], refs[-2:]
+    mine = me_ref[0] & 1
+
+    def work(name, other, source):
+        slot = KINDS.index(name) * 2 + other
+        core = mine ^ other
+
+        def one(i, _):
+            code = jobs_ref[slot, i]
+            halved, code = code % 2, code // 2
+            b, code = code % sides, code // sides
+            a, code = code % sides, code // sides
+            node, first = code % nodes, code // nodes
+
+            @pl.when(halved == 0)
             def _():
-                high, low = split(value.T)
-                place(high_ref, low_ref, node, b, a, high, low)
-
-        @pl.when((d == half) & (r < half))
-        def _():
-            first = pl.multiple_of(r * share + half * TILE, HALF)
-            second = pl.multiple_of(q * share + half * TILE, HALF)
-            value = jnp.concatenate([packed_ref[pl.ds(first, HALF), :], packed_ref[pl.ds(second, HALF), :]], axis=0)
-            high, low = split(value)
-            place(high_ref, low_ref, node, a, b, high, low)
-            high, low = split(value.T)
-            place(high_ref, low_ref, node, b, a, high, low)
-
-        return 0
-
-    lax.fori_loop(0, nodes * sides * sides, one, 0)
+                if name == "rows":
+                    value = source[:, pl.ds(pl.multiple_of(first * TILE, TILE), TILE)]
+                else:
+                    value = source[pl.ds(pl.multiple_of(first * HALF, HALF), TILE), :]
+                high, low = split(value)
+                place(high_ref, low_ref, node, a, b, high, low)
+
+                @pl.when(a != b)
+                def _():
+                    high, low = split(value.T)
+                    place(high_ref, low_ref, node, b, a, high, low)
+
+            if name == "rows" or not PIECES[name][1]:
+                return 0
+
+            @pl.when(halved == 1)
+            def _():
+                value = source[pl.ds(pl.multiple_of(first * HALF, HALF), HALF), :]
+                high, low = split(value)
+                rows = pl.ds(pl.multiple_of(a * TILE + core * HALF, HALF), HALF)
+                cols = pl.ds(pl.multiple_of(b * TILE, TILE), TILE)
+                high_ref[node, rows, cols] = high
+                low_ref[node, rows, cols] = low
+                rows = pl.ds(pl.multiple_of(b * TILE, TILE), TILE)
+                cols = pl.ds(pl.multiple_of(a * TILE, TILE), TILE)
+                for ref, part in zip((high_ref, low_ref), split(value.T), strict=True):
+                    old = ref[node, rows, cols]
+                    both = jnp.concatenate([part, part], axis=1)
+                    column = lax.broadcasted_iota(jnp.int32, both.shape, 1)
+                    ref[node, rows, cols] = jnp.where(column // HALF == core, both, old)
+
+            return 0
+
+        lax.fori_loop(0, count_ref[slot], one, 0)
+
+    for i, name in enumerate(names):
+        for other in range(2):
+            work(name, other, sources[2 * i + other])
+
+
+def assemble(names, me, jobs, count, patterns, sources, blocks):
+    nodes, sides = patterns.shape
+    side = sides * TILE
+    smem, vmem = pl.BlockSpec(memory_space=pltpu.SMEM), pl.BlockSpec(memory_space=pltpu.VMEM)
+    given = [pltpu.with_memory_space_constraint(block, pltpu.VMEM) for block in blocks]
+    return pl.pallas_call(
+        functools.partial(assemble_kernel, names, nodes, sides),
+        out_shape=[pltpu.VMEM((nodes, side, side), jnp.bfloat16)] * 2,
+        in_specs=[smem] * 3 + [vmem] * (len(sources) + len(given)),
+        out_specs=[vmem] * 2,
+        input_output_aliases={3 + len(sources) + i: i for i in range(len(given))},
+        compiler_params=pltpu.CompilerParams(vmem_limit_bytes=32 * MIB),
+        name="assemble_" + names[0],
+    )(me, jobs, count, *sources, *given)
 
 
 def assemble_full_kernel(nodes, sides, patterns_ref, whole_ref, high_ref, low_ref):
@@ -107,16 +234,16 @@
     lax.fori_loop(0, nodes * sides * sides, one, 0)
 
 
-def assemble(kernel, patterns, source):
+def assemble_full(patterns, source):
     nodes, sides = patterns.shape
     side = sides * TILE
     return pl.pallas_call(
-        kernel,
+        functools.partial(assemble_full_kernel, nodes, sides),
         out_shape=[pltpu.VMEM((nodes, side, side), jnp.bfloat16)] * 2,
         in_specs=[pl.BlockSpec(memory_space=pltpu.SMEM), pl.BlockSpec(memory_space=pltpu.VMEM)],
         out_specs=[pl.BlockSpec(memory_space=pltpu.VMEM)] * 2,
         compiler_params=pltpu.CompilerParams(vmem_limit_bytes=32 * MIB),
-        name="assemble_blocks",
+        name="assemble_full",
     )(patterns, source)
 
 
@@ -191,19 +318,36 @@
     return out, marg.reshape(cols)
 
 
+def swap(value, mask):
+    return lax.ppermute(value, "pr", [(i, i ^ mask) for i in range(DEVICES)])
+
+
+def planned_blocks(sep_inv, patterns):
+    me = lax.axis_index("pr").astype(jnp.int32).reshape(1)
+    packed = {}
+    for names in (SENT[:2], SENT[2:]):
+        packed |= zip(names, pack(names, me, sep_inv), strict=True)
+    here = {"rows": sep_inv}
+    for name in SENT:
+        here[name] = swap(packed[name], 2 * PIECES[name][0])
+    for name, source in PASSED_ON.items():
+        here[name] = swap(here[source], 2)
+    jobs, count = plan_jobs(me, patterns)
+    blocks = ()
+    for names in PHASES:
+        sources = []
+        for name in names:
+            sources += [here[name], swap(here[name], 1)]
+        blocks = assemble(names, me, jobs, count, patterns, sources, blocks)
+    return blocks
+
+
 def shards(sep_inv, factor, widths, patterns, dinv):
     own_rows, order = sep_inv.shape
-    tiles = order // TILE
-    nodes, sides = patterns.shape
-    if own_rows == TILE and tiles % 2 == 0:
-        me = lax.axis_index("pr").astype(jnp.int32).reshape(1)
-        packed = pack(sep_inv, me, tiles)
-        gathered = lax.all_gather(packed, "pr", axis=0, tiled=True)
-        kernel = functools.partial(assemble_kernel, tiles, nodes, sides)
+    if own_rows == TILE and order == DEVICES * TILE:
+        high, low = planned_blocks(sep_inv, patterns)
     else:
-        gathered = lax.all_gather(sep_inv, "pr", axis=0, tiled=True)
-        kernel = functools.partial(assemble_full_kernel, nodes, sides)
-    high, low = assemble(kernel, patterns, gathered)
+        high, low = assemble_full(patterns, lax.all_gather(sep_inv, "pr", axis=0, tiled=True))
     return products(widths, high, low, factor, dinv)
 
 

time: 131 us -> 112 us (0.85)
  the two profiles are of different devices: /device:TPU:0 before, /device:TPU:11 now
where the time goes in v2:
time: 112 us; the launch traced here: 111 us
  Pallas kernels  37.7 us (34%)
  waiting for transfers between devices  30.9 us (28%)
  starting transfers between devices  30.5 us (27%)
  local copies, waits for them, and re-layouts  11.2 us (10%)
    ppermute x21, waiting for transfers between devices, swap(): return lax.ppermute(value, 'pr', [(i, i ^ mask) for i in range(DEVICES)])  30.9 us
    ppermute x21, starting transfers between devices, swap(): return lax.ppermute(value, 'pr', [(i, i ^ mask) for i in range(DEVICES)])  30.5 us
    pallas_call x1, Pallas kernels, products(): pl.pallas_call(functools.partial(product_kernel, nodes), grid=(cols // (2...  17.8 us
    pallas_call x4, Pallas kernels, assemble(): pl.pallas_call(functools.partial(assemble_kernel, names, nodes, sides), o...  12.7 us
    unnamed x41, local copies, waits for them, and re-layouts  11.2 us
    pallas_call x1, Pallas kernels, plan_jobs(): pl.pallas_call(functools.partial(jobs_kernel, nodes, sides), out_shape=[j...  6.92 us
  transfers between devices with their start and end apart: 21, of which 7 were waited for; matrix products, arithmetic and copies ran while one was open for 1% of the time, Pallas kernels for 16%

profile of v2, /device:TPU:11, one launch (start us, length us, event | category | flops | bytes accessed | tf_op | source)
XLA Modules:
  0.0 111.1 jit_solution(18346550141178087823)
XLA Ops:
  0.6 1.2 %copy-done = f32[128,2048]{1,0:T(8,128)S(1)} copy-done((f32[128,2048]{1,0:T(8,128)S(1)}, f32[128,2048]{1,0:T(8,128)}, u32[]{:S(2)}) %copy-start) | copy-done | bytes 1048600
  2.3 1.2 %collective-permute-start.18 = (f32[1472,128]{1,0:T(8,128)S(1)}, f32[1472,128]{1,0:T(8,128)S(1)}, u32[]{:S(2)}, u32[]{:S(2)}) collective-permute-start(f32[1472,128]{1,0:T(8,128)S(1)} %get-tuple-element.29), channel_id=1, source_target_pairs={{0,2},{1,3},{2,0},{3,1},{4,6},{5,7},{6,4},{7,5},{8,10},{9,11},{10,... | collective-permute-start | bytes 2261000 | tf_op jit(solution)/shard_map/ppermute | solution.py:322
  3.7 2.5 %collective-permute-start.7 = (f32[192,128]{1,0:T(8,128)S(1)}, f32[192,128]{1,0:T(8,128)S(1)}, u32[]{:S(2)}, u32[]{:S(2)}) collective-permute-start(f32[192,128]{1,0:T(8,128)S(1)} %get-tuple-element.26), channel_id=1, source_target_pairs={{0,12},{1,13},{2,14},{3,15},{4,8},{5,9},{6,10},{7,11},{8,4},{9,5},... | collective-permute-start | bytes 294920 | tf_op jit(solution)/shard_map/ppermute | solution.py:322
  6.2 1.0 collective-permute-start.4
  7.1 1.3 %collective-permute-done.7.refs_4_ = f32[192,128]{1,0:T(8,128)S(1)} collective-permute-done((f32[192,128]{1,0:T(8,128)S(1)}, f32[192,128]{1,0:T(8,128)S(1)}, u32[]{:S(2)}, u32[]{:S(2)}) %collective-permute-start.7) | collective-permute-done | bytes 98336 | tf_op jit(solution)/shard_map/ppermute | solution.py:322
  8.5 2.5 %collective-permute-start.13 = (f32[192,128]{1,0:T(8,128)S(1)}, f32[192,128]{1,0:T(8,128)S(1)}, u32[]{:S(2)}, u32[]{:S(2)}) collective-permute-start(f32[192,128]{1,0:T(8,128)S(1)} %collective-permute-done.7.refs_4_), channel_id=1, source_target_pairs={{0,1},{1,0},{2,3},{3,2},{4,5},{5,4},{6,7},{7,6},{8,9},{9,8},{10,11... | collective-permute-start | bytes 294920 | tf_op jit(solution)/shard_map/ppermute | solution.py:322
  12.5 14.0 %collective-permute-start.10 = (f32[512,128]{1,0:T(8,128)S(1)}, f32[512,128]{1,0:T(8,128)S(1)}, u32[]{:S(2)}, u32[]{:S(2)}) collective-permute-start(f32[512,128]{1,0:T(8,128)S(1)} %get-tuple-element.27), channel_id=1, source_target_pairs={{0,4},{1,5},{2,6},{3,7},{4,0},{5,1},{6,2},{7,3},{8,12},{9,13},{10,... | collective-permute-start | bytes 786440 | tf_op jit(solution)/shard_map/ppermute | solution.py:322
  27.5 2.9 %collective-permute-start = (f32[512,128]{1,0:T(8,128)S(1)}, f32[512,128]{1,0:T(8,128)S(1)}, u32[]{:S(2)}, u32[]{:S(2)}) collective-permute-start(f32[512,128]{1,0:T(8,128)S(1)} %get-tuple-element.23), channel_id=1, source_target_pairs={{0,8},{1,9},{2,10},{3,11},{4,12},{5,13},{6,14},{7,15},{8,0},{9,1},... | collective-permute-start | bytes 786440 | tf_op jit(solution)/shard_map/ppermute | solution.py:322
  30.4 2.7 %collective-permute-done.10.refs_0_ = f32[512,128]{1,0:T(8,128)S(1)} collective-permute-done((f32[512,128]{1,0:T(8,128)S(1)}, f32[512,128]{1,0:T(8,128)S(1)}, u32[]{:S(2)}, u32[]{:S(2)}) %collective-permute-start.10) | collective-permute-done | bytes 262176 | tf_op jit(solution)/shard_map/ppermute | solution.py:322
  33.3 13.8 %collective-permute-done.refs_0_ = f32[512,128]{1,0:T(8,128)S(1)} collective-permute-done((f32[512,128]{1,0:T(8,128)S(1)}, f32[512,128]{1,0:T(8,128)S(1)}, u32[]{:S(2)}, u32[]{:S(2)}) %collective-permute-start) | collective-permute-done | bytes 262176 | tf_op jit(solution)/shard_map/ppermute | solution.py:322
  47.1 1.8 %collective-permute-start.12 = (f32[448,128]{1,0:T(8,128)S(1)}, f32[448,128]{1,0:T(8,128)S(1)}, u32[]{:S(2)}, u32[]{:S(2)}) collective-permute-start(f32[448,128]{1,0:T(8,128)S(1)} %collective-permute-done.4.refs_2_), channel_id=1, source_target_pairs={{0,1},{1,0},{2,3},{3,2},{4,5},{5,4},{6,7},{7,6},{8,9},{9,8},{10,11... | collective-permute-start | bytes 688136 | tf_op jit(solution)/shard_map/ppermute | solution.py:322
  48.9 6.3 %collective-permute-done.2.refs_2_ = f32[512,128]{1,0:T(8,128)} collective-permute-done((f32[512,128]{1,0:T(8,128)S(1)}, f32[512,128]{1,0:T(8,128)}, u32[]{:S(2)}, u32[]{:S(2)}) %collective-permute-start.2) | collective-permute-done | bytes 262176 | tf_op jit(solution)/shard_map/ppermute | solution.py:322
  57.7 6.1 %collective-permute-done.5.refs_4_ = f32[448,128]{1,0:T(8,128)} collective-permute-done((f32[448,128]{1,0:T(8,128)S(1)}, f32[448,128]{1,0:T(8,128)}, u32[]{:S(2)}, u32[]{:S(2)}) %collective-permute-start.5) | collective-permute-done | bytes 229408 | tf_op jit(solution)/shard_map/ppermute | solution.py:322
  63.9 0.8 collective-permute-start.11
  67.1 0.8 copy-done.2
  68.4 1.3 %copy.14.patterns_ref = s32[8,4]{1,0:T(8,128)} copy(s32[8,4]{0,1:T(4,128)} %param.9) | data formatting | bytes 256 | tf_op args[3]
  69.8 6.9 %plan_jobs.1 = (s32[22,32]{1,0:T(8,128)}, s32[22]{0:T(128)}) custom-call(s32[1]{0:T(128)} %bitcast.me_ref, s32[64]{0:T(128)} %constant.6.clone.table_ref, s32[8,4]{1,0:T(8,128)} %copy.14.patterns_ref), custom_call_target="tpu_custom_call" | custom-call | tf_op jit(solution)/shard_map/plan_jobs/pallas_call | solution.py:131
  76.7 1.2 %copy-done.1 = f32[128,2048]{1,0:T(8,128)S(1)} copy-done((f32[128,2048]{1,0:T(8,128)S(1)}, f32[128,2048]{1,0:T(8,128)}, u32[]{:S(2)}) %copy-start.1) | copy-done | bytes 1048600
  79.3 2.6 %assemble_rows.1 = (bf16[8,512,512]{2,1,0:T(8,128)(2,1)S(1)}, bf16[8,512,512]{2,1,0:T(8,128)(2,1)S(1)}) custom-call(s32[1]{0:T(128)} %bitcast.me_ref, s32[22,32]{1,0:T(8,128)S(1)} %copy-done.12, s32[22]{0:T(128)S(1)} %copy-done.17, f32[128,2048]{1,0:T(8,128)S(1)} %copy-done.1, f32[128,2048]{1,0:T(8,128)S(1)} %collective-permute-done.20.refs_1_), custom_call_target="tpu_custom_call" | custom-call | tf_op jit(solution)/shard_map/assemble_rows/pallas_call | solution.py:212
  81.9 1.1 copy-done.3
  83.0 4.0 %assemble_near.1 = (bf16[8,512,512]{2,1,0:T(8,128)(2,1)S(1)}, bf16[8,512,512]{2,1,0:T(8,128)(2,1)S(1)}) custom-call(s32[1]{0:T(128)} %bitcast.me_ref, s32[22,32]{1,0:T(8,128)S(1)} %copy-done.12, s32[22]{0:T(128)S(1)} %copy-done.17, f32[1216,128]{1,0:T(8,128)S(1)} %collective-permute-done.14.refs_0_, ...), custom_call_target="tpu_custom_call", output_to_operand_aliasing={{0}: (7, {}), {1}: (8, {})} | custom-call | tf_op jit(solution)/shard_map/assemble_near/pallas_call | solution.py:212
  87.1 3.7 %assemble_near_rest.1 = (bf16[8,512,512]{2,1,0:T(8,128)(2,1)S(1)}, bf16[8,512,512]{2,1,0:T(8,128)(2,1)S(1)}) custom-call(s32[1]{0:T(128)} %bitcast.me_ref, s32[22,32]{1,0:T(8,128)S(1)} %copy-done.12, s32[22]{0:T(128)S(1)} %copy-done.17, f32[512,128]{1,0:T(8,128)S(1)} %copy-done.5, ...), custom_call_target="tpu_custom_call", output_to_operand_aliasing={{0}: (11, {}), {1}: (12, {})} | custom-call | tf_op jit(solution)/shard_map/assemble_near_rest/pallas_call | solution.py:212
  90.9 2.4 %assemble_mid_rest.1 = (bf16[8,512,512]{2,1,0:T(8,128)(2,1)S(1)}, bf16[8,512,512]{2,1,0:T(8,128)(2,1)S(1)}) custom-call(s32[1]{0:T(128)} %bitcast.me_ref, s32[22,32]{1,0:T(8,128)S(1)} %copy-done.12, s32[22]{0:T(128)S(1)} %copy-done.17, f32[512,128]{1,0:T(8,128)S(1)} %collective-permute-done.refs_0_, ...), custom_call_target="tpu_custom_call", output_to_operand_aliasing={{0}: (11, {}), {1}: (12, {})} | custom-call | tf_op jit(solution)/shard_map/assemble_mid_rest/pallas_call | solution.py:212
  93.3 17.8 %products.1 = (f32[512,4096]{1,0:T(8,128)}, f32[32,128]{1,0:T(8,128)}) custom-call(s32[1,8]{1,0:T(1,128)S(1)} %copy-done.19, bf16[8,512,512]{2,1,0:T(8,128)(2,1)S(1)} %get-tuple-element.36.high_ref, bf16[8,512,512]{2,1,0:T(8,128)(2,1)S(1)} %get-tuple-element.37.low_ref, f32[512,4096]{1,0:T(8,128)} %factor_ref.1, f32[32,128]{1,0:T(8,128)S(1)} %bitcast.3), custom_call_target="tpu_custom_call" | custom-call | flops 6442450944 | bytes 16777216 | tf_op jit(solution)/shard_map/products/pallas_call | solution.py:308
  (67 shorter events, 10.2 us)
Async XLA Ops:
  2.1 25.0 %collective-permute-start.14 = (f32[1216,128]{1,0:T(8,128)S(1)}, f32[1216,128]{1,0:T(8,128)S(1)}, u32[]{:S(2)}, u32[]{:S(2)}) collective-permute-start(f32[1216,128]{1,0:T(8,128)S(1)} %get-tuple-element.28), channel_id=1, source_target_pairs={{0,4},{1,5},{2,6},{3,7},{4,0},{5,1},{6,2},{7,3},{8,12},{9,13},{10,... | collective-permute-start | bytes 1867784 | tf_op jit(solution)/shard_map/ppermute | solution.py:322
  2.3 46.6 %collective-permute-start.18 = (f32[1472,128]{1,0:T(8,128)S(1)}, f32[1472,128]{1,0:T(8,128)S(1)}, u32[]{:S(2)}, u32[]{:S(2)}) collective-permute-start(f32[1472,128]{1,0:T(8,128)S(1)} %get-tuple-element.29), channel_id=1, source_target_pairs={{0,2},{1,3},{2,0},{3,1},{4,6},{5,7},{6,4},{7,5},{8,10},{9,11},{10,... | collective-permute-start | bytes 2261000 | tf_op jit(solution)/shard_map/ppermute | solution.py:322
  3.7 4.8 %collective-permute-start.7 = (f32[192,128]{1,0:T(8,128)S(1)}, f32[192,128]{1,0:T(8,128)S(1)}, u32[]{:S(2)}, u32[]{:S(2)}) collective-permute-start(f32[192,128]{1,0:T(8,128)S(1)} %get-tuple-element.26), channel_id=1, source_target_pairs={{0,12},{1,13},{2,14},{3,15},{4,8},{5,9},{6,10},{7,11},{8,4},{9,5},... | collective-permute-start | bytes 294920 | tf_op jit(solution)/shard_map/ppermute | solution.py:322
  6.2 21.3 %collective-permute-start.4 = (f32[448,128]{1,0:T(8,128)S(1)}, f32[448,128]{1,0:T(8,128)S(1)}, u32[]{:S(2)}, u32[]{:S(2)}) collective-permute-start(f32[448,128]{1,0:T(8,128)S(1)} %get-tuple-element.25), channel_id=1, source_target_pairs={{0,8},{1,9},{2,10},{3,11},{4,12},{5,13},{6,14},{7,15},{8,0},{9,1},... | collective-permute-start | bytes 688136 | tf_op jit(solution)/shard_map/ppermute | solution.py:322
  8.5 3.4 %collective-permute-start.13 = (f32[192,128]{1,0:T(8,128)S(1)}, f32[192,128]{1,0:T(8,128)S(1)}, u32[]{:S(2)}, u32[]{:S(2)}) collective-permute-start(f32[192,128]{1,0:T(8,128)S(1)} %collective-permute-done.7.refs_4_), channel_id=1, source_target_pairs={{0,1},{1,0},{2,3},{3,2},{4,5},{5,4},{6,7},{7,6},{8,9},{9,8},{10,11... | collective-permute-start | bytes 294920 | tf_op jit(solution)/shard_map/ppermute | solution.py:322
  10.9 15.6 %collective-permute-start.8 = (f32[192,128]{1,0:T(8,128)S(1)}, f32[192,128]{1,0:T(8,128)S(1)}, u32[]{:S(2)}, u32[]{:S(2)}) collective-permute-start(f32[192,128]{1,0:T(8,128)S(1)} %collective-permute-done.7.refs_4_), channel_id=1, source_target_pairs={{0,2},{1,3},{2,0},{3,1},{4,6},{5,7},{6,4},{7,5},{8,10},{9,11},{10,... | collective-permute-start | bytes 294920 | tf_op jit(solution)/shard_map/ppermute | solution.py:322
  12.5 20.6 %collective-permute-start.10 = (f32[512,128]{1,0:T(8,128)S(1)}, f32[512,128]{1,0:T(8,128)S(1)}, u32[]{:S(2)}, u32[]{:S(2)}) collective-permute-start(f32[512,128]{1,0:T(8,128)S(1)} %get-tuple-element.27), channel_id=1, source_target_pairs={{0,4},{1,5},{2,6},{3,7},{4,0},{5,1},{6,2},{7,3},{8,12},{9,13},{10,... | collective-permute-start | bytes 786440 | tf_op jit(solution)/shard_map/ppermute | solution.py:322
  26.5 40.4 %collective-permute-start.20 = (f32[128,2048]{1,0:T(8,128)S(1)}, f32[128,2048]{1,0:T(8,128)S(1)}, u32[]{:S(2)}, u32[]{:S(2)}) collective-permute-start(f32[128,2048]{1,0:T(8,128)S(1)} %copy-done), channel_id=1, source_target_pairs={{0,1},{1,0},{2,3},{3,2},{4,5},{5,4},{6,7},{7,6},{8,9},{9,8},{10,11... | collective-permute-start | bytes 3145736 | tf_op jit(solution)/shard_map/ppermute | solution.py:322
  27.1 30.4 %collective-permute-start.15 = (f32[1216,128]{1,0:T(8,128)S(1)}, f32[1216,128]{1,0:T(8,128)}, u32[]{:S(2)}, u32[]{:S(2)}) collective-permute-start(f32[1216,128]{1,0:T(8,128)S(1)} %collective-permute-done.14.refs_0_), channel_id=1, source_target_pairs={{0,2},{1,3},{2,0},{3,1},{4,6},{5,7},{6,4},{7,5},{8,10},{9,11},{10,... | collective-permute-start | bytes 1867784 | tf_op jit(solution)/shard_map/ppermute | solution.py:322
  27.5 19.6 %collective-permute-start = (f32[512,128]{1,0:T(8,128)S(1)}, f32[512,128]{1,0:T(8,128)S(1)}, u32[]{:S(2)}, u32[]{:S(2)}) collective-permute-start(f32[512,128]{1,0:T(8,128)S(1)} %get-tuple-element.23), channel_id=1, source_target_pairs={{0,8},{1,9},{2,10},{3,11},{4,12},{5,13},{6,14},{7,15},{8,0},{9,1},... | collective-permute-start | bytes 786440 | tf_op jit(solution)/shard_map/ppermute | solution.py:322
  33.1 22.0 %collective-permute-start.2 = (f32[512,128]{1,0:T(8,128)S(1)}, f32[512,128]{1,0:T(8,128)}, u32[]{:S(2)}, u32[]{:S(2)}) collective-permute-start(f32[512,128]{1,0:T(8,128)S(1)} %get-tuple-element.24), channel_id=1, source_target_pairs={{0,12},{1,13},{2,14},{3,15},{4,8},{5,9},{6,10},{7,11},{8,4},{9,5},... | collective-permute-start | bytes 786440 | tf_op jit(solution)/shard_map/ppermute | solution.py:322
  47.1 8.8 %collective-permute-start.12 = (f32[448,128]{1,0:T(8,128)S(1)}, f32[448,128]{1,0:T(8,128)S(1)}, u32[]{:S(2)}, u32[]{:S(2)}) collective-permute-start(f32[448,128]{1,0:T(8,128)S(1)} %collective-permute-done.4.refs_2_), channel_id=1, source_target_pairs={{0,1},{1,0},{2,3},{3,2},{4,5},{5,4},{6,7},{7,6},{8,9},{9,8},{10,11... | collective-permute-start | bytes 688136 | tf_op jit(solution)/shard_map/ppermute | solution.py:322
  48.9 19.4 %collective-permute-start.19 = (f32[1472,128]{1,0:T(8,128)S(1)}, f32[1472,128]{1,0:T(8,128)S(1)}, u32[]{:S(2)}, u32[]{:S(2)}) collective-permute-start(f32[1472,128]{1,0:T(8,128)S(1)} %collective-permute-done.18.refs_2_), channel_id=1, source_target_pairs={{0,1},{1,0},{2,3},{3,2},{4,5},{5,4},{6,7},{7,6},{8,9},{9,8},{10,11... | collective-permute-start | bytes 2261000 | tf_op jit(solution)/shard_map/ppermute | solution.py:322
  55.1 12.0 %collective-permute-start.17 = (f32[1216,128]{1,0:T(8,128)S(1)}, f32[1216,128]{1,0:T(8,128)S(1)}, u32[]{:S(2)}, u32[]{:S(2)}) collective-permute-start(f32[1216,128]{1,0:T(8,128)S(1)} %collective-permute-done.14.refs_0_), channel_id=1, source_target_pairs={{0,1},{1,0},{2,3},{3,2},{4,5},{5,4},{6,7},{7,6},{8,9},{9,8},{10,11... | collective-permute-start | bytes 1867784 | tf_op jit(solution)/shard_map/ppermute | solution.py:322
  56.6 7.3 %collective-permute-start.5 = (f32[448,128]{1,0:T(8,128)S(1)}, f32[448,128]{1,0:T(8,128)}, u32[]{:S(2)}, u32[]{:S(2)}) collective-permute-start(f32[448,128]{1,0:T(8,128)S(1)} %collective-permute-done.4.refs_2_), channel_id=1, source_target_pairs={{0,2},{1,3},{2,0},{3,1},{4,6},{5,7},{6,4},{7,5},{8,10},{9,11},{10,... | collective-permute-start | bytes 688136 | tf_op jit(solution)/shard_map/ppermute | solution.py:322
  57.5 29.6 %collective-permute-start.16 = (f32[1216,128]{1,0:T(8,128)}, f32[1216,128]{1,0:T(8,128)}, u32[]{:S(2)}, u32[]{:S(2)}) collective-permute-start(f32[1216,128]{1,0:T(8,128)} %collective-permute-done.15.refs_6_), channel_id=1, source_target_pairs={{0,1},{1,0},{2,3},{3,2},{4,5},{5,4},{6,7},{7,6},{8,9},{9,8},{10,11... | collective-permute-start | bytes 1867784 | tf_op jit(solution)/shard_map/ppermute | solution.py:322
  63.9 1.9 %collective-permute-start.11 = (f32[512,128]{1,0:T(8,128)S(1)}, f32[512,128]{1,0:T(8,128)S(1)}, u32[]{:S(2)}, u32[]{:S(2)}) collective-permute-start(f32[512,128]{1,0:T(8,128)S(1)} %collective-permute-done.10.refs_0_), channel_id=1, source_target_pairs={{0,1},{1,0},{2,3},{3,2},{4,5},{5,4},{6,7},{7,6},{8,9},{9,8},{10,11... | collective-permute-start | bytes 786440 | tf_op jit(solution)/shard_map/ppermute | solution.py:322
  66.6 24.2 %collective-permute-start.1 = (f32[512,128]{1,0:T(8,128)S(1)}, f32[512,128]{1,0:T(8,128)}, u32[]{:S(2)}, u32[]{:S(2)}) collective-permute-start(f32[512,128]{1,0:T(8,128)S(1)} %collective-permute-done.refs_0_), channel_id=1, source_target_pairs={{0,1},{1,0},{2,3},{3,2},{4,5},{5,4},{6,7},{7,6},{8,9},{9,8},{10,11... | collective-permute-start | bytes 786440 | tf_op jit(solution)/shard_map/ppermute | solution.py:322
  67.0 23.9 %collective-permute-start.3 = (f32[512,128]{1,0:T(8,128)}, f32[512,128]{1,0:T(8,128)}, u32[]{:S(2)}, u32[]{:S(2)}) collective-permute-start(f32[512,128]{1,0:T(8,128)} %collective-permute-done.2.refs_2_), channel_id=1, source_target_pairs={{0,1},{1,0},{2,3},{3,2},{4,5},{5,4},{6,7},{7,6},{8,9},{9,8},{10,11... | collective-permute-start | bytes 786440 | tf_op jit(solution)/shard_map/ppermute | solution.py:322
  67.9 22.9 %collective-permute-start.6 = (f32[448,128]{1,0:T(8,128)}, f32[448,128]{1,0:T(8,128)}, u32[]{:S(2)}, u32[]{:S(2)}) collective-permute-start(f32[448,128]{1,0:T(8,128)} %collective-permute-done.5.refs_4_), channel_id=1, source_target_pairs={{0,1},{1,0},{2,3},{3,2},{4,5},{5,4},{6,7},{7,6},{8,9},{9,8},{10,11... | collective-permute-start | bytes 688136 | tf_op jit(solution)/shard_map/ppermute | solution.py:322
  68.3 22.5 %collective-permute-start.9 = (f32[192,128]{1,0:T(8,128)S(1)}, f32[192,128]{1,0:T(8,128)}, u32[]{:S(2)}, u32[]{:S(2)}) collective-permute-start(f32[192,128]{1,0:T(8,128)S(1)} %collective-permute-done.8.refs_6_), channel_id=1, source_target_pairs={{0,1},{1,0},{2,3},{3,2},{4,5},{5,4},{6,7},{7,6},{8,9},{9,8},{10,11... | collective-permute-start | bytes 294920 | tf_op jit(solution)/shard_map/ppermute | solution.py:322
  83.0 4.1 %copy-start.11 = (f32[448,128]{1,0:T(8,128)S(1)}, f32[448,128]{1,0:T(8,128)}, u32[]{:S(2)}) copy-start(f32[448,128]{1,0:T(8,128)} %copy-done.10) | copy-start | bytes 688132
  83.0 4.1 %copy-start.14 = (f32[192,128]{1,0:T(8,128)S(1)}, f32[192,128]{1,0:T(8,128)}, u32[]{:S(2)}) copy-start(f32[192,128]{1,0:T(8,128)} %copy-done.13) | copy-start | bytes 294916
  83.0 4.1 %copy-start.16 = (f32[192,128]{1,0:T(8,128)S(1)}, f32[192,128]{1,0:T(8,128)}, u32[]{:S(2)}) copy-start(f32[192,128]{1,0:T(8,128)} %copy-done.15) | copy-start | bytes 294916
  (17 other events, 26.8 us)

commit v3 on v0

v3 whole, which is shorter than its diff:
```python
import functools

import jax
import jax.numpy as jnp
from jax import lax
from jax.experimental import pallas as pl
from jax.experimental.pallas import tpu as pltpu
from jax.sharding import PartitionSpec as P

TILE = 128
HALF = TILE // 2
MIB = 1024 * 1024

ORDER = (0, 2, 1, 3, 4, 6, 5, 7)
PIECES = {
    "near": (2, True, (4, 6, 5, 7, 1, 3)),
    "side": (1, True, (3, 4, 6, 5, 7)),
    "mid": (4, True, (6, 5, 7)),
    "side_near": (3, True, (5, 7, 4, 6)),
    "far": (6, True, ()),
    "side_mid": (5, True, (7,)),
    "side_far": (7, True, ()),
    "far_rest": (6, False, (5, 7)),
}
ROUNDS = (("near", "side"), ("mid", "side_near", "far"), ("side_mid", "side_far", "far_rest"))
KINDS = ("rows",) + tuple(PIECES)
DEVICES = 16
CLASSES = DEVICES // 2


def class_of(device, seen_from):
    place, here = device >> 2, seen_from >> 2
    outer = ((place >> 1) ^ place ^ 1) & 1
    z = jnp.where((place ^ here) >> 1 != 0, 2 + outer, (place ^ here) & 1)
    return 2 * z + (((device ^ seen_from) >> 1) & 1)


def device_of(column, seen_from, core):
    here, z = seen_from >> 2, column >> 1
    half = (here >> 1) ^ (z >> 1)
    inner_first = half ^ 1 ^ (z & 1)
    place = 2 * half + (inner_first if z >= 2 else (here & 1) ^ z)
    return 4 * place + 2 * (((seen_from >> 1) & 1) ^ (column & 1)) + core


def piece_rows(*names):
    return sum((TILE + HALF if PIECES[name][1] else 0) + 2 * TILE * len(PIECES[name][2]) for name in names)


def piece_table():
    table = [0] * (CLASSES * CLASSES)
    for name, (owner, own, classes) in PIECES.items():
        kind = KINDS.index(name)
        for place, column in enumerate(classes):
            table[owner * CLASSES + column] = kind * 64 + (3 if own else 0) + 4 * place
        if own:
            table[owner * CLASSES + owner] = kind * 64 + 2
    return jnp.array(table, jnp.int32)


def call(kernel, name, given, out_shape, out_specs, after=(), vmem=6, cost=0, **more):
    places = {"smem": pltpu.SMEM, "vmem": pltpu.VMEM, "any": pl.ANY}
    arrays = [pltpu.with_memory_space_constraint(x, pltpu.VMEM) if space == "vmem" else x for space, x in given]
    inputs = len(given)

    def body(*refs):
        kernel(*refs[:inputs], *refs[inputs + len(after) :])

    return pl.pallas_call(
        body,
        out_shape=out_shape,
        in_specs=[pl.BlockSpec(memory_space=places[space]) for space, _ in given] + [pl.BlockSpec(memory_space=pl.ANY)] * len(after),
        out_specs=out_specs,
        compiler_params=pltpu.CompilerParams(vmem_limit_bytes=vmem * MIB),
        cost_estimate=pl.CostEstimate(flops=0, bytes_accessed=cost, transcendentals=0),
        name=name,
        **more,
    )(*arrays, *after)


SMEM = pl.BlockSpec(memory_space=pltpu.SMEM)
VMEM = pl.BlockSpec(memory_space=pltpu.VMEM)
US = 3_000_000


def split(value):
    high = value.astype(jnp.bfloat16)
    low = (value - high.astype(jnp.float32)).astype(jnp.bfloat16)
    return high, low


def pack_kernel(sets, me_ref, rows_ref, *packed_refs):
    me = me_ref[0]

    def tile(q):
        return rows_ref[:, pl.ds(pl.multiple_of(q * TILE, TILE), TILE)]

    diagonal, pair = tile(me), tile(me ^ 1)
    half = jnp.where(me % 2 == 0, pair[:HALF, :], pair.T[HALF:, :])
    for names, packed_ref in zip(sets, packed_refs, strict=True):
        row = 0
        for name in names:
            owner, own, classes = PIECES[name]
            receiver = device_of(owner, me, 0) if owner < 4 else me ^ 12
            if own:
                packed_ref[row : row + TILE, :] = diagonal
                packed_ref[row + TILE : row + TILE + HALF, :] = half
                row += TILE + HALF
            for column in classes:
                for core in range(2):
                    packed_ref[row : row + TILE, :] = tile(device_of(column, receiver, core))
                    row += TILE


def pack(sets, me, sep_rows):
    return call(
        functools.partial(pack_kernel, sets),
        "pack",
        [("smem", me), ("vmem", sep_rows)],
        [pltpu.VMEM((piece_rows(*names), TILE), jnp.float32) for names in sets],
        [VMEM] * len(sets),
    )


def jobs_kernel(nodes, sides, me_ref, table_ref, patterns_ref, jobs_ref, count_ref):
    me = me_ref[0]
    ranks = sum(ORDER.index(c) << (3 * c) for c in range(CLASSES))
    for s in range(2 * len(KINDS)):
        count_ref[s] = 0

    def add(kind, core, code):
        slot = kind * 2 + ((core ^ me) & 1)
        at = count_ref[slot]
        jobs_ref[slot, at] = code
        count_ref[slot] = at + 1

    def one(node, _):
        tiles = [patterns_ref[node, a] for a in range(sides)]
        classes = [class_of(tile, me) for tile in tiles]
        order = [(ranks >> (3 * c)) & 7 for c in classes]
        for a in range(sides):
            r, c = tiles[a], classes[a]
            entry = table_ref[c * CLASSES + c]
            first = jnp.where(c == 0, r, 0)
            add(entry // 64, r & 1, (((first * nodes + node) * sides + a) * sides + a) * 2)
        for a in range(sides):
            for b in range(a + 1, sides):
                turned = jnp.where(classes[a] == classes[b], (tiles[a] & 1) == 1, order[a] > order[b])
                r, q = jnp.where(turned, tiles[b], tiles[a]), jnp.where(turned, tiles[a], tiles[b])
                c, d = jnp.where(turned, classes[b], classes[a]), jnp.where(turned, classes[a], classes[b])
                i, j = jnp.where(turned, b, a), jnp.where(turned, a, b)
                entry = table_ref[c * CLASSES + d]
                halved = (c == d) & (c != 0)
                first = entry % 64 + jnp.where(halved, 0, 2 * (q & 1))
                first = jnp.where(c == 0, q, first)
                code = (((first * nodes + node) * sides + i) * sides + j) * 2 + halved.astype(jnp.int32)
                add(entry // 64, r & 1, code)

                @pl.when(halved)
                def _():
                    add(entry // 64, q & 1, code)

        return 0

    lax.fori_loop(0, nodes, one, 0)


def place(high_ref, low_ref, node, a, b, high, low):
    rows = pl.ds(pl.multiple_of(a * TILE, TILE), TILE)
    cols = pl.ds(pl.multiple_of(b * TILE, TILE), TILE)
    high_ref[node, rows, cols] = high
    low_ref[node, rows, cols] = low


def assemble_kernel(sets, nodes, sides, me_ref, jobs_ref, count_ref, *refs):
    sources, (high_ref, low_ref) = refs[:-2], refs[-2:]
    mine = me_ref[0] & 1

    def work(name, other, source, start):
        slot = KINDS.index(name) * 2 + other
        core = mine ^ other

        def one(i, _):
            code = jobs_ref[slot, i]
            halved, code = code % 2, code // 2
            b, code = code % sides, code // sides
            a, code = code % sides, code // sides
            node, first = code % nodes, code // nodes

            @pl.when(halved == 0)
            def _():
                if name == "rows":
                    value = source[:, pl.ds(pl.multiple_of(first * TILE, TILE), TILE)]
                else:
                    value = source[pl.ds(pl.multiple_of(start + first * HALF, HALF), TILE), :]
                high, low = split(value)
                place(high_ref, low_ref, node, a, b, high, low)

                @pl.when(a != b)
                def _():
                    high, low = split(value.T)
                    place(high_ref, low_ref, node, b, a, high, low)

            if name == "rows" or not PIECES[name][1]:
                return 0

            @pl.when(halved == 1)
            def _():
                value = source[pl.ds(pl.multiple_of(start + first * HALF, HALF), HALF), :]
                high, low = split(value)
                rows = pl.ds(pl.multiple_of(a * TILE + core * HALF, HALF), HALF)
                cols = pl.ds(pl.multiple_of(b * TILE, TILE), TILE)
                high_ref[node, rows, cols] = high
                low_ref[node, rows, cols] = low
                rows = pl.ds(pl.multiple_of(b * TILE, TILE), TILE)
                cols = pl.ds(pl.multiple_of(a * TILE, TILE), TILE)
                for ref, part in zip((high_ref, low_ref), split(value.T), strict=True):
                    old = ref[node, rows, cols]
                    both = jnp.concatenate([part, part], axis=1)
                    column = lax.broadcasted_iota(jnp.int32, both.shape, 1)
                    ref[node, rows, cols] = jnp.where(column // HALF == core, both, old)

            return 0

        lax.fori_loop(0, count_ref[slot], one, 0)

    at = 0
    for names in sets:
        start = 0
        for name in names:
            for other in range(2):
                work(name, other, sources[at + other], start)
            start += 0 if name == "rows" else piece_rows(name)
        at += 2


def assemble(sets, me, jobs, count, patterns, sources, blocks, after=()):
    nodes, sides = patterns.shape
    side = sides * TILE
    given = [("smem", me), ("smem", jobs), ("smem", count)]
    given += [("vmem", x) for x in (*sources, *blocks)]
    return call(
        functools.partial(assemble_kernel, sets, nodes, sides),
        "assemble_" + sets[0][0],
        given,
        [pltpu.VMEM((nodes, side, side), jnp.bfloat16)] * 2,
        [VMEM] * 2,
        after,
        input_output_aliases={len(given) - len(blocks) + i: i for i in range(len(blocks))},
    )


def assemble_full_kernel(nodes, sides, patterns_ref, whole_ref, high_ref, low_ref):
    def one(step, _):
        node = step // (sides * sides)
        a = lax.rem(step // sides, sides)
        b = lax.rem(step, sides)
        rows = pl.ds(pl.multiple_of(patterns_ref[node, a] * TILE, TILE), TILE)
        cols = pl.ds(pl.multiple_of(patterns_ref[node, b] * TILE, TILE), TILE)
        high, low = split(whole_ref[rows, cols])
        place(high_ref, low_ref, node, a, b, high, low)
        return 0

    lax.fori_loop(0, nodes * sides * sides, one, 0)


def assemble_full(patterns, source):
    nodes, sides = patterns.shape
    side = sides * TILE
    return call(
        functools.partial(assemble_full_kernel, nodes, sides),
        "assemble_full",
        [("smem", patterns), ("vmem", source)],
        [pltpu.VMEM((nodes, side, side), jnp.bfloat16)] * 2,
        [VMEM] * 2,
    )


def halves_kernel(factor_ref, high_ref, low_ref):
    step = 4 * TILE
    for start in range(0, factor_ref.shape[1], step):
        where = slice(start, start + step)
        high_ref[:, where], low_ref[:, where] = split(factor_ref[:, where])


def factor_halves(factor, after=()):
    out = [pltpu.VMEM(factor.shape, jnp.bfloat16)] * 2
    return call(halves_kernel, "factor_halves", [("vmem", factor)], out, [VMEM] * 2, after)


def product_kernel(nodes, widths_ref, high_ref, low_ref, f_high_ref, f_low_ref, dinv_ref, out_ref, marg_ref, product_ref, sems):
    rows, cols = product_ref.shape
    step = 2 * TILE
    dot = functools.partial(jnp.dot, preferred_element_type=jnp.float32)

    def node_of(tile):
        node, end = 0, 0
        for j in range(nodes):
            end = end + widths_ref[0, j]
            node = node + (tile >= end).astype(jnp.int32)
        return jnp.minimum(node, nodes - 1)

    def columns(node, tile, count):
        where = pl.ds(pl.multiple_of(tile * TILE, TILE), count * TILE)
        high, low = high_ref[node], low_ref[node]
        f_high, f_low = f_high_ref[:, where], f_low_ref[:, where]
        product = -(dot(high, f_high) + (dot(high, f_low) + dot(low, f_high)))
        product_ref[:, where] = product
        factor = f_high.astype(jnp.float32) + f_low.astype(jnp.float32)
        total = jnp.sum(factor * product, axis=0, keepdims=True)
        for k in range(count):
            row = pl.ds(tile + k, 1)
            marg_ref[row, :] = dinv_ref[row, :] - total[:, k * TILE : (k + 1) * TILE]

    def write(pair):
        where = pl.ds(pl.multiple_of(pair * step, step), step)
        return pltpu.make_async_copy(product_ref.at[:, where], out_ref.at[:, where], sems.at[pair])

    def one(pair, _):
        first, second = node_of(2 * pair), node_of(2 * pair + 1)

        @pl.when(first == second)
        def _():
            columns(first, 2 * pair, 2)

        @pl.when(first != second)
        def _():
            columns(first, 2 * pair, 1)
            columns(second, 2 * pair + 1, 1)

        write(pair).start()
        return 0

    def finish(pair, _):
        write(pair).wait()
        return 0

    lax.fori_loop(0, cols // step, one, 0)
    lax.fori_loop(0, cols // step, finish, 0)


def products(widths, blocks, factors, dinv):
    rows, cols = factors[0].shape
    nodes = widths.shape[1]
    pairs = cols // (2 * TILE)
    given = [("smem", widths)] + [("vmem", part) for part in (*blocks, *factors)] + [("vmem", dinv.reshape(cols // TILE, TILE))]
    out, marg = call(
        functools.partial(product_kernel, nodes),
        "products",
        given,
        [jax.ShapeDtypeStruct((rows, cols), jnp.float32), jax.ShapeDtypeStruct((cols // TILE, TILE), jnp.float32)],
        [pl.BlockSpec(memory_space=pl.ANY), VMEM],
        vmem=14,
        cost=9 * US,
        scratch_shapes=[pltpu.VMEM((rows, cols), jnp.float32), pltpu.SemaphoreType.DMA((pairs,))],
    )
    return out, marg.reshape(cols)


def swap(value, mask):
    return lax.ppermute(value, "pr", [(i, i ^ mask) for i in range(DEVICES)])


def move(value, places):
    pairs = [(4 * old + k, 4 * new + k) for old, new in places.items() for k in range(4)]
    return lax.ppermute(value, "pr", pairs)


def plan_jobs(me, patterns, after):
    nodes, sides = patterns.shape
    shapes = [
        jax.ShapeDtypeStruct((2 * len(KINDS), nodes * sides), jnp.int32),
        jax.ShapeDtypeStruct((2 * len(KINDS),), jnp.int32),
    ]
    given = [("smem", me), ("smem", piece_table()), ("smem", patterns)]
    return call(functools.partial(jobs_kernel, nodes, sides), "plan_jobs", given, shapes, [SMEM] * 2, after)


def turn(name, kernel, me, given, rows, held, after=()):
    shapes = [pltpu.VMEM((n, TILE), jnp.float32) for n in rows] + [pltpu.VMEM(x.shape, x.dtype) for x in held]

    def body(me_ref, *refs):
        place = me_ref[0] >> 2
        kernel((place == 1) | (place == 2), *refs[: len(given)], *refs[len(given) + len(held) :][: len(rows)])

    inputs = [("smem", me)] + [("vmem", x) for x in (*given, *held)]
    aliases = {1 + len(given) + i: len(rows) + i for i in range(len(held))}
    return call(body, name, inputs, shapes, [VMEM] * len(shapes), after, input_output_aliases=aliases)


def copy_rows(target_ref, row, source_ref, first=0, count=None):
    count = source_ref.shape[0] - first if count is None else count
    target_ref[row : row + count, :] = source_ref[first : first + count, :]
    return row + count


def turn_1(inner, near_ref, side_ref, first_ref, part_ref, held_ref, far_ref, far_first_ref):
    copy_rows(part_ref, 0, near_ref, 0, part_ref.shape[0])
    copy_rows(held_ref, copy_rows(held_ref, 0, near_ref), side_ref)
    first, rest = piece_rows("far"), piece_rows("far_rest")
    copy_rows(far_ref, 0, near_ref, 0, first)
    copy_rows(far_ref, first, near_ref, near_ref.shape[0] - rest, rest)
    copy_rows(far_first_ref, 0, first_ref)


def turn_2(inner, mid_ref, mid_outer_ref, far_ref, far_outer_ref, side_near_ref, part_ref, held_ref, rest_ref):
    mid, far, onward = piece_rows("mid"), piece_rows("far"), piece_rows("side_mid")

    def take(m_ref, f_ref):
        copy_rows(part_ref, copy_rows(part_ref, 0, m_ref, 0, onward), f_ref, 0, far)
        copy_rows(held_ref, 0, m_ref)
        copy_rows(held_ref, mid + side_near_ref.shape[0], f_ref, 0, far)

    pl.when(inner)(lambda: take(mid_ref, far_ref))
    pl.when(jnp.logical_not(inner))(lambda: take(mid_outer_ref, far_outer_ref))
    copy_rows(held_ref, mid, side_near_ref)
    copy_rows(rest_ref, 0, far_ref, far)


def turn_3(inner, side_last_ref, rest_ref, rest_outer_ref, held_ref):
    row = copy_rows(held_ref, 0, side_last_ref)

    def take(ref):
        copy_rows(held_ref, row, ref)

    pl.when(inner)(lambda: take(rest_ref))
    pl.when(jnp.logical_not(inner))(lambda: take(rest_outer_ref))


def planned_blocks(sep_inv, factor, patterns):
    me = lax.axis_index("pr").astype(jnp.int32).reshape(1)
    between_inner, outward, between_outer = {1: 2, 2: 1}, {1: 0, 2: 3}, {0: 3, 3: 0}

    near, side, mid, first = pack((("near",), ("side",), ("mid",), ("far",)), me, sep_inv)
    rows_other = swap(sep_inv, 1)
    near, side, mid = swap(near, 4), swap(side, 2), move(mid, between_inner)
    jobs, count = plan_jobs(me, patterns, (rows_other,))
    rows = (piece_rows("side_near"), piece_rows(*ROUNDS[0]), piece_rows("far", "far_rest"), piece_rows("far"))
    part, held, far, first, mid = turn("turn_1", turn_1, me, (near, side, first), rows, (mid,), (count,))

    def put(sets, sources, blocks):
        return assemble(sets, me, jobs, count, patterns, sources, blocks)

    side_near, mid_outer = swap(part, 2), move(mid, outward)
    far, far_outer = move(far, between_inner), move(first, between_outer)
    blocks = put((("rows",), ROUNDS[0]), (sep_inv, rows_other, held, swap(held, 1)), ())
    rows = (piece_rows("side_mid", "side_far"), piece_rows(*ROUNDS[1]), piece_rows("far_rest"))
    part, held, rest = turn("turn_2", turn_2, me, (mid, mid_outer, far, far_outer, side_near), rows, (), blocks[:1])

    side_last, rest_outer = swap(part, 2), move(rest, outward)
    blocks = put(ROUNDS[1:2], (held, swap(held, 1)), blocks)
    factors = factor_halves(factor, blocks[:1])
    (held,) = turn("turn_3", turn_3, me, (side_last, rest, rest_outer), (piece_rows(*ROUNDS[2]),), (), factors[:1])
    return put(ROUNDS[2:], (held, swap(held, 1)), blocks), factors


def shards(sep_inv, factor, widths, patterns, dinv):
    own_rows, order = sep_inv.shape
    if own_rows == TILE and order == DEVICES * TILE:
        blocks, factors = planned_blocks(sep_inv, factor, patterns)
    else:
        factors = factor_halves(factor)
        blocks = assemble_full(patterns, lax.all_gather(sep_inv, "pr", axis=0, tiled=True))
    return products(widths, blocks, factors, dinv)


def solution(mesh):
    placed = (
        P(("cfg", "pr"), None),
        P("cfg", "pr"),
        P("pr", None),
        P("pr", None),
        P(("cfg", "pr")),
    )
    return jax.shard_map(
        shards,
        mesh=mesh,
        in_specs=placed,
        out_specs=(P("cfg", "pr"), P(("cfg", "pr"))),
        check_vma=False,
    )
```

time: 310 us -> 78 us (0.25)
  waiting for transfers between devices: 131 us -> 23.8 us
  matrix products: 59.4 us -> 0 us
  local copies, waits for them, and re-layouts: 47.9 us -> 4.2 us
  Pallas kernels: 0 us -> 32.7 us
  other arithmetic: 31.1 us -> 0.01 us
  loops' own time: 25.2 us -> 0 us
  starting transfers between devices: 0.04 us -> 16.6 us
  between operations: 14 us -> 0.84 us
    all_gather x1 -> x0, waiting for transfers between devices: 130 us -> none  [shards(): whole_inv = lax.all_gather(sep_inv, 'pr', axis=0, tiled=True)]
    dot_general x8 -> x0, matrix products: 59.4 us -> none  [one_node(): jnp.dot(block, factor_part, precision=lax.Precision.HIGHEST, preferred_el...]
    dynamic_slice x40 -> x0, local copies, waits for them, and re-layouts: 38.3 us -> none  [the longest x8 21.4 us: cut_block(): lax.dynamic_slice_in_dim(whole_inv, tile_row[a] * TILE, TILE, 0)]
    pallas_call x0 -> x10, Pallas kernels: none -> 32.7 us  [call(): pl.pallas_call(body, out_shape=out_shape, in_specs=[pl.BlockSpec(memory_s...]
    another operation x2 -> x0, loops' own time: 25.2 us -> none  [the longest x1 20.2 us: shards(): blocks = lax.map(pick_block, patterns)]
    ppermute x0 -> x13, waiting for transfers between devices: none -> 23.8 us  [the longest x8 16.7 us: swap(): return lax.ppermute(value, 'pr', [(i, i ^ mask) for i in range(DEVICES)])]
    ppermute x0 -> x13, starting transfers between devices: none -> 16.6 us  [the longest x5 9.56 us: move(): return lax.ppermute(value, 'pr', pairs)]
    and x8 -> x0, other arithmetic: 9.83 us -> none  [one_node(): inside = (tile_pos >= start) & (tile_pos < tile_ends[node])]
  transfers between devices with their start and end apart: 1 -> 13, of which waited for: 1 -> 6; matrix products, arithmetic and copies ran while one was open for 0% -> 1% of each run, Pallas kernels for 0% -> 19%
where the time goes in v3:
time: 78 us; the launch traced here: 78.1 us
  Pallas kernels  32.7 us (42%)
  waiting for transfers between devices  23.8 us (31%)
  starting transfers between devices  16.6 us (21%)
  local copies, waits for them, and re-layouts  4.2 us (5%)
  between operations  0.84 us (1%)
    pallas_call x10, Pallas kernels, call(): pl.pallas_call(body, out_shape=out_shape, in_specs=[pl.BlockSpec(memory_s...  32.7 us
    ppermute x8, waiting for transfers between devices, swap(): return lax.ppermute(value, 'pr', [(i, i ^ mask) for i in range(DEVICES)])  16.7 us
    ppermute x5, starting transfers between devices, move(): return lax.ppermute(value, 'pr', pairs)  9.56 us
    ppermute x5, waiting for transfers between devices, move(): return lax.ppermute(value, 'pr', pairs)  7.16 us
    ppermute x8, starting transfers between devices, swap(): return lax.ppermute(value, 'pr', [(i, i ^ mask) for i in range(DEVICES)])  6.99 us
    unnamed x19, local copies, waits for them, and re-layouts  4.2 us
  transfers between devices with their start and end apart: 13, of which 6 were waited for; matrix products, arithmetic and copies ran while one was open for 1% of the time, Pallas kernels for 19%

profile of v3, /device:TPU:0, one launch (start us, length us, event | category | flops | bytes accessed | tf_op | source)
XLA Modules:
  0.0 78.1 jit_solution(643204876710471534)
XLA Ops:
  1.1 1.2 %copy-done = f32[128,2048]{1,0:T(8,128)S(1)} copy-done((f32[128,2048]{1,0:T(8,128)S(1)}, f32[128,2048]{1,0:T(8,128)}, u32[]{:S(2)}) %copy-start) | copy-done | bytes 1048600
  2.4 1.5 %pack.1 = (f32[1728,128]{1,0:T(8,128)}, f32[1472,128]{1,0:T(8,128)}, f32[960,128]{1,0:T(8,128)}, f32[192,128]{1,0:T(8,128)S(1)}) custom-call(s32[1]{0:T(128)} %bitcast.refs_0_, f32[128,2048]{1,0:T(8,128)S(1)} %copy-done), custom_call_target="tpu_custom_call" | custom-call | tf_op jit(solution)/shard_map/pack/pallas_call | solution.py:69
  4.6 2.6 %collective-permute-start.1 = (f32[1728,128]{1,0:T(8,128)}, f32[1728,128]{1,0:T(8,128)S(1)}, u32[]{:S(2)}, u32[]{:S(2)}) collective-permute-start(f32[1728,128]{1,0:T(8,128)} %get-tuple-element.28), channel_id=1, source_target_pairs={{0,4},{1,5},{2,6},{3,7},{4,0},{5,1},{6,2},{7,3},{8,12},{9,13},{10,... | collective-permute-start | bytes 2654216 | tf_op jit(solution)/shard_map/ppermute | solution.py:361
  7.2 1.5 %collective-permute-start.2 = (f32[1472,128]{1,0:T(8,128)}, f32[1472,128]{1,0:T(8,128)}, u32[]{:S(2)}, u32[]{:S(2)}) collective-permute-start(f32[1472,128]{1,0:T(8,128)} %get-tuple-element.29), channel_id=1, source_target_pairs={{0,2},{1,3},{2,0},{3,1},{4,6},{5,7},{6,4},{7,5},{8,10},{9,11},{10,... | collective-permute-start | bytes 2261000 | tf_op jit(solution)/shard_map/ppermute | solution.py:361
  9.4 0.8 copy.13.refs_2_
  10.8 3.2 %plan_jobs.1 = (s32[18,32]{1,0:T(8,128)S(1)}, s32[18]{0:T(128)S(1)}) custom-call(s32[1]{0:T(128)} %bitcast.refs_0_, s32[64]{0:T(128)S(1)} %copy-done.5, s32[8,4]{1,0:T(8,128)S(1)} %copy.13.refs_2_, f32[128,2048]{1,0:T(8,128)S(1)} %collective-permute-done.refs_3_.refs_4_), custom_call_target="tpu_custom_call" | custom-call | tf_op jit(solution)/shard_map/plan_jobs/pallas_call | solution.py:69
  14.0 12.4 %collective-permute-done.2.refs_2_ = f32[1472,128]{1,0:T(8,128)} collective-permute-done((f32[1472,128]{1,0:T(8,128)}, f32[1472,128]{1,0:T(8,128)}, u32[]{:S(2)}, u32[]{:S(2)}) %collective-permute-start.2) | collective-permute-done | bytes 753696 | tf_op jit(solution)/shard_map/ppermute | solution.py:361
  26.4 1.2 %collective-permute-done.1.refs_1_ = f32[1728,128]{1,0:T(8,128)S(1)} collective-permute-done((f32[1728,128]{1,0:T(8,128)}, f32[1728,128]{1,0:T(8,128)S(1)}, u32[]{:S(2)}, u32[]{:S(2)}) %collective-permute-start.1) | collective-permute-done | bytes 884768 | tf_op jit(solution)/shard_map/ppermute | solution.py:361
  27.7 0.9 %copy-done.3 = f32[192,128]{1,0:T(8,128)S(1)} copy-done((f32[192,128]{1,0:T(8,128)S(1)}, f32[192,128]{1,0:T(8,128)}, u32[]{:S(2)}) %copy-start.3) | copy-done | bytes 98328
  28.6 1.3 %turn_1.1 = (f32[1216,128]{1,0:T(8,128)S(1)}, f32[3200,128]{1,0:T(8,128)S(1)}, f32[704,128]{1,0:T(8,128)S(1)}, f32[192,128]{1,0:T(8,128)S(1)}, f32[960,128]{1,0:T(8,128)S(1)}) custom-call(s32[1]{0:T(128)} %bitcast.refs_0_, f32[1728,128]{1,0:T(8,128)S(1)} %collective-permute-done.1.refs_1_, ...), custom_call_target="tpu_custom_call", output_to_operand_aliasing={{4}: (4, {})} | custom-call | tf_op jit(solution)/shard_map/turn_1/pallas_call | solution.py:69
  29.9 1.8 %collective-permute-start.7 = (f32[1216,128]{1,0:T(8,128)S(1)}, f32[1216,128]{1,0:T(8,128)S(1)}, u32[]{:S(2)}, u32[]{:S(2)}) collective-permute-start(f32[1216,128]{1,0:T(8,128)S(1)} %get-tuple-element.35), channel_id=1, source_target_pairs={{0,2},{1,3},{2,0},{3,1},{4,6},{5,7},{6,4},{7,5},{8,10},{9,11},{10,... | collective-permute-start | bytes 1867784 | tf_op jit(solution)/shard_map/ppermute | solution.py:361
  31.7 1.3 %collective-permute-start.4 = (f32[960,128]{1,0:T(8,128)S(1)}, f32[960,128]{1,0:T(8,128)S(1)}, u32[]{:S(2)}, u32[]{:S(2)}) collective-permute-start(f32[960,128]{1,0:T(8,128)S(1)} %get-tuple-element.32.refs_1_), channel_id=1, source_target_pairs={{4,0},{5,1},{6,2},{7,3},{8,12},{9,13},{10,14},{11,15},{20,16},{21,... | collective-permute-start | bytes 1474568 | tf_op jit(solution)/shard_map/ppermute | solution.py:366
  33.0 0.7 collective-permute-start.5
  33.7 5.5 %collective-permute-start.6 = (f32[192,128]{1,0:T(8,128)S(1)}, f32[192,128]{1,0:T(8,128)S(1)}, u32[]{:S(2)}, u32[]{:S(2)}) collective-permute-start(f32[192,128]{1,0:T(8,128)S(1)} %get-tuple-element.34), channel_id=1, source_target_pairs={{0,12},{1,13},{2,14},{3,15},{12,0},{13,1},{14,2},{15,3},{16,28},{1... | collective-permute-start | bytes 294920 | tf_op jit(solution)/shard_map/ppermute | solution.py:366
  39.2 5.9 %assemble_rows.1 = (bf16[8,512,512]{2,1,0:T(8,128)(2,1)S(1)}, bf16[8,512,512]{2,1,0:T(8,128)(2,1)S(1)}) custom-call(s32[1]{0:T(128)} %bitcast.refs_0_, s32[18,32]{1,0:T(8,128)S(1)} %get-tuple-element.26.refs_1_, s32[18]{0:T(128)S(1)} %get-tuple-element.27.refs_5_.refs_2_, f32[128,2048]{1,0:T(8,128)S(1)} %copy-done.1, ...), custom_call_target="tpu_custom_call" | custom-call | tf_op jit(solution)/shard_map/assemble_rows/pallas_call | solution.py:69
  45.1 3.9 %collective-permute-done.4.refs_2_ = f32[960,128]{1,0:T(8,128)S(1)} collective-permute-done((f32[960,128]{1,0:T(8,128)S(1)}, f32[960,128]{1,0:T(8,128)S(1)}, u32[]{:S(2)}, u32[]{:S(2)}) %collective-permute-start.4) | collective-permute-done | bytes 491552 | tf_op jit(solution)/shard_map/ppermute | solution.py:366
  49.6 1.4 %collective-permute-start.10 = (f32[512,128]{1,0:T(8,128)S(1)}, f32[512,128]{1,0:T(8,128)S(1)}, u32[]{:S(2)}, u32[]{:S(2)}) collective-permute-start(f32[512,128]{1,0:T(8,128)S(1)} %get-tuple-element.39.refs_2_), channel_id=1, source_target_pairs={{4,0},{5,1},{6,2},{7,3},{8,12},{9,13},{10,14},{11,15},{20,16},{21,... | collective-permute-start | bytes 786440 | tf_op jit(solution)/shard_map/ppermute | solution.py:366
  51.0 1.1 %collective-permute-done.11.refs_4_ = f32[2368,128]{1,0:T(8,128)S(1)} collective-permute-done((f32[2368,128]{1,0:T(8,128)S(1)}, f32[2368,128]{1,0:T(8,128)S(1)}, u32[]{:S(2)}, u32[]{:S(2)}) %collective-permute-start.11) | collective-permute-done | bytes 1212448 | tf_op jit(solution)/shard_map/ppermute | solution.py:361
  52.1 3.1 %assemble_mid.1 = (bf16[8,512,512]{2,1,0:T(8,128)(2,1)S(1)}, bf16[8,512,512]{2,1,0:T(8,128)(2,1)S(1)}) custom-call(s32[1]{0:T(128)} %bitcast.refs_0_, s32[18,32]{1,0:T(8,128)S(1)} %get-tuple-element.26.refs_1_, s32[18]{0:T(128)S(1)} %get-tuple-element.27.refs_5_.refs_2_, ...), custom_call_target="tpu_custom_call", output_to_operand_aliasing={{0}: (5, {}), {1}: (6, {})} | custom-call | tf_op jit(solution)/shard_map/assemble_mid/pallas_call | solution.py:69
  55.2 1.3 %factor_halves.1 = (bf16[512,4096]{1,0:T(8,128)(2,1)S(1)}, bf16[512,4096]{1,0:T(8,128)(2,1)S(1)}) custom-call(f32[512,4096]{1,0:T(8,128)S(1)} %bitcast.4, bf16[8,512,512]{2,1,0:T(8,128)(2,1)S(1)} %get-tuple-element.42.refs_1_.refs_5_), custom_call_target="tpu_custom_call" | custom-call | tf_op jit(solution)/shard_map/factor_halves/pallas_call | solution.py:69
  56.6 3.3 %collective-permute-done.10.refs_3_ = f32[512,128]{1,0:T(8,128)S(1)} collective-permute-done((f32[512,128]{1,0:T(8,128)S(1)}, f32[512,128]{1,0:T(8,128)S(1)}, u32[]{:S(2)}, u32[]{:S(2)}) %collective-permute-start.10) | collective-permute-done | bytes 262176 | tf_op jit(solution)/shard_map/ppermute | solution.py:366
  60.0 2.0 %collective-permute-done.12.refs_4_ = f32[1152,128]{1,0:T(8,128)S(1)} collective-permute-done((f32[1152,128]{1,0:T(8,128)S(1)}, f32[1152,128]{1,0:T(8,128)S(1)}, u32[]{:S(2)}, u32[]{:S(2)}) %collective-permute-start.12) | collective-permute-done | bytes 589856 | tf_op jit(solution)/shard_map/ppermute | solution.py:361
  62.0 1.8 %assemble_side_mid.1 = (bf16[8,512,512]{2,1,0:T(8,128)(2,1)S(1)}, bf16[8,512,512]{2,1,0:T(8,128)(2,1)S(1)}) custom-call(s32[1]{0:T(128)} %bitcast.refs_0_, s32[18,32]{1,0:T(8,128)S(1)} %get-tuple-element.26.refs_1_, s32[18]{0:T(128)S(1)} %get-tuple-element.27.refs_5_.refs_2_, ...), custom_call_target="tpu_custom_call", output_to_operand_aliasing={{0}: (5, {}), {1}: (6, {})} | custom-call | tf_op jit(solution)/shard_map/assemble_side_mid/pallas_call | solution.py:69
  63.8 14.3 %products.1 = (f32[512,4096]{1,0:T(8,128)}, f32[32,128]{1,0:T(8,128)}) custom-call(s32[1,8]{1,0:T(1,128)S(1)} %copy-done.6, bf16[8,512,512]{2,1,0:T(8,128)(2,1)S(1)} %get-tuple-element.45.refs_1_, bf16[8,512,512]{2,1,0:T(8,128)(2,1)S(1)} %get-tuple-element.46.refs_2_, bf16[512,4096]{1,0:T(8,128)(2,1)S(1)} %get-tuple-element.43.refs_4_.refs_3_, ...), custom_call_target="tpu_custom_call" | custom-call | bytes 27000000 | tf_op jit(solution)/shard_map/products/pallas_call | solution.py:69
  (32 shorter events, 3.3 us)
Async XLA Ops:
  0.6 9.5 %collective-permute-start = (f32[128,2048]{1,0:T(8,128)}, f32[128,2048]{1,0:T(8,128)S(1)}, u32[]{:S(2)}, u32[]{:S(2)}) collective-permute-start(f32[128,2048]{1,0:T(8,128)} %refs_3_.1), channel_id=1, source_target_pairs={{0,1},{1,0},{2,3},{3,2},{4,5},{5,4},{6,7},{7,6},{8,9},{9,8},{10,11... | collective-permute-start | bytes 3145736 | tf_op jit(solution)/shard_map/ppermute | solution.py:361
  1.1 1.2 %copy-start = (f32[128,2048]{1,0:T(8,128)S(1)}, f32[128,2048]{1,0:T(8,128)}, u32[]{:S(2)}) copy-start(f32[128,2048]{1,0:T(8,128)} %refs_3_.1) | copy-start | bytes 3145732
  2.4 36.8 %copy-start.1 = (f32[128,2048]{1,0:T(8,128)S(1)}, f32[128,2048]{1,0:T(8,128)}, u32[]{:S(2)}) copy-start(f32[128,2048]{1,0:T(8,128)} %refs_3_.1) | copy-start | bytes 3145732
  3.9 0.7 copy-start.2
  4.6 23.1 %collective-permute-start.1 = (f32[1728,128]{1,0:T(8,128)}, f32[1728,128]{1,0:T(8,128)S(1)}, u32[]{:S(2)}, u32[]{:S(2)}) collective-permute-start(f32[1728,128]{1,0:T(8,128)} %get-tuple-element.28), channel_id=1, source_target_pairs={{0,4},{1,5},{2,6},{3,7},{4,0},{5,1},{6,2},{7,3},{8,12},{9,13},{10,... | collective-permute-start | bytes 2654216 | tf_op jit(solution)/shard_map/ppermute | solution.py:361
  7.2 19.3 %collective-permute-start.2 = (f32[1472,128]{1,0:T(8,128)}, f32[1472,128]{1,0:T(8,128)}, u32[]{:S(2)}, u32[]{:S(2)}) collective-permute-start(f32[1472,128]{1,0:T(8,128)} %get-tuple-element.29), channel_id=1, source_target_pairs={{0,2},{1,3},{2,0},{3,1},{4,6},{5,7},{6,4},{7,5},{8,10},{9,11},{10,... | collective-permute-start | bytes 2261000 | tf_op jit(solution)/shard_map/ppermute | solution.py:361
  8.7 5.4 %collective-permute-start.3 = (f32[960,128]{1,0:T(8,128)}, f32[960,128]{1,0:T(8,128)S(1)}, u32[]{:S(2)}, u32[]{:S(2)}) collective-permute-start(f32[960,128]{1,0:T(8,128)} %get-tuple-element.31), channel_id=1, source_target_pairs={{4,8},{5,9},{6,10},{7,11},{8,4},{9,5},{10,6},{11,7},{20,24},{21,25... | collective-permute-start | bytes 1474568 | tf_op jit(solution)/shard_map/ppermute | solution.py:366
  10.1 0.7 copy-start.5
  27.7 0.9 %copy-start.3 = (f32[192,128]{1,0:T(8,128)S(1)}, f32[192,128]{1,0:T(8,128)}, u32[]{:S(2)}) copy-start(f32[192,128]{1,0:T(8,128)} %copy-done.2) | copy-start | bytes 294916
  29.9 9.3 %collective-permute-start.8 = (f32[3200,128]{1,0:T(8,128)S(1)}, f32[3200,128]{1,0:T(8,128)S(1)}, u32[]{:S(2)}, u32[]{:S(2)}) collective-permute-start(f32[3200,128]{1,0:T(8,128)S(1)} %get-tuple-element.36.refs_5_), channel_id=1, source_target_pairs={{0,1},{1,0},{2,3},{3,2},{4,5},{5,4},{6,7},{7,6},{8,9},{9,8},{10,11... | collective-permute-start | bytes 4915208 | tf_op jit(solution)/shard_map/ppermute | solution.py:361
  29.9 19.0 %collective-permute-start.7 = (f32[1216,128]{1,0:T(8,128)S(1)}, f32[1216,128]{1,0:T(8,128)S(1)}, u32[]{:S(2)}, u32[]{:S(2)}) collective-permute-start(f32[1216,128]{1,0:T(8,128)S(1)} %get-tuple-element.35), channel_id=1, source_target_pairs={{0,2},{1,3},{2,0},{3,1},{4,6},{5,7},{6,4},{7,5},{8,10},{9,11},{10,... | collective-permute-start | bytes 1867784 | tf_op jit(solution)/shard_map/ppermute | solution.py:361
  31.7 17.3 %collective-permute-start.4 = (f32[960,128]{1,0:T(8,128)S(1)}, f32[960,128]{1,0:T(8,128)S(1)}, u32[]{:S(2)}, u32[]{:S(2)}) collective-permute-start(f32[960,128]{1,0:T(8,128)S(1)} %get-tuple-element.32.refs_1_), channel_id=1, source_target_pairs={{4,0},{5,1},{6,2},{7,3},{8,12},{9,13},{10,14},{11,15},{20,16},{21,... | collective-permute-start | bytes 1474568 | tf_op jit(solution)/shard_map/ppermute | solution.py:366
  33.0 12.1 %collective-permute-start.5 = (f32[704,128]{1,0:T(8,128)S(1)}, f32[704,128]{1,0:T(8,128)S(1)}, u32[]{:S(2)}, u32[]{:S(2)}) collective-permute-start(f32[704,128]{1,0:T(8,128)S(1)} %get-tuple-element.33), channel_id=1, source_target_pairs={{4,8},{5,9},{6,10},{7,11},{8,4},{9,5},{10,6},{11,7},{20,24},{21,25... | collective-permute-start | bytes 1081352 | tf_op jit(solution)/shard_map/ppermute | solution.py:366
  33.7 11.4 %collective-permute-start.6 = (f32[192,128]{1,0:T(8,128)S(1)}, f32[192,128]{1,0:T(8,128)S(1)}, u32[]{:S(2)}, u32[]{:S(2)}) collective-permute-start(f32[192,128]{1,0:T(8,128)S(1)} %get-tuple-element.34), channel_id=1, source_target_pairs={{0,12},{1,13},{2,14},{3,15},{12,0},{13,1},{14,2},{15,3},{16,28},{1... | collective-permute-start | bytes 294920 | tf_op jit(solution)/shard_map/ppermute | solution.py:366
  49.0 6.2 %slice-start = ((s8[8388608]{0:T(1024)(128)(4,1)}), s8[4194304]{0:T(1024)(128)(4,1)S(1)}, s32[]{:S(2)}) async-start(s8[8388608]{0:T(1024)(128)(4,1)} %bitcast.3), calls=%async_computation | async-start | bytes 8388608
  49.1 3.0 %collective-permute-start.11 = (f32[2368,128]{1,0:T(8,128)S(1)}, f32[2368,128]{1,0:T(8,128)S(1)}, u32[]{:S(2)}, u32[]{:S(2)}) collective-permute-start(f32[2368,128]{1,0:T(8,128)S(1)} %get-tuple-element.40.refs_3_), channel_id=1, source_target_pairs={{0,1},{1,0},{2,3},{3,2},{4,5},{5,4},{6,7},{7,6},{8,9},{9,8},{10,11... | collective-permute-start | bytes 3637256 | tf_op jit(solution)/shard_map/ppermute | solution.py:361
  49.2 10.7 %collective-permute-start.9 = (f32[640,128]{1,0:T(8,128)S(1)}, f32[640,128]{1,0:T(8,128)S(1)}, u32[]{:S(2)}, u32[]{:S(2)}) collective-permute-start(f32[640,128]{1,0:T(8,128)S(1)} %get-tuple-element.38), channel_id=1, source_target_pairs={{0,2},{1,3},{2,0},{3,1},{4,6},{5,7},{6,4},{7,5},{8,10},{9,11},{10,... | collective-permute-start | bytes 983048 | tf_op jit(solution)/shard_map/ppermute | solution.py:361
  49.6 10.3 %collective-permute-start.10 = (f32[512,128]{1,0:T(8,128)S(1)}, f32[512,128]{1,0:T(8,128)S(1)}, u32[]{:S(2)}, u32[]{:S(2)}) collective-permute-start(f32[512,128]{1,0:T(8,128)S(1)} %get-tuple-element.39.refs_2_), channel_id=1, source_target_pairs={{4,0},{5,1},{6,2},{7,3},{8,12},{9,13},{10,14},{11,15},{20,16},{21,... | collective-permute-start | bytes 786440 | tf_op jit(solution)/shard_map/ppermute | solution.py:366
  52.1 3.1 %slice-start.1 = ((s8[8388608]{0:T(1024)(128)(4,1)}), s8[4194304]{0:T(1024)(128)(4,1)S(1)}, s32[]{:S(2)}) async-start(s8[8388608]{0:T(1024)(128)(4,1)} %bitcast.3), calls=%async_computation.1 | async-start | bytes 8388608
  59.9 2.1 %collective-permute-start.12 = (f32[1152,128]{1,0:T(8,128)S(1)}, f32[1152,128]{1,0:T(8,128)S(1)}, u32[]{:S(2)}, u32[]{:S(2)}) collective-permute-start(f32[1152,128]{1,0:T(8,128)S(1)} %turn_3.1.refs_3_), channel_id=1, source_target_pairs={{0,1},{1,0},{2,3},{3,2},{4,5},{5,4},{6,7},{7,6},{8,9},{9,8},{10,11... | collective-permute-start | bytes 1769480 | tf_op jit(solution)/shard_map/ppermute | solution.py:361
  62.0 1.8 %copy-start.4 = (f32[4096]{0:T(1024)S(1)}, f32[4096]{0:T(1024)}, u32[]{:S(2)}) copy-start(f32[4096]{0:T(1024)} %param.10) | copy-start | bytes 49156
  62.0 1.8 %copy-start.6 = (s32[1,8]{1,0:T(1,128)S(1)}, s32[1,8]{1,0:T(1,128)}, u32[]{:S(2)}) copy-start(s32[1,8]{1,0:T(1,128)} %refs_0_.3) | copy-start | bytes 100

commit v4 on v3

v4 whole, which is shorter than its diff:
```python
import functools

import jax
import jax.numpy as jnp
from jax import lax
from jax.experimental import pallas as pl
from jax.experimental.pallas import tpu as pltpu
from jax.sharding import PartitionSpec as P

TILE = 128
HALF = TILE // 2
MIB = 1024 * 1024

ORDER = (0, 2, 1, 3, 4, 6, 5, 7)
PIECES = {
    "near": (2, True, (4, 6, 5, 7, 1, 3)),
    "side": (1, True, (3, 4, 6, 5, 7)),
    "mid": (4, True, (6, 5, 7)),
    "side_near": (3, True, (5, 7, 4, 6)),
    "far": (6, True, ()),
    "side_mid": (5, True, (7,)),
    "side_far": (7, True, ()),
    "far_rest": (6, False, (5, 7)),
}
ROUNDS = (("near", "side"), ("mid", "side_near", "far"), ("side_mid", "side_far", "far_rest"))
KINDS = ("rows",) + tuple(PIECES)
DEVICES = 16
LISTS = 6
WHOLE = (0, 0, 0, 1, 1, 2, 2, 2)
CLASSES = DEVICES // 2


def class_of(device, seen_from):
    place, here = device >> 2, seen_from >> 2
    outer = ((place >> 1) ^ place ^ 1) & 1
    z = jnp.where((place ^ here) >> 1 != 0, 2 + outer, (place ^ here) & 1)
    return 2 * z + (((device ^ seen_from) >> 1) & 1)


def device_of(column, seen_from, core):
    here, z = seen_from >> 2, column >> 1
    half = (here >> 1) ^ (z >> 1)
    inner_first = half ^ 1 ^ (z & 1)
    place = 2 * half + (inner_first if z >= 2 else (here & 1) ^ z)
    return 4 * place + 2 * (((seen_from >> 1) & 1) ^ (column & 1)) + core


def piece_rows(*names):
    return sum((TILE + HALF if PIECES[name][1] else 0) + 2 * TILE * len(PIECES[name][2]) for name in names)


def piece_table():
    table = [0] * (CLASSES * CLASSES)
    for name, (owner, own, classes) in PIECES.items():
        kind = KINDS.index(name)
        for place, column in enumerate(classes):
            table[owner * CLASSES + column] = kind * 64 + (3 if own else 0) + 4 * place
        if own:
            table[owner * CLASSES + owner] = kind * 64 + 2
    return jnp.array(table, jnp.int32)


def call(kernel, name, given, out_shape, out_specs, after=(), vmem=6, cost=0, **more):
    places = {"smem": pltpu.SMEM, "vmem": pltpu.VMEM, "any": pl.ANY}
    arrays = [pltpu.with_memory_space_constraint(x, pltpu.VMEM) if space == "vmem" else x for space, x in given]
    inputs = len(given)

    def body(*refs):
        kernel(*refs[:inputs], *refs[inputs + len(after) :])

    return pl.pallas_call(
        body,
        out_shape=out_shape,
        in_specs=[pl.BlockSpec(memory_space=places[space]) for space, _ in given] + [pl.BlockSpec(memory_space=pl.ANY)] * len(after),
        out_specs=out_specs,
        compiler_params=pltpu.CompilerParams(vmem_limit_bytes=vmem * MIB),
        cost_estimate=pl.CostEstimate(flops=0, bytes_accessed=cost, transcendentals=0),
        name=name,
        **more,
    )(*arrays, *after)


SMEM = pl.BlockSpec(memory_space=pltpu.SMEM)
VMEM = pl.BlockSpec(memory_space=pltpu.VMEM)
US = 3_000_000


def split(value):
    high = value.astype(jnp.bfloat16)
    low = (value - high.astype(jnp.float32)).astype(jnp.bfloat16)
    return high, low


def pack_kernel(sets, me_ref, rows_ref, *packed_refs):
    me = me_ref[0]

    def tile(q):
        return rows_ref[:, pl.ds(pl.multiple_of(q * TILE, TILE), TILE)]

    diagonal, pair = tile(me), tile(me ^ 1)
    half = jnp.where(me % 2 == 0, pair[:HALF, :], pair.T[HALF:, :])
    for names, packed_ref in zip(sets, packed_refs, strict=True):
        row = 0
        for name in names:
            owner, own, classes = PIECES[name]
            receiver = device_of(owner, me, 0) if owner < 4 else me ^ 12
            if own:
                packed_ref[row : row + TILE, :] = diagonal
                packed_ref[row + TILE : row + TILE + HALF, :] = half
                row += TILE + HALF
            for column in classes:
                for core in range(2):
                    packed_ref[row : row + TILE, :] = tile(device_of(column, receiver, core))
                    row += TILE


def pack(sets, me, sep_rows):
    return call(
        functools.partial(pack_kernel, sets),
        "pack",
        [("smem", me), ("vmem", sep_rows)],
        [pltpu.VMEM((piece_rows(*names), TILE), jnp.float32) for names in sets],
        [VMEM] * len(sets),
    )


def jobs_kernel(nodes, sides, me_ref, table_ref, patterns_ref, jobs_ref, count_ref, slots_ref):
    me = me_ref[0]
    ranks = sum(ORDER.index(c) << (3 * c) for c in range(CLASSES))
    phases = sum(WHOLE[c] << (2 * c) for c in range(CLASSES))
    for s in range(LISTS * len(KINDS)):
        count_ref[s] = 0

    def one(node, _):
        tiles = [patterns_ref[node, a] for a in range(sides)]
        classes = [class_of(tile, me) for tile in tiles]
        order = [(ranks >> (3 * c)) & 7 for c in classes]
        phase = [(phases >> (2 * c)) & 3 for c in classes]
        slots = []
        for a in range(sides):
            slot = sum(((phase[b] < phase[a]) if b > a else (phase[b] <= phase[a])).astype(jnp.int32) for b in range(sides) if b != a)
            slots_ref[0, node * sides + a] = slot
            slots_ref[1, node * sides + slot] = a
            slots.append(slot)
        for p in range(len(ROUNDS)):
            slots_ref[2 + p, node] = sum((phase[a] == p).astype(jnp.int32) for a in range(sides))

        def add(which, first, i, j):
            at = count_ref[which]
            code = (first * nodes + node) * sides + i
            jobs_ref[which, at] = ((code * sides + j) * sides + pick(slots, i)) * sides + pick(slots, j)
            count_ref[which] = at + 1

        def pick(values, i):
            value = values[0]
            for k in range(1, sides):
                value = jnp.where(i == k, values[k], value)
            return value

        for a in range(sides):
            r, c = tiles[a], classes[a]
            entry = table_ref[c * CLASSES + c]
            first = jnp.where(c == 0, r, 0)
            add(((entry >> 6) * 2 + ((r ^ me) & 1)) * 3 + 1, first, jnp.int32(a), jnp.int32(a))
        for a in range(sides):
            for b in range(a + 1, sides):
                turned = jnp.where(classes[a] == classes[b], (tiles[a] & 1) == 1, order[a] > order[b])
                r, q = jnp.where(turned, tiles[b], tiles[a]), jnp.where(turned, tiles[a], tiles[b])
                c, d = jnp.where(turned, classes[b], classes[a]), jnp.where(turned, classes[a], classes[b])
                i, j = jnp.where(turned, b, a), jnp.where(turned, a, b)
                entry = table_ref[c * CLASSES + d]
                halved = (c == d) & (c != 0)
                first = (entry & 63) + jnp.where(halved, 0, 2 * (q & 1))
                first = jnp.where(c == 0, q, first)
                which = ((entry >> 6) * 2 + jnp.where(halved, 0, (r ^ me) & 1)) * 3 + jnp.where(halved, 2, 0)
                add(which, first, i, j)

        return 0

    lax.fori_loop(0, nodes, one, 0)


def place(high_ref, low_ref, node, a, b, value):
    rows = pl.ds(pl.multiple_of(a * TILE, TILE), TILE)
    cols = pl.ds(pl.multiple_of(b * TILE, TILE), TILE)
    high_ref[node, rows, cols], low_ref[node, rows, cols] = split(value)


def assemble_kernel(sets, nodes, sides, me_ref, jobs_ref, count_ref, slots_ref, *refs):
    sources, (high_ref, low_ref) = refs[:-2], refs[-2:]
    even = (me_ref[0] & 1) == 0

    def work(name, pair, start):
        def read(which, sort, i):
            code = jobs_ref[which, i]
            fields = []
            for size in (sides, sides, sides, sides, nodes):
                fields.append(lax.rem(code, size))
                code = lax.div(code, size)
            slot_j, slot_i, j, i, node = fields
            other = (which // 3) % 2
            if name == "rows":
                value = pair[other][:, pl.ds(pl.multiple_of(code * TILE, TILE), TILE)]
            elif sort == 2:
                rows = pl.ds(pl.multiple_of(start + code * HALF, HALF), HALF)
                mine, theirs = pair[0][rows, :], pair[1][rows, :]
                value = jnp.concatenate([jnp.where(even, mine, theirs), jnp.where(even, theirs, mine)], axis=0)
            else:
                value = pair[other][pl.ds(pl.multiple_of(start + code * HALF, HALF), TILE), :]
            return node, i, j, slot_i, slot_j, value

        def put(sort, node, i, j, slot_i, slot_j, value):
            place(high_ref, low_ref, node, slot_i, j, value)
            if sort != 1:
                place(high_ref, low_ref, node, slot_j, i, value.T)

        for other in range(2):
            for sort in range(3):
                which = (KINDS.index(name) * 2 + other) * 3 + sort
                if sort == 2 and (other == 1 or name == "rows" or not PIECES[name][1]) or sort == 1 and name == "far_rest":
                    continue
                if sort == 0 and name != "rows" and not PIECES[name][2]:
                    continue
                number = count_ref[which]

                def two(i, _):
                    first, second = read(which, sort, 2 * i), read(which, sort, 2 * i + 1)
                    put(sort, *first)
                    put(sort, *second)
                    return 0

                lax.fori_loop(0, lax.div(number, 2), two, 0)

                @pl.when(lax.rem(number, 2) == 1)
                def _():
                    put(sort, *read(which, sort, number - 1))

    at = 0
    for names in sets:
        start = 0
        for name in names:
            work(name, sources[at : at + 2], start)
            start += 0 if name == "rows" else piece_rows(name)
        at += 2


def assemble(sets, me, plan, patterns, sources, blocks, after=()):
    nodes, sides = patterns.shape
    side = sides * TILE
    given = [("smem", x) for x in (me, *plan)] + [("vmem", x) for x in (*sources, *blocks)]
    return call(
        functools.partial(assemble_kernel, sets, nodes, sides),
        "assemble_" + sets[0][0],
        given,
        [pltpu.VMEM((nodes, side, side), jnp.bfloat16)] * 2,
        [VMEM] * 2,
        after,
        input_output_aliases={len(given) - len(blocks) + i: i for i in range(len(blocks))},
    )


def assemble_full_kernel(nodes, sides, patterns_ref, whole_ref, high_ref, low_ref):
    def one(step, _):
        node = step // (sides * sides)
        a = lax.rem(step // sides, sides)
        b = lax.rem(step, sides)
        rows = pl.ds(pl.multiple_of(patterns_ref[node, a] * TILE, TILE), TILE)
        cols = pl.ds(pl.multiple_of(patterns_ref[node, b] * TILE, TILE), TILE)
        place(high_ref, low_ref, node, a, b, whole_ref[rows, cols])
        return 0

    lax.fori_loop(0, nodes * sides * sides, one, 0)


def assemble_full(patterns, source):
    nodes, sides = patterns.shape
    side = sides * TILE
    return call(
        functools.partial(assemble_full_kernel, nodes, sides),
        "assemble_full",
        [("smem", patterns), ("vmem", source)],
        [pltpu.VMEM((nodes, side, side), jnp.bfloat16)] * 2,
        [VMEM] * 2,
    )


def halves_kernel(factor_ref, high_ref, low_ref):
    step = 4 * TILE
    for start in range(0, factor_ref.shape[1], step):
        where = slice(start, start + step)
        high_ref[:, where], low_ref[:, where] = split(factor_ref[:, where])


def factor_halves(factor, after=()):
    out = [pltpu.VMEM(factor.shape, jnp.bfloat16)] * 2
    return call(halves_kernel, "factor_halves", [("vmem", factor)], out, [VMEM] * 2, after)


def product_kernel(nodes, sides, phase, widths_ref, slots_ref, high_ref, low_ref, f_high_ref, f_low_ref, before_ref, *refs):
    out_ref, marg_ref, product_ref, sems = refs[-4:]
    dot = functools.partial(jnp.dot, preferred_element_type=jnp.float32)
    most = 4
    marg_ref[...] = before_ref[...]

    def tile_rows(node, slot):
        return pl.ds(pl.multiple_of(slots_ref[1, node * sides + slot] * TILE, TILE), TILE)

    def copies(node, first, tile, height, width):
        cols = pl.ds(pl.multiple_of(tile * TILE, TILE), width * TILE)
        for i in range(height):
            rows = tile_rows(node, first + i)
            yield pltpu.make_async_copy(product_ref.at[rows, cols], out_ref.at[rows, cols], sems.at[tile, i])

    def multiply(node, first, tile, height, width):
        cols = pl.ds(pl.multiple_of(tile * TILE, TILE), width * TILE)
        rows = pl.ds(pl.multiple_of(first * TILE, TILE), height * TILE)
        high, low = high_ref[node, rows, :], low_ref[node, rows, :]
        f_high, f_low = f_high_ref[:, cols], f_low_ref[:, cols]
        product = -(dot(high, f_high) + (dot(high, f_low) + dot(low, f_high)))
        total = jnp.zeros((1, width * TILE), jnp.float32)
        for i in range(height):
            part = product[i * TILE : (i + 1) * TILE, :]
            here = tile_rows(node, first + i)
            product_ref[here, cols] = part
            factor = f_high_ref[here, cols].astype(jnp.float32) + f_low_ref[here, cols].astype(jnp.float32)
            total = total + jnp.sum(factor * part, axis=0, keepdims=True)
        for k in range(width):
            row = pl.ds(tile + k, 1)
            marg_ref[row, :] = marg_ref[row, :] - total[:, k * TILE : (k + 1) * TILE]
        for copy in copies(node, first, tile, height, width):
            copy.start()

    def finish(*place):
        for copy in copies(*place):
            copy.wait()

    def each(step):
        def one(node, start):
            width = widths_ref[0, node]
            first, height = sum((slots_ref[2 + p, node] for p in range(phase)), 0), slots_ref[2 + phase, node]
            for h in range(1, sides + 1):

                @pl.when(height == h)
                def _():
                    def whole(i, _):
                        step(node, first, start + most * i, h, most)
                        return 0

                    lax.fori_loop(0, width // most, whole, 0)
                    rest = width % most
                    for w in range(1, most):
                        pl.when(rest == w)(lambda: step(node, first, start + width - rest, h, w))

            return start + width

        lax.fori_loop(0, nodes, one, 0)

    each(multiply)
    each(finish)


def products(phase, widths, slots, blocks, factors, before, out=()):
    rows, cols = factors[0].shape
    nodes, sides = widths.shape[1], rows // TILE
    given = [("smem", widths), ("smem", slots)]
    given += [("vmem", x) for x in (*blocks, *factors, before)] + [("any", x) for x in out]
    return call(
        functools.partial(product_kernel, nodes, sides, phase),
        f"products_{phase}",
        given,
        [jax.ShapeDtypeStruct((rows, cols), jnp.float32), jax.ShapeDtypeStruct((cols // TILE, TILE), jnp.float32)],
        [pl.BlockSpec(memory_space=pl.ANY), VMEM],
        vmem=14,
        scratch_shapes=[pltpu.VMEM((rows, cols), jnp.float32), pltpu.SemaphoreType.DMA((cols // TILE, sides))],
        input_output_aliases={len(given) - 1: 0} if out else {},
    )


def swap(value, mask):
    return lax.ppermute(value, "pr", [(i, i ^ mask) for i in range(DEVICES)])


def move(value, places):
    pairs = [(4 * old + k, 4 * new + k) for old, new in places.items() for k in range(4)]
    return lax.ppermute(value, "pr", pairs)


def plan_jobs(me, patterns, after):
    nodes, sides = patterns.shape
    shapes = [
        jax.ShapeDtypeStruct((LISTS * len(KINDS), nodes * sides), jnp.int32),
        jax.ShapeDtypeStruct((LISTS * len(KINDS),), jnp.int32),
        jax.ShapeDtypeStruct((2 + len(ROUNDS), nodes * sides), jnp.int32),
    ]
    given = [("smem", me), ("smem", piece_table()), ("smem", patterns)]
    return call(functools.partial(jobs_kernel, nodes, sides), "plan_jobs", given, shapes, [SMEM] * 3, after)


def turn(name, kernel, me, given, rows, held, after=()):
    shapes = [pltpu.VMEM((n, TILE), jnp.float32) for n in rows] + [pltpu.VMEM(x.shape, x.dtype) for x in held]

    def body(me_ref, *refs):
        place = me_ref[0] >> 2
        kernel((place == 1) | (place == 2), *refs[: len(given)], *refs[len(given) + len(held) :][: len(rows)])

    inputs = [("smem", me)] + [("vmem", x) for x in (*given, *held)]
    aliases = {1 + len(given) + i: len(rows) + i for i in range(len(held))}
    return call(body, name, inputs, shapes, [VMEM] * len(shapes), after, input_output_aliases=aliases)


def copy_rows(target_ref, row, source_ref, first=0, count=None):
    count = source_ref.shape[0] - first if count is None else count
    target_ref[row : row + count, :] = source_ref[first : first + count, :]
    return row + count


def turn_1(inner, near_ref, side_ref, part_ref, held_ref, far_ref, far_first_ref):
    copy_rows(part_ref, 0, near_ref, 0, part_ref.shape[0])
    copy_rows(held_ref, copy_rows(held_ref, 0, near_ref), side_ref)
    first, rest = piece_rows("far"), piece_rows("far_rest")
    copy_rows(far_ref, 0, near_ref, 0, first)
    copy_rows(far_ref, first, near_ref, near_ref.shape[0] - rest, rest)
    copy_rows(far_first_ref, 0, near_ref, 0, first)


def turn_2(inner, mid_ref, mid_outer_ref, far_ref, far_outer_ref, side_near_ref, part_ref, held_ref, rest_ref):
    mid, far, onward = piece_rows("mid"), piece_rows("far"), piece_rows("side_mid")

    def take(m_ref, f_ref):
        copy_rows(part_ref, copy_rows(part_ref, 0, m_ref, 0, onward), f_ref, 0, far)
        copy_rows(held_ref, 0, m_ref)
        copy_rows(held_ref, mid + side_near_ref.shape[0], f_ref, 0, far)

    pl.when(inner)(lambda: take(mid_ref, far_ref))
    pl.when(jnp.logical_not(inner))(lambda: take(mid_outer_ref, far_outer_ref))
    copy_rows(held_ref, mid, side_near_ref)
    copy_rows(rest_ref, 0, far_ref, far)


def turn_3(inner, side_last_ref, rest_ref, rest_outer_ref, held_ref):
    row = copy_rows(held_ref, 0, side_last_ref)

    def take(ref):
        copy_rows(held_ref, row, ref)

    pl.when(inner)(lambda: take(rest_ref))
    pl.when(jnp.logical_not(inner))(lambda: take(rest_outer_ref))


def planned(sep_inv, factor, widths, patterns, dinv):
    me = lax.axis_index("pr").astype(jnp.int32).reshape(1)
    between_inner, outward, across = {1: 2, 2: 1}, {1: 0, 2: 3}, {1: 3, 2: 0}

    near, side, mid = pack((("near",), ("side",), ("mid",)), me, sep_inv)
    rows_other = swap(sep_inv, 1)
    near, side, mid = swap(near, 4), swap(side, 2), move(mid, between_inner)
    plan = plan_jobs(me, patterns, (rows_other,))
    factors = factor_halves(factor, plan[1:2])
    blocks = assemble((("rows",),), me, plan, patterns, (sep_inv, rows_other), (), factors[:1])
    rows = (piece_rows("side_near"), piece_rows(*ROUNDS[0]), piece_rows("far", "far_rest"), piece_rows("far"))
    part, held, far, far_first, mid = turn("turn_1", turn_1, me, (near, side), rows, (mid,), blocks[:1])

    def put(sets, sources, blocks, after=()):
        return assemble(sets, me, plan, patterns, sources, blocks, after)

    side_near, mid_outer = swap(part, 2), move(mid, outward)
    far, far_outer = move(far, between_inner), move(far_first, across)
    blocks = put(ROUNDS[:1], (held, swap(held, 1)), blocks)
    out, marg = products(0, widths, plan[2], blocks, factors, dinv)
    rows = (piece_rows("side_mid", "side_far"), piece_rows(*ROUNDS[1]), piece_rows("far_rest"))
    part, held, rest = turn("turn_2", turn_2, me, (mid, mid_outer, far, far_outer, side_near), rows, (), (marg,))

    side_last, rest_outer = swap(part, 2), move(rest, outward)
    blocks = put(ROUNDS[1:2], (held, swap(held, 1)), blocks, (marg,))
    out, marg = products(1, widths, plan[2], blocks, factors, marg, (out,))
    (held,) = turn("turn_3", turn_3, me, (side_last, rest, rest_outer), (piece_rows(*ROUNDS[2]),), (), (marg,))
    blocks = put(ROUNDS[2:], (held, swap(held, 1)), blocks, (marg,))
    return products(2, widths, plan[2], blocks, factors, marg, (out,))


def shards(sep_inv, factor, widths, patterns, dinv):
    own_rows, order = sep_inv.shape
    cols = factor.shape[1]
    dinv = dinv.reshape(cols // TILE, TILE)
    if own_rows == TILE and order == DEVICES * TILE:
        out, marg = planned(sep_inv, factor, widths, patterns, dinv)
    else:
        nodes, sides = patterns.shape
        blocks = assemble_full(patterns, lax.all_gather(sep_inv, "pr", axis=0, tiled=True))
        order = jnp.tile(jnp.arange(sides, dtype=jnp.int32), nodes)
        slots = jnp.stack([order, order, jnp.full_like(order, sides)])
        out, marg = products(0, widths, slots, blocks, factor_halves(factor), dinv)
    return out, marg.reshape(cols)


def solution(mesh):
    placed = (
        P(("cfg", "pr"), None),
        P("cfg", "pr"),
        P("pr", None),
        P("pr", None),
        P(("cfg", "pr")),
    )
    return jax.shard_map(
        shards,
        mesh=mesh,
        in_specs=placed,
        out_specs=(P("cfg", "pr"), P(("cfg", "pr"))),
        check_vma=False,
    )
```

time: 78 us -> 72.4 us (0.928)
  waiting for transfers between devices: 23.8 us -> 13.8 us
  Pallas kernels: 32.7 us -> 38.5 us
  starting transfers between devices: 16.6 us -> 12.7 us
  local copies, waits for them, and re-layouts: 4.2 us -> 6.03 us
    ppermute x8, waiting for transfers between devices: 16.7 us -> 9.13 us  [swap(): return lax.ppermute(value, 'pr', [(i, i ^ mask) for i in range(DEVICES)])]
    pallas_call x10 -> x13, Pallas kernels: 32.7 us -> 38.5 us  [call(): pl.pallas_call(body, out_shape=out_shape, in_specs=[pl.BlockSpec(memory_s...]
    ppermute x5, starting transfers between devices: 9.56 us -> 5.22 us  [move(): return lax.ppermute(value, 'pr', pairs)]
    ppermute x5, waiting for transfers between devices: 7.16 us -> 4.69 us  [move(): return lax.ppermute(value, 'pr', pairs)]
    unnamed x19 -> x13, local copies, waits for them, and re-layouts: 4.2 us -> 6.03 us
  transfers between devices with their start and end apart: 13 -> 13, of which waited for: 6 -> 5; matrix products, arithmetic and copies ran while one was open for 1% -> 1% of each run, Pallas kernels for 19% -> 39%
where the time goes in v4:
time: 72.4 us; the launch traced here: 72.1 us
  Pallas kernels  38.5 us (53%)
  waiting for transfers between devices  13.8 us (19%)
  starting transfers between devices  12.7 us (18%)
  local copies, waits for them, and re-layouts  6.03 us (8%)
  between operations  1.04 us (1%)
    pallas_call x13, Pallas kernels, call(): pl.pallas_call(body, out_shape=out_shape, in_specs=[pl.BlockSpec(memory_s...  38.5 us
    ppermute x8, waiting for transfers between devices, swap(): return lax.ppermute(value, 'pr', [(i, i ^ mask) for i in range(DEVICES)])  9.13 us
    ppermute x8, starting transfers between devices, swap(): return lax.ppermute(value, 'pr', [(i, i ^ mask) for i in range(DEVICES)])  7.45 us
    unnamed x13, local copies, waits for them, and re-layouts  6.03 us
    ppermute x5, starting transfers between devices, move(): return lax.ppermute(value, 'pr', pairs)  5.22 us
    ppermute x5, waiting for transfers between devices, move(): return lax.ppermute(value, 'pr', pairs)  4.69 us
  transfers between devices with their start and end apart: 13, of which 5 were waited for; matrix products, arithmetic and copies ran while one was open for 1% of the time, Pallas kernels for 39%

profile of v4, /device:TPU:0, one launch (start us, length us, event | category | flops | bytes accessed | tf_op | source)
XLA Modules:
  0.0 72.1 jit_solution(5108967688703796405)
XLA Ops:
  1.1 1.2 %copy-done.1 = f32[128,2048]{1,0:T(8,128)S(1)} copy-done((f32[128,2048]{1,0:T(8,128)S(1)}, f32[128,2048]{1,0:T(8,128)}, u32[]{:S(2)}) %copy-start.1) | copy-done | bytes 1048600
  2.4 1.6 %pack.1 = (f32[1728,128]{1,0:T(8,128)}, f32[1472,128]{1,0:T(8,128)}, f32[960,128]{1,0:T(8,128)}) custom-call(s32[1]{0:T(128)} %bitcast.refs_0_, f32[128,2048]{1,0:T(8,128)S(1)} %copy-done.1), custom_call_target="tpu_custom_call" | custom-call | tf_op jit(solution)/shard_map/pack/pallas_call | solution.py:71
  3.9 2.6 %collective-permute-start.1 = (f32[1728,128]{1,0:T(8,128)}, f32[1728,128]{1,0:T(8,128)S(1)}, u32[]{:S(2)}, u32[]{:S(2)}) collective-permute-start(f32[1728,128]{1,0:T(8,128)} %get-tuple-element.35), channel_id=1, source_target_pairs={{0,4},{1,5},{2,6},{3,7},{4,0},{5,1},{6,2},{7,3},{8,12},{9,13},{10,... | collective-permute-start | bytes 2654216 | tf_op jit(solution)/shard_map/ppermute | solution.py:380
  6.5 1.5 %collective-permute-start.2 = (f32[1472,128]{1,0:T(8,128)}, f32[1472,128]{1,0:T(8,128)S(1)}, u32[]{:S(2)}, u32[]{:S(2)}) collective-permute-start(f32[1472,128]{1,0:T(8,128)} %get-tuple-element.36), channel_id=1, source_target_pairs={{0,2},{1,3},{2,0},{3,1},{4,6},{5,7},{6,4},{7,5},{8,10},{9,11},{10,... | collective-permute-start | bytes 2261000 | tf_op jit(solution)/shard_map/ppermute | solution.py:380
  8.7 0.8 %copy.17.refs_2_ = s32[8,4]{1,0:T(8,128)S(1)} copy(s32[8,4]{0,1:T(4,128)} %param.9) | data formatting | bytes 256 | tf_op args[3]
  10.2 3.7 %plan_jobs.1 = (s32[54,32]{1,0:T(8,128)S(1)}, s32[54]{0:T(128)S(1)}, s32[5,32]{1,0:T(8,128)S(1)}) custom-call(s32[1]{0:T(128)} %bitcast.refs_0_, s32[64]{0:T(128)S(1)} %copy-done.5, s32[8,4]{1,0:T(8,128)S(1)} %copy.17.refs_2_, f32[128,2048]{1,0:T(8,128)S(1)} %collective-permute-done.refs_3_.refs_5_), custom_call_target="tpu_custom_call" | custom-call | tf_op jit(solution)/shard_map/plan_jobs/pallas_call | solution.py:71
  13.9 3.4 %copy-done = f32[512,4096]{1,0:T(8,128)S(1)} copy-done((f32[512,4096]{1,0:T(8,128)S(1)}, f32[512,4096]{1,0:T(8,128)}, u32[]{:S(2)}) %copy-start) | copy-done | bytes 8388632
  17.2 1.3 %factor_halves.1 = (bf16[512,4096]{1,0:T(8,128)(2,1)S(1)}, bf16[512,4096]{1,0:T(8,128)(2,1)S(1)}) custom-call(f32[512,4096]{1,0:T(8,128)S(1)} %copy-done, s32[54]{0:T(128)S(1)} %get-tuple-element.34.refs_1_.refs_2_), custom_call_target="tpu_custom_call" | custom-call | tf_op jit(solution)/shard_map/factor_halves/pallas_call | solution.py:71
  18.6 2.1 %assemble_rows.1 = (bf16[8,512,512]{2,1,0:T(8,128)(2,1)S(1)}, bf16[8,512,512]{2,1,0:T(8,128)(2,1)S(1)}) custom-call(s32[1]{0:T(128)} %bitcast.refs_0_, s32[54,32]{1,0:T(8,128)S(1)} %get-tuple-element.33.refs_1_, s32[54]{0:T(128)S(1)} %get-tuple-element.34.refs_1_.refs_2_, s32[5,32]{1,0:T(8,128)S(1)} %get-tuple-element.32.refs_3_.refs_1_, ...), custom_call_target="tpu_custom_call" | custom-call | tf_op jit(solution)/shard_map/assemble_rows/pallas_call | solution.py:71
  20.7 5.0 %collective-permute-done.2.refs_2_ = f32[1472,128]{1,0:T(8,128)S(1)} collective-permute-done((f32[1472,128]{1,0:T(8,128)}, f32[1472,128]{1,0:T(8,128)S(1)}, u32[]{:S(2)}, u32[]{:S(2)}) %collective-permute-start.2) | collective-permute-done | bytes 753696 | tf_op jit(solution)/shard_map/ppermute | solution.py:380
  25.7 1.3 %collective-permute-done.1.refs_1_ = f32[1728,128]{1,0:T(8,128)S(1)} collective-permute-done((f32[1728,128]{1,0:T(8,128)}, f32[1728,128]{1,0:T(8,128)S(1)}, u32[]{:S(2)}, u32[]{:S(2)}) %collective-permute-start.1) | collective-permute-done | bytes 884768 | tf_op jit(solution)/shard_map/ppermute | solution.py:380
  27.3 1.8 %collective-permute-start.7 = (f32[1216,128]{1,0:T(8,128)S(1)}, f32[1216,128]{1,0:T(8,128)S(1)}, u32[]{:S(2)}, u32[]{:S(2)}) collective-permute-start(f32[1216,128]{1,0:T(8,128)S(1)} %get-tuple-element.43), channel_id=1, source_target_pairs={{0,2},{1,3},{2,0},{3,1},{4,6},{5,7},{6,4},{7,5},{8,10},{9,11},{10,... | collective-permute-start | bytes 1867784 | tf_op jit(solution)/shard_map/ppermute | solution.py:380
  29.1 1.3 %collective-permute-start.4 = (f32[960,128]{1,0:T(8,128)S(1)}, f32[960,128]{1,0:T(8,128)S(1)}, u32[]{:S(2)}, u32[]{:S(2)}) collective-permute-start(f32[960,128]{1,0:T(8,128)S(1)} %get-tuple-element.40.refs_1_), channel_id=1, source_target_pairs={{4,0},{5,1},{6,2},{7,3},{8,12},{9,13},{10,14},{11,15},{20,16},{21,... | collective-permute-start | bytes 1474568 | tf_op jit(solution)/shard_map/ppermute | solution.py:385
  31.0 1.3 %collective-permute-start.6 = (f32[192,128]{1,0:T(8,128)S(1)}, f32[192,128]{1,0:T(8,128)S(1)}, u32[]{:S(2)}, u32[]{:S(2)}) collective-permute-start(f32[192,128]{1,0:T(8,128)S(1)} %get-tuple-element.42), channel_id=1, source_target_pairs={{4,12},{5,13},{6,14},{7,15},{8,0},{9,1},{10,2},{11,3},{20,28},{21,... | collective-permute-start | bytes 294920 | tf_op jit(solution)/shard_map/ppermute | solution.py:385
  32.4 2.8 %assemble_near.1 = (bf16[8,512,512]{2,1,0:T(8,128)(2,1)S(1)}, bf16[8,512,512]{2,1,0:T(8,128)(2,1)S(1)}) custom-call(s32[1]{0:T(128)} %bitcast.refs_0_, s32[54,32]{1,0:T(8,128)S(1)} %get-tuple-element.33.refs_1_, s32[54]{0:T(128)S(1)} %get-tuple-element.34.refs_1_.refs_2_, ...), custom_call_target="tpu_custom_call", output_to_operand_aliasing={{0}: (6, {}), {1}: (7, {})} | custom-call | tf_op jit(solution)/shard_map/assemble_near/pallas_call | solution.py:71
  35.2 7.7 %products_0.1 = (f32[512,4096]{1,0:T(8,128)}, f32[32,128]{1,0:T(8,128)S(1)}) custom-call(s32[1,8]{1,0:T(1,128)S(1)} %copy-done.4, s32[5,32]{1,0:T(8,128)S(1)} %get-tuple-element.32.refs_3_.refs_1_, bf16[8,512,512]{2,1,0:T(8,128)(2,1)S(1)} %get-tuple-element.46.refs_2_.refs_6_, bf16[8,512,512]{2,1,0:T(8,128)(2,1)S(1)} %get-tuple-element.47.refs_3_.refs_7_, ...), custom_call_target="tpu_custom_call" | custom-call | tf_op jit(solution)/shard_map/products_0/pallas_call | solution.py:71
  42.9 4.7 %collective-permute-done.6.refs_4_ = f32[192,128]{1,0:T(8,128)S(1)} collective-permute-done((f32[192,128]{1,0:T(8,128)S(1)}, f32[192,128]{1,0:T(8,128)S(1)}, u32[]{:S(2)}, u32[]{:S(2)}) %collective-permute-start.6) | collective-permute-done | bytes 98336 | tf_op jit(solution)/shard_map/ppermute | solution.py:385
  48.6 1.3 %collective-permute-start.10 = (f32[512,128]{1,0:T(8,128)S(1)}, f32[512,128]{1,0:T(8,128)S(1)}, u32[]{:S(2)}, u32[]{:S(2)}) collective-permute-start(f32[512,128]{1,0:T(8,128)S(1)} %get-tuple-element.51.refs_2_), channel_id=1, source_target_pairs={{4,0},{5,1},{6,2},{7,3},{8,12},{9,13},{10,14},{11,15},{20,16},{21,... | collective-permute-start | bytes 786440 | tf_op jit(solution)/shard_map/ppermute | solution.py:385
  49.9 1.0 %collective-permute-done.11.refs_5_ = f32[2368,128]{1,0:T(8,128)S(1)} collective-permute-done((f32[2368,128]{1,0:T(8,128)S(1)}, f32[2368,128]{1,0:T(8,128)S(1)}, u32[]{:S(2)}, u32[]{:S(2)}) %collective-permute-start.11) | collective-permute-done | bytes 1212448 | tf_op jit(solution)/shard_map/ppermute | solution.py:380
  50.9 2.4 %assemble_mid.1 = (bf16[8,512,512]{2,1,0:T(8,128)(2,1)S(1)}, bf16[8,512,512]{2,1,0:T(8,128)(2,1)S(1)}) custom-call(s32[1]{0:T(128)} %bitcast.refs_0_, s32[54,32]{1,0:T(8,128)S(1)} %get-tuple-element.33.refs_1_, s32[54]{0:T(128)S(1)} %get-tuple-element.34.refs_1_.refs_2_, ...), custom_call_target="tpu_custom_call", output_to_operand_aliasing={{0}: (6, {}), {1}: (7, {})} | custom-call | tf_op jit(solution)/shard_map/assemble_mid/pallas_call | solution.py:71
  53.3 6.6 %products_1.1 = (f32[512,4096]{1,0:T(8,128)}, f32[32,128]{1,0:T(8,128)S(1)}) custom-call(s32[1,8]{1,0:T(1,128)S(1)} %copy-done.4, s32[5,32]{1,0:T(8,128)S(1)} %get-tuple-element.32.refs_3_.refs_1_, bf16[8,512,512]{2,1,0:T(8,128)(2,1)S(1)} %get-tuple-element.53.refs_2_.refs_6_, ...), custom_call_target="tpu_custom_call", output_to_operand_aliasing={{0}: (7, {})} | custom-call | tf_op jit(solution)/shard_map/products_1/pallas_call | solution.py:71
  60.4 1.7 %collective-permute-done.12.refs_5_ = f32[1152,128]{1,0:T(8,128)S(1)} collective-permute-done((f32[1152,128]{1,0:T(8,128)S(1)}, f32[1152,128]{1,0:T(8,128)S(1)}, u32[]{:S(2)}, u32[]{:S(2)}) %collective-permute-start.12) | collective-permute-done | bytes 589856 | tf_op jit(solution)/shard_map/ppermute | solution.py:380
  62.1 1.9 %assemble_side_mid.1 = (bf16[8,512,512]{2,1,0:T(8,128)(2,1)S(1)}, bf16[8,512,512]{2,1,0:T(8,128)(2,1)S(1)}) custom-call(s32[1]{0:T(128)} %bitcast.refs_0_, s32[54,32]{1,0:T(8,128)S(1)} %get-tuple-element.33.refs_1_, s32[54]{0:T(128)S(1)} %get-tuple-element.34.refs_1_.refs_2_, ...), custom_call_target="tpu_custom_call", output_to_operand_aliasing={{0}: (6, {}), {1}: (7, {})} | custom-call | tf_op jit(solution)/shard_map/assemble_side_mid/pallas_call | solution.py:71
  64.0 7.8 %products_2.1 = (f32[512,4096]{1,0:T(8,128)}, f32[32,128]{1,0:T(8,128)}) custom-call(s32[1,8]{1,0:T(1,128)S(1)} %copy-done.4, s32[5,32]{1,0:T(8,128)S(1)} %get-tuple-element.32.refs_3_.refs_1_, bf16[8,512,512]{2,1,0:T(8,128)(2,1)S(1)} %get-tuple-element.57.refs_2_, ...), custom_call_target="tpu_custom_call", output_to_operand_aliasing={{0}: (7, {})} | custom-call | tf_op jit(solution)/shard_map/products_2/pallas_call | solution.py:71
  (28 shorter events, 4.2 us)
Async XLA Ops:
  0.6 8.9 %collective-permute-start = (f32[128,2048]{1,0:T(8,128)}, f32[128,2048]{1,0:T(8,128)S(1)}, u32[]{:S(2)}, u32[]{:S(2)}) collective-permute-start(f32[128,2048]{1,0:T(8,128)} %refs_4_.1), channel_id=1, source_target_pairs={{0,1},{1,0},{2,3},{3,2},{4,5},{5,4},{6,7},{7,6},{8,9},{9,8},{10,11... | collective-permute-start | bytes 3145736 | tf_op jit(solution)/shard_map/ppermute | solution.py:380
  1.1 1.2 %copy-start.1 = (f32[128,2048]{1,0:T(8,128)S(1)}, f32[128,2048]{1,0:T(8,128)}, u32[]{:S(2)}) copy-start(f32[128,2048]{1,0:T(8,128)} %refs_4_.1) | copy-start | bytes 3145732
  3.9 23.1 %collective-permute-start.1 = (f32[1728,128]{1,0:T(8,128)}, f32[1728,128]{1,0:T(8,128)S(1)}, u32[]{:S(2)}, u32[]{:S(2)}) collective-permute-start(f32[1728,128]{1,0:T(8,128)} %get-tuple-element.35), channel_id=1, source_target_pairs={{0,4},{1,5},{2,6},{3,7},{4,0},{5,1},{6,2},{7,3},{8,12},{9,13},{10,... | collective-permute-start | bytes 2654216 | tf_op jit(solution)/shard_map/ppermute | solution.py:380
  6.5 19.2 %collective-permute-start.2 = (f32[1472,128]{1,0:T(8,128)}, f32[1472,128]{1,0:T(8,128)S(1)}, u32[]{:S(2)}, u32[]{:S(2)}) collective-permute-start(f32[1472,128]{1,0:T(8,128)} %get-tuple-element.36), channel_id=1, source_target_pairs={{0,2},{1,3},{2,0},{3,1},{4,6},{5,7},{6,4},{7,5},{8,10},{9,11},{10,... | collective-permute-start | bytes 2261000 | tf_op jit(solution)/shard_map/ppermute | solution.py:380
  8.1 12.6 %collective-permute-start.3 = (f32[960,128]{1,0:T(8,128)}, f32[960,128]{1,0:T(8,128)S(1)}, u32[]{:S(2)}, u32[]{:S(2)}) collective-permute-start(f32[960,128]{1,0:T(8,128)} %get-tuple-element.37), channel_id=1, source_target_pairs={{4,8},{5,9},{6,10},{7,11},{8,4},{9,5},{10,6},{11,7},{20,24},{21,25... | collective-permute-start | bytes 1474568 | tf_op jit(solution)/shard_map/ppermute | solution.py:385
  9.5 0.7 copy-start.5
  13.9 3.4 %copy-start = (f32[512,4096]{1,0:T(8,128)S(1)}, f32[512,4096]{1,0:T(8,128)}, u32[]{:S(2)}) copy-start(f32[512,4096]{1,0:T(8,128)} %refs_0_.4) | copy-start | bytes 25165828
  17.2 1.3 %copy-start.2 = (f32[128,2048]{1,0:T(8,128)S(1)}, f32[128,2048]{1,0:T(8,128)}, u32[]{:S(2)}) copy-start(f32[128,2048]{1,0:T(8,128)} %refs_4_.1) | copy-start | bytes 3145732
  27.2 5.1 %collective-permute-start.8 = (f32[3200,128]{1,0:T(8,128)S(1)}, f32[3200,128]{1,0:T(8,128)S(1)}, u32[]{:S(2)}, u32[]{:S(2)}) collective-permute-start(f32[3200,128]{1,0:T(8,128)S(1)} %get-tuple-element.44.refs_4_), channel_id=1, source_target_pairs={{0,1},{1,0},{2,3},{3,2},{4,5},{5,4},{6,7},{7,6},{8,9},{9,8},{10,11... | collective-permute-start | bytes 4915208 | tf_op jit(solution)/shard_map/ppermute | solution.py:380
  27.3 20.3 %collective-permute-start.7 = (f32[1216,128]{1,0:T(8,128)S(1)}, f32[1216,128]{1,0:T(8,128)S(1)}, u32[]{:S(2)}, u32[]{:S(2)}) collective-permute-start(f32[1216,128]{1,0:T(8,128)S(1)} %get-tuple-element.43), channel_id=1, source_target_pairs={{0,2},{1,3},{2,0},{3,1},{4,6},{5,7},{6,4},{7,5},{8,10},{9,11},{10,... | collective-permute-start | bytes 1867784 | tf_op jit(solution)/shard_map/ppermute | solution.py:380
  29.1 18.6 %collective-permute-start.4 = (f32[960,128]{1,0:T(8,128)S(1)}, f32[960,128]{1,0:T(8,128)S(1)}, u32[]{:S(2)}, u32[]{:S(2)}) collective-permute-start(f32[960,128]{1,0:T(8,128)S(1)} %get-tuple-element.40.refs_1_), channel_id=1, source_target_pairs={{4,0},{5,1},{6,2},{7,3},{8,12},{9,13},{10,14},{11,15},{20,16},{21,... | collective-permute-start | bytes 1474568 | tf_op jit(solution)/shard_map/ppermute | solution.py:385
  30.3 17.3 %collective-permute-start.5 = (f32[704,128]{1,0:T(8,128)S(1)}, f32[704,128]{1,0:T(8,128)S(1)}, u32[]{:S(2)}, u32[]{:S(2)}) collective-permute-start(f32[704,128]{1,0:T(8,128)S(1)} %get-tuple-element.41), channel_id=1, source_target_pairs={{4,8},{5,9},{6,10},{7,11},{8,4},{9,5},{10,6},{11,7},{20,24},{21,25... | collective-permute-start | bytes 1081352 | tf_op jit(solution)/shard_map/ppermute | solution.py:385
  31.0 16.6 %collective-permute-start.6 = (f32[192,128]{1,0:T(8,128)S(1)}, f32[192,128]{1,0:T(8,128)S(1)}, u32[]{:S(2)}, u32[]{:S(2)}) collective-permute-start(f32[192,128]{1,0:T(8,128)S(1)} %get-tuple-element.42), channel_id=1, source_target_pairs={{4,12},{5,13},{6,14},{7,15},{8,0},{9,1},{10,2},{11,3},{20,28},{21,... | collective-permute-start | bytes 294920 | tf_op jit(solution)/shard_map/ppermute | solution.py:385
  32.3 2.8 %copy-start.3 = (f32[4096]{0:T(1024)S(1)}, f32[4096]{0:T(1024)}, u32[]{:S(2)}) copy-start(f32[4096]{0:T(1024)} %param.10) | copy-start | bytes 49156
  32.4 2.8 %copy-start.4 = (s32[1,8]{1,0:T(1,128)S(1)}, s32[1,8]{1,0:T(1,128)}, u32[]{:S(2)}) copy-start(s32[1,8]{1,0:T(1,128)} %refs_0_.7) | copy-start | bytes 100
  48.0 3.0 %collective-permute-start.11 = (f32[2368,128]{1,0:T(8,128)S(1)}, f32[2368,128]{1,0:T(8,128)S(1)}, u32[]{:S(2)}, u32[]{:S(2)}) collective-permute-start(f32[2368,128]{1,0:T(8,128)S(1)} %get-tuple-element.52.refs_4_), channel_id=1, source_target_pairs={{0,1},{1,0},{2,3},{3,2},{4,5},{5,4},{6,7},{7,6},{8,9},{9,8},{10,11... | collective-permute-start | bytes 3637256 | tf_op jit(solution)/shard_map/ppermute | solution.py:380
  48.0 11.9 %collective-permute-start.9 = (f32[640,128]{1,0:T(8,128)S(1)}, f32[640,128]{1,0:T(8,128)S(1)}, u32[]{:S(2)}, u32[]{:S(2)}) collective-permute-start(f32[640,128]{1,0:T(8,128)S(1)} %get-tuple-element.50), channel_id=1, source_target_pairs={{0,2},{1,3},{2,0},{3,1},{4,6},{5,7},{6,4},{7,5},{8,10},{9,11},{10,... | collective-permute-start | bytes 983048 | tf_op jit(solution)/shard_map/ppermute | solution.py:380
  48.6 11.3 %collective-permute-start.10 = (f32[512,128]{1,0:T(8,128)S(1)}, f32[512,128]{1,0:T(8,128)S(1)}, u32[]{:S(2)}, u32[]{:S(2)}) collective-permute-start(f32[512,128]{1,0:T(8,128)S(1)} %get-tuple-element.51.refs_2_), channel_id=1, source_target_pairs={{4,0},{5,1},{6,2},{7,3},{8,12},{9,13},{10,14},{11,15},{20,16},{21,... | collective-permute-start | bytes 786440 | tf_op jit(solution)/shard_map/ppermute | solution.py:385
  60.0 2.1 %collective-permute-start.12 = (f32[1152,128]{1,0:T(8,128)S(1)}, f32[1152,128]{1,0:T(8,128)S(1)}, u32[]{:S(2)}, u32[]{:S(2)}) collective-permute-start(f32[1152,128]{1,0:T(8,128)S(1)} %turn_3.1.refs_4_), channel_id=1, source_target_pairs={{0,1},{1,0},{2,3},{3,2},{4,5},{5,4},{6,7},{7,6},{8,9},{9,8},{10,11... | collective-permute-start | bytes 1769480 | tf_op jit(solution)/shard_map/ppermute | solution.py:380

commit v5 on v4

--- a/solution.py
+++ b/solution.py
@@ -186,8 +186,7 @@
     high_ref[node, rows, cols], low_ref[node, rows, cols] = split(value)
 
 
-def assemble_kernel(sets, nodes, sides, me_ref, jobs_ref, count_ref, slots_ref, *refs):
-    sources, (high_ref, low_ref) = refs[:-2], refs[-2:]
+def put_tiles(sets, nodes, sides, me_ref, jobs_ref, count_ref, sources, high_ref, low_ref):
     even = (me_ref[0] & 1) == 0
 
     def work(name, pair, start):
@@ -244,21 +243,6 @@
         at += 2
 
 
-def assemble(sets, me, plan, patterns, sources, blocks, after=()):
-    nodes, sides = patterns.shape
-    side = sides * TILE
-    given = [("smem", x) for x in (me, *plan)] + [("vmem", x) for x in (*sources, *blocks)]
-    return call(
-        functools.partial(assemble_kernel, sets, nodes, sides),
-        "assemble_" + sets[0][0],
-        given,
-        [pltpu.VMEM((nodes, side, side), jnp.bfloat16)] * 2,
-        [VMEM] * 2,
-        after,
-        input_output_aliases={len(given) - len(blocks) + i: i for i in range(len(blocks))},
-    )
-
-
 def assemble_full_kernel(nodes, sides, patterns_ref, whole_ref, high_ref, low_ref):
     def one(step, _):
         node = step // (sides * sides)
@@ -296,20 +280,11 @@
     return call(halves_kernel, "factor_halves", [("vmem", factor)], out, [VMEM] * 2, after)
 
 
-def product_kernel(nodes, sides, phase, widths_ref, slots_ref, high_ref, low_ref, f_high_ref, f_low_ref, before_ref, *refs):
-    out_ref, marg_ref, product_ref, sems = refs[-4:]
+def multiply_rows(phase, sides, widths_ref, slots_ref, high_ref, low_ref, f_high_ref, f_low_ref, out_ref, marg_ref, product_ref, sem):
     dot = functools.partial(jnp.dot, preferred_element_type=jnp.float32)
-    most = 4
-    marg_ref[...] = before_ref[...]
-
-    def tile_rows(node, slot):
-        return pl.ds(pl.multiple_of(slots_ref[1, node * sides + slot] * TILE, TILE), TILE)
-
-    def copies(node, first, tile, height, width):
-        cols = pl.ds(pl.multiple_of(tile * TILE, TILE), width * TILE)
-        for i in range(height):
-            rows = tile_rows(node, first + i)
-            yield pltpu.make_async_copy(product_ref.at[rows, cols], out_ref.at[rows, cols], sems.at[tile, i])
+    nodes = widths_ref.shape[1]
+    most = 8
+    tall = 2
 
     def multiply(node, first, tile, height, width):
         cols = pl.ds(pl.multiple_of(tile * TILE, TILE), width * TILE)
@@ -320,59 +295,102 @@
         total = jnp.zeros((1, width * TILE), jnp.float32)
         for i in range(height):
             part = product[i * TILE : (i + 1) * TILE, :]
-            here = tile_rows(node, first + i)
+            here = pl.ds(pl.multiple_of(slots_ref[1, node * sides + first + i] * TILE, TILE), TILE)
             product_ref[here, cols] = part
             factor = f_high_ref[here, cols].astype(jnp.float32) + f_low_ref[here, cols].astype(jnp.float32)
             total = total + jnp.sum(factor * part, axis=0, keepdims=True)
+            pltpu.make_async_copy(product_ref.at[here, cols], out_ref.at[here, cols], sem).start()
         for k in range(width):
             row = pl.ds(tile + k, 1)
             marg_ref[row, :] = marg_ref[row, :] - total[:, k * TILE : (k + 1) * TILE]
-        for copy in copies(node, first, tile, height, width):
-            copy.start()
-
-    def finish(*place):
-        for copy in copies(*place):
-            copy.wait()
-
-    def each(step):
-        def one(node, start):
-            width = widths_ref[0, node]
-            first, height = sum((slots_ref[2 + p, node] for p in range(phase)), 0), slots_ref[2 + phase, node]
-            for h in range(1, sides + 1):
-
-                @pl.when(height == h)
-                def _():
-                    def whole(i, _):
-                        step(node, first, start + most * i, h, most)
-                        return 0
-
-                    lax.fori_loop(0, width // most, whole, 0)
-                    rest = width % most
-                    for w in range(1, most):
-                        pl.when(rest == w)(lambda: step(node, first, start + width - rest, h, w))
-
-            return start + width
-
-        lax.fori_loop(0, nodes, one, 0)
-
-    each(multiply)
-    each(finish)
-
-
-def products(phase, widths, slots, blocks, factors, before, out=()):
-    rows, cols = factors[0].shape
-    nodes, sides = widths.shape[1], rows // TILE
-    given = [("smem", widths), ("smem", slots)]
-    given += [("vmem", x) for x in (*blocks, *factors, before)] + [("any", x) for x in out]
+
+    def one(node, carry):
+        start, written = carry
+        width = widths_ref[0, node]
+        first, height = sum((slots_ref[2 + p, node] for p in range(phase)), 0), slots_ref[2 + phase, node]
+
+        def across(row, h):
+            def whole(i, _):
+                multiply(node, row, start + most * i, h, most)
+                return 0
+
+            lax.fori_loop(0, lax.div(width, most), whole, 0)
+            rest = lax.rem(width, most)
+            for w in range(1, most):
+                pl.when(rest == w)(lambda: multiply(node, row, start + width - rest, h, w))
+
+        def down(i, _):
+            across(first + tall * i, tall)
+            return 0
+
+        lax.fori_loop(0, lax.div(height, tall), down, 0)
+        for h in range(1, tall):
+            pl.when(lax.rem(height, tall) == h)(lambda: across(first + height - h, h))
+        return start + width, written + width * height
+
+    _, written = lax.fori_loop(0, nodes, one, (0, 0))
+
+    def finish():
+        rows, cols = product_ref.shape
+        size = 1
+        while size <= rows * cols // (TILE * TILE):
+            wide = min(size, cols // TILE)
+            part = (pl.ds(0, TILE * size // wide), pl.ds(0, TILE * wide))
+            pl.when((written & size) != 0)(lambda: pltpu.make_async_copy(product_ref.at[part], out_ref.at[part], sem).wait())
+            size *= 2
+
+    return finish
+
+
+def work_kernel(sets, phase, last, sides, *refs):
+    me_ref, jobs_ref, count_ref, slots_ref, widths_ref, *refs = refs
+    nodes = widths_ref.shape[1]
+    sources, refs = refs[: 2 * len(sets)], refs[2 * len(sets) :]
+    if phase is None:
+        put_tiles(sets, nodes, sides, me_ref, jobs_ref, count_ref, sources, *refs[-2:])
+        return
+    f_high_ref, f_low_ref, before_ref, *_ = refs
+    if not last:
+        high_to, low_to, marg_ref, out_ref, product_ref, sems = refs[-6:]
+    else:
+        high_to, low_to, marg_out, out_ref, product_ref, sems, marg_ref = refs[-7:]
+    if sets:
+        put_tiles(sets, nodes, sides, me_ref, jobs_ref, count_ref, sources, high_to, low_to)
+    marg_ref[...] = before_ref[...]
+    finish = multiply_rows(
+        phase, sides, widths_ref, slots_ref, high_to, low_to, f_high_ref, f_low_ref, out_ref, marg_ref, product_ref, sems.at[0]
+    )
+    if last:
+        copy = pltpu.make_async_copy(marg_ref, marg_out, sems.at[1])
+        copy.start()
+        copy.wait()
+    finish()
+
+
+def work(me, plan, widths, sides, blocks, sets=(), sources=(), phase=None, factors=(), before=None, out=(), last=False, after=()):
+    given = [("smem", x) for x in (me, *plan, widths)] + [("vmem", x) for x in sources]
+    shapes = [pltpu.VMEM((widths.shape[1], sides * TILE, sides * TILE), jnp.bfloat16)] * 2
+    specs, scratch, aliases = [VMEM] * 2, [], {}
+    if phase is not None:
+        given += [("vmem", x) for x in (*factors, before)]
+    if blocks:
+        aliases = {len(given): 0, len(given) + 1: 1}
+        given += [("vmem", x) for x in blocks]
+    if phase is not None:
+        given += [("any", x) for x in out]
+        rows, cols = factors[0].shape
+        if out:
+            aliases[len(given) - 1] = 3
+        anywhere = pl.BlockSpec(memory_space=pl.ANY)
+        marg = jax.ShapeDtypeStruct(before.shape, jnp.float32) if last else pltpu.VMEM(before.shape, jnp.float32)
+        shapes += [marg, jax.ShapeDtypeStruct((rows, cols), jnp.float32)]
+        specs += [anywhere if last else VMEM, anywhere]
+        scratch = [pltpu.VMEM((rows, cols), jnp.float32), pltpu.SemaphoreType.DMA((2,))]
+        scratch += [pltpu.VMEM(before.shape, jnp.float32)] if last else []
+    name = "_".join([f"put_{names[0]}" for names in sets[:1]] + [f"multiply_{phase}"] * (phase is not None))
+    kernel = functools.partial(work_kernel, sets, phase, last, sides)
     return call(
-        functools.partial(product_kernel, nodes, sides, phase),
-        f"products_{phase}",
-        given,
-        [jax.ShapeDtypeStruct((rows, cols), jnp.float32), jax.ShapeDtypeStruct((cols // TILE, TILE), jnp.float32)],
-        [pl.BlockSpec(memory_space=pl.ANY), VMEM],
-        vmem=14,
-        scratch_shapes=[pltpu.VMEM((rows, cols), jnp.float32), pltpu.SemaphoreType.DMA((cols // TILE, sides))],
-        input_output_aliases={len(given) - 1: 0} if out else {},
+        kernel, name, given, shapes, specs, after, vmem=14 if scratch else 6, scratch_shapes=scratch, input_output_aliases=aliases
     )
 
 
@@ -456,26 +474,22 @@
     near, side, mid = swap(near, 4), swap(side, 2), move(mid, between_inner)
     plan = plan_jobs(me, patterns, (rows_other,))
     factors = factor_halves(factor, plan[1:2])
-    blocks = assemble((("rows",),), me, plan, patterns, (sep_inv, rows_other), (), factors[:1])
+    do = functools.partial(work, me, plan, widths, patterns.shape[1])
+    blocks = do((), (("rows",),), (sep_inv, rows_other), after=factors[:1])
     rows = (piece_rows("side_near"), piece_rows(*ROUNDS[0]), piece_rows("far", "far_rest"), piece_rows("far"))
     part, held, far, far_first, mid = turn("turn_1", turn_1, me, (near, side), rows, (mid,), blocks[:1])
 
-    def put(sets, sources, blocks, after=()):
-        return assemble(sets, me, plan, patterns, sources, blocks, after)
-
     side_near, mid_outer = swap(part, 2), move(mid, outward)
     far, far_outer = move(far, between_inner), move(far_first, across)
-    blocks = put(ROUNDS[:1], (held, swap(held, 1)), blocks)
-    out, marg = products(0, widths, plan[2], blocks, factors, dinv)
+    *blocks, marg, out = do(blocks, ROUNDS[:1], (held, swap(held, 1)), 0, factors, dinv)
     rows = (piece_rows("side_mid", "side_far"), piece_rows(*ROUNDS[1]), piece_rows("far_rest"))
     part, held, rest = turn("turn_2", turn_2, me, (mid, mid_outer, far, far_outer, side_near), rows, (), (marg,))
 
     side_last, rest_outer = swap(part, 2), move(rest, outward)
-    blocks = put(ROUNDS[1:2], (held, swap(held, 1)), blocks, (marg,))
-    out, marg = products(1, widths, plan[2], blocks, factors, marg, (out,))
+    *blocks, marg, out = do(blocks, ROUNDS[1:2], (held, swap(held, 1)), 1, factors, marg, (out,))
     (held,) = turn("turn_3", turn_3, me, (side_last, rest, rest_outer), (piece_rows(*ROUNDS[2]),), (), (marg,))
-    blocks = put(ROUNDS[2:], (held, swap(held, 1)), blocks, (marg,))
-    return products(2, widths, plan[2], blocks, factors, marg, (out,))
+    *_, marg, out = do(blocks, ROUNDS[2:], (held, swap(held, 1)), 2, factors, marg, (out,), last=True)
+    return out, marg
 
 
 def shards(sep_inv, factor, widths, patterns, dinv):
@@ -488,8 +502,9 @@
         nodes, sides = patterns.shape
         blocks = assemble_full(patterns, lax.all_gather(sep_inv, "pr", axis=0, tiled=True))
         order = jnp.tile(jnp.arange(sides, dtype=jnp.int32), nodes)
-        slots = jnp.stack([order, order, jnp.full_like(order, sides)])
-        out, marg = products(0, widths, slots, blocks, factor_halves(factor), dinv)
+        nothing = jnp.zeros((1,), jnp.int32)
+        plan = (nothing, nothing, jnp.stack([order, order, jnp.full_like(order, sides)]))
+        *_, marg, out = work(nothing, plan, widths, sides, blocks, phase=0, factors=factor_halves(factor), before=dinv, last=True)
     return out, marg.reshape(cols)
 
 

time: 72.4 us -> 68.7 us (0.949)
  Pallas kernels: 38.5 us -> 31.9 us
  waiting for transfers between devices: 13.8 us -> 17.1 us
    pallas_call x13 -> x10, Pallas kernels: 38.5 us -> 31.9 us  [call(): pl.pallas_call(body, out_shape=out_shape, in_specs=[pl.BlockSpec(memory_s...]
    ppermute x5, waiting for transfers between devices: 4.69 us -> 7.71 us  [move(): return lax.ppermute(value, 'pr', pairs)]
  transfers between devices with their start and end apart: 13 -> 13, of which waited for: 5 -> 6; matrix products, arithmetic and copies ran while one was open for 1% -> 1% of each run, Pallas kernels for 39% -> 35%
where the time goes in v5:
time: 68.7 us; the launch traced here: 68.4 us
  Pallas kernels  31.9 us (46%)
  waiting for transfers between devices  17.1 us (25%)
  starting transfers between devices  12.4 us (18%)
  local copies, waits for them, and re-layouts  6.03 us (9%)
  between operations  1.02 us (1%)
    pallas_call x10, Pallas kernels, call(): pl.pallas_call(body, out_shape=out_shape, in_specs=[pl.BlockSpec(memory_s...  31.9 us
    ppermute x8, waiting for transfers between devices, swap(): return lax.ppermute(value, 'pr', [(i, i ^ mask) for i in range(DEVICES)])  9.37 us
    ppermute x5, waiting for transfers between devices, move(): return lax.ppermute(value, 'pr', pairs)  7.71 us
    ppermute x8, starting transfers between devices, swap(): return lax.ppermute(value, 'pr', [(i, i ^ mask) for i in range(DEVICES)])  7.16 us
    unnamed x13, local copies, waits for them, and re-layouts  6.03 us
    ppermute x5, starting transfers between devices, move(): return lax.ppermute(value, 'pr', pairs)  5.22 us
  transfers between devices with their start and end apart: 13, of which 6 were waited for; matrix products, arithmetic and copies ran while one was open for 1% of the time, Pallas kernels for 35%

profile of v5, /device:TPU:0, one launch (start us, length us, event | category | flops | bytes accessed | tf_op | source)
XLA Modules:
  0.0 68.4 jit_solution(17832025669456758604)
XLA Ops:
  1.1 1.2 %copy-done.1 = f32[128,2048]{1,0:T(8,128)S(1)} copy-done((f32[128,2048]{1,0:T(8,128)S(1)}, f32[128,2048]{1,0:T(8,128)}, u32[]{:S(2)}) %copy-start.1) | copy-done | bytes 1048600
  2.4 1.6 %pack.1 = (f32[1728,128]{1,0:T(8,128)}, f32[1472,128]{1,0:T(8,128)}, f32[960,128]{1,0:T(8,128)}) custom-call(s32[1]{0:T(128)} %bitcast.refs_0_, f32[128,2048]{1,0:T(8,128)S(1)} %copy-done.1), custom_call_target="tpu_custom_call" | custom-call | tf_op jit(solution)/shard_map/pack/pallas_call | solution.py:71
  3.9 2.6 %collective-permute-start.1 = (f32[1728,128]{1,0:T(8,128)}, f32[1728,128]{1,0:T(8,128)S(1)}, u32[]{:S(2)}, u32[]{:S(2)}) collective-permute-start(f32[1728,128]{1,0:T(8,128)} %get-tuple-element.33), channel_id=1, source_target_pairs={{0,4},{1,5},{2,6},{3,7},{4,0},{5,1},{6,2},{7,3},{8,12},{9,13},{10,... | collective-permute-start | bytes 2654216 | tf_op jit(solution)/shard_map/ppermute | solution.py:398
  6.5 1.5 %collective-permute-start.2 = (f32[1472,128]{1,0:T(8,128)}, f32[1472,128]{1,0:T(8,128)S(1)}, u32[]{:S(2)}, u32[]{:S(2)}) collective-permute-start(f32[1472,128]{1,0:T(8,128)} %get-tuple-element.34), channel_id=1, source_target_pairs={{0,2},{1,3},{2,0},{3,1},{4,6},{5,7},{6,4},{7,5},{8,10},{9,11},{10,... | collective-permute-start | bytes 2261000 | tf_op jit(solution)/shard_map/ppermute | solution.py:398
  8.0 0.7 collective-permute-start.3
  8.7 0.8 %copy.17.refs_2_ = s32[8,4]{1,0:T(8,128)S(1)} copy(s32[8,4]{0,1:T(4,128)} %param.9) | data formatting | bytes 256 | tf_op args[3]
  10.2 3.7 %plan_jobs.1 = (s32[54,32]{1,0:T(8,128)S(1)}, s32[54]{0:T(128)S(1)}, s32[5,32]{1,0:T(8,128)S(1)}) custom-call(s32[1]{0:T(128)} %bitcast.refs_0_, s32[64]{0:T(128)S(1)} %copy-done.5, s32[8,4]{1,0:T(8,128)S(1)} %copy.17.refs_2_, f32[128,2048]{1,0:T(8,128)S(1)} %collective-permute-done.refs_3_.refs_6_), custom_call_target="tpu_custom_call" | custom-call | tf_op jit(solution)/shard_map/plan_jobs/pallas_call | solution.py:71
  13.9 3.4 %copy-done = f32[512,4096]{1,0:T(8,128)S(1)} copy-done((f32[512,4096]{1,0:T(8,128)S(1)}, f32[512,4096]{1,0:T(8,128)}, u32[]{:S(2)}) %copy-start) | copy-done | bytes 8388632
  17.2 1.3 %factor_halves.1 = (bf16[512,4096]{1,0:T(8,128)(2,1)S(1)}, bf16[512,4096]{1,0:T(8,128)(2,1)S(1)}) custom-call(f32[512,4096]{1,0:T(8,128)S(1)} %copy-done, s32[54]{0:T(128)S(1)} %get-tuple-element.31.refs_1_.refs_2_), custom_call_target="tpu_custom_call" | custom-call | tf_op jit(solution)/shard_map/factor_halves/pallas_call | solution.py:71
  18.6 2.1 %put_rows.1 = (bf16[8,512,512]{2,1,0:T(8,128)(2,1)S(1)}, bf16[8,512,512]{2,1,0:T(8,128)(2,1)S(1)}) custom-call(s32[1]{0:T(128)} %bitcast.refs_0_, s32[54,32]{1,0:T(8,128)S(1)} %get-tuple-element.30.refs_1_, s32[54]{0:T(128)S(1)} %get-tuple-element.31.refs_1_.refs_2_, s32[5,32]{1,0:T(8,128)S(1)} %get-tuple-element.32.refs_3_, s32[1,8]{1,0:T(1,128)S(1)} %copy-done.4, ...), custom_call_target="tpu_custom_call" | custom-call | tf_op jit(solution)/shard_map/put_rows/pallas_call | solution.py:71
  20.7 5.0 %collective-permute-done.2.refs_2_ = f32[1472,128]{1,0:T(8,128)S(1)} collective-permute-done((f32[1472,128]{1,0:T(8,128)}, f32[1472,128]{1,0:T(8,128)S(1)}, u32[]{:S(2)}, u32[]{:S(2)}) %collective-permute-start.2) | collective-permute-done | bytes 753696 | tf_op jit(solution)/shard_map/ppermute | solution.py:398
  25.7 1.3 %collective-permute-done.1.refs_1_ = f32[1728,128]{1,0:T(8,128)S(1)} collective-permute-done((f32[1728,128]{1,0:T(8,128)}, f32[1728,128]{1,0:T(8,128)S(1)}, u32[]{:S(2)}, u32[]{:S(2)}) %collective-permute-start.1) | collective-permute-done | bytes 884768 | tf_op jit(solution)/shard_map/ppermute | solution.py:398
  27.3 1.8 %collective-permute-start.7 = (f32[1216,128]{1,0:T(8,128)S(1)}, f32[1216,128]{1,0:T(8,128)S(1)}, u32[]{:S(2)}, u32[]{:S(2)}) collective-permute-start(f32[1216,128]{1,0:T(8,128)S(1)} %get-tuple-element.41), channel_id=1, source_target_pairs={{0,2},{1,3},{2,0},{3,1},{4,6},{5,7},{6,4},{7,5},{8,10},{9,11},{10,... | collective-permute-start | bytes 1867784 | tf_op jit(solution)/shard_map/ppermute | solution.py:398
  29.0 1.3 %collective-permute-start.4 = (f32[960,128]{1,0:T(8,128)S(1)}, f32[960,128]{1,0:T(8,128)S(1)}, u32[]{:S(2)}, u32[]{:S(2)}) collective-permute-start(f32[960,128]{1,0:T(8,128)S(1)} %get-tuple-element.38.refs_1_), channel_id=1, source_target_pairs={{4,0},{5,1},{6,2},{7,3},{8,12},{9,13},{10,14},{11,15},{20,16},{21,... | collective-permute-start | bytes 1474568 | tf_op jit(solution)/shard_map/ppermute | solution.py:403
  30.3 0.7 %collective-permute-start.5 = (f32[704,128]{1,0:T(8,128)S(1)}, f32[704,128]{1,0:T(8,128)S(1)}, u32[]{:S(2)}, u32[]{:S(2)}) collective-permute-start(f32[704,128]{1,0:T(8,128)S(1)} %get-tuple-element.39), channel_id=1, source_target_pairs={{4,8},{5,9},{6,10},{7,11},{8,4},{9,5},{10,6},{11,7},{20,24},{21,25... | collective-permute-start | bytes 1081352 | tf_op jit(solution)/shard_map/ppermute | solution.py:403
  31.0 1.3 %collective-permute-start.6 = (f32[192,128]{1,0:T(8,128)S(1)}, f32[192,128]{1,0:T(8,128)S(1)}, u32[]{:S(2)}, u32[]{:S(2)}) collective-permute-start(f32[192,128]{1,0:T(8,128)S(1)} %get-tuple-element.40), channel_id=1, source_target_pairs={{4,12},{5,13},{6,14},{7,15},{8,0},{9,1},{10,2},{11,3},{20,28},{21,... | collective-permute-start | bytes 294920 | tf_op jit(solution)/shard_map/ppermute | solution.py:403
  32.3 8.4 %put_near_multiply_0.1 = (bf16[8,512,512]{2,1,0:T(8,128)(2,1)S(1)}, bf16[8,512,512]{2,1,0:T(8,128)(2,1)S(1)}, f32[32,128]{1,0:T(8,128)S(1)}, f32[512,4096]{1,0:T(8,128)}) custom-call(s32[1]{0:T(128)} %bitcast.refs_0_, s32[54,32]{1,0:T(8,128)S(1)} %get-tuple-element.30.refs_1_, ...), custom_call_target="tpu_custom_call", output_to_operand_aliasing={{0}: (10, {}), {1}: (11, {})} | custom-call | tf_op jit(solution)/shard_map/put_near_multiply_0/pallas_call | solution.py:71
  40.7 6.9 %collective-permute-done.6.refs_4_ = f32[192,128]{1,0:T(8,128)S(1)} collective-permute-done((f32[192,128]{1,0:T(8,128)S(1)}, f32[192,128]{1,0:T(8,128)S(1)}, u32[]{:S(2)}, u32[]{:S(2)}) %collective-permute-start.6) | collective-permute-done | bytes 98336 | tf_op jit(solution)/shard_map/ppermute | solution.py:403
  48.4 1.3 %collective-permute-start.10 = (f32[512,128]{1,0:T(8,128)S(1)}, f32[512,128]{1,0:T(8,128)S(1)}, u32[]{:S(2)}, u32[]{:S(2)}) collective-permute-start(f32[512,128]{1,0:T(8,128)S(1)} %get-tuple-element.47.refs_2_), channel_id=1, source_target_pairs={{4,0},{5,1},{6,2},{7,3},{8,12},{9,13},{10,14},{11,15},{20,16},{21,... | collective-permute-start | bytes 786440 | tf_op jit(solution)/shard_map/ppermute | solution.py:403
  49.7 1.0 %collective-permute-done.11.refs_6_ = f32[2368,128]{1,0:T(8,128)S(1)} collective-permute-done((f32[2368,128]{1,0:T(8,128)S(1)}, f32[2368,128]{1,0:T(8,128)S(1)}, u32[]{:S(2)}, u32[]{:S(2)}) %collective-permute-start.11) | collective-permute-done | bytes 1212448 | tf_op jit(solution)/shard_map/ppermute | solution.py:398
  50.7 7.1 %put_mid_multiply_1.1 = (bf16[8,512,512]{2,1,0:T(8,128)(2,1)S(1)}, bf16[8,512,512]{2,1,0:T(8,128)(2,1)S(1)}, f32[32,128]{1,0:T(8,128)S(1)}, f32[512,4096]{1,0:T(8,128)}) custom-call(s32[1]{0:T(128)} %bitcast.refs_0_, s32[54,32]{1,0:T(8,128)S(1)} %get-tuple-element.30.refs_1_, ...), custom_call_target="tpu_custom_call", output_to_operand_aliasing={{0}: (10, {}), {1}: (11, {}), {3}: (12, {})} | custom-call | tf_op jit(solution)/shard_map/put_mid_multiply_1/pallas_call | solution.py:71
  57.9 0.8 %collective-permute-done.10.refs_3_ = f32[512,128]{1,0:T(8,128)S(1)} collective-permute-done((f32[512,128]{1,0:T(8,128)S(1)}, f32[512,128]{1,0:T(8,128)S(1)}, u32[]{:S(2)}, u32[]{:S(2)}) %collective-permute-start.10) | collective-permute-done | bytes 262176 | tf_op jit(solution)/shard_map/ppermute | solution.py:403
  58.8 2.0 %collective-permute-done.12.refs_6_ = f32[1152,128]{1,0:T(8,128)S(1)} collective-permute-done((f32[1152,128]{1,0:T(8,128)S(1)}, f32[1152,128]{1,0:T(8,128)S(1)}, u32[]{:S(2)}, u32[]{:S(2)}) %collective-permute-start.12) | collective-permute-done | bytes 589856 | tf_op jit(solution)/shard_map/ppermute | solution.py:398
  60.8 7.4 %put_side_mid_multiply_2.1 = (bf16[8,512,512]{2,1,0:T(8,128)(2,1)S(1)}, bf16[8,512,512]{2,1,0:T(8,128)(2,1)S(1)}, f32[32,128]{1,0:T(8,128)}, f32[512,4096]{1,0:T(8,128)}) custom-call(s32[1]{0:T(128)} %bitcast.refs_0_, s32[54,32]{1,0:T(8,128)S(1)} %get-tuple-element.30.refs_1_, ...), custom_call_target="tpu_custom_call", output_to_operand_aliasing={{0}: (10, {}), {1}: (11, {}), {3}: (12, {})} | custom-call | tf_op jit(solution)/shard_map/put_side_mid_multiply_2/pallas_call | solution.py:71
  (25 shorter events, 2.3 us)
Async XLA Ops:
  0.6 8.9 %collective-permute-start = (f32[128,2048]{1,0:T(8,128)}, f32[128,2048]{1,0:T(8,128)S(1)}, u32[]{:S(2)}, u32[]{:S(2)}) collective-permute-start(f32[128,2048]{1,0:T(8,128)} %refs_5_.1), channel_id=1, source_target_pairs={{0,1},{1,0},{2,3},{3,2},{4,5},{5,4},{6,7},{7,6},{8,9},{9,8},{10,11... | collective-permute-start | bytes 3145736 | tf_op jit(solution)/shard_map/ppermute | solution.py:398
  1.1 1.2 %copy-start.1 = (f32[128,2048]{1,0:T(8,128)S(1)}, f32[128,2048]{1,0:T(8,128)}, u32[]{:S(2)}) copy-start(f32[128,2048]{1,0:T(8,128)} %refs_5_.1) | copy-start | bytes 3145732
  3.9 23.1 %collective-permute-start.1 = (f32[1728,128]{1,0:T(8,128)}, f32[1728,128]{1,0:T(8,128)S(1)}, u32[]{:S(2)}, u32[]{:S(2)}) collective-permute-start(f32[1728,128]{1,0:T(8,128)} %get-tuple-element.33), channel_id=1, source_target_pairs={{0,4},{1,5},{2,6},{3,7},{4,0},{5,1},{6,2},{7,3},{8,12},{9,13},{10,... | collective-permute-start | bytes 2654216 | tf_op jit(solution)/shard_map/ppermute | solution.py:398
  6.5 19.2 %collective-permute-start.2 = (f32[1472,128]{1,0:T(8,128)}, f32[1472,128]{1,0:T(8,128)S(1)}, u32[]{:S(2)}, u32[]{:S(2)}) collective-permute-start(f32[1472,128]{1,0:T(8,128)} %get-tuple-element.34), channel_id=1, source_target_pairs={{0,2},{1,3},{2,0},{3,1},{4,6},{5,7},{6,4},{7,5},{8,10},{9,11},{10,... | collective-permute-start | bytes 2261000 | tf_op jit(solution)/shard_map/ppermute | solution.py:398
  8.0 12.6 %collective-permute-start.3 = (f32[960,128]{1,0:T(8,128)}, f32[960,128]{1,0:T(8,128)S(1)}, u32[]{:S(2)}, u32[]{:S(2)}) collective-permute-start(f32[960,128]{1,0:T(8,128)} %get-tuple-element.35), channel_id=1, source_target_pairs={{4,8},{5,9},{6,10},{7,11},{8,4},{9,5},{10,6},{11,7},{20,24},{21,25... | collective-permute-start | bytes 1474568 | tf_op jit(solution)/shard_map/ppermute | solution.py:403
  9.5 0.7 copy-start.5
  13.8 3.4 %copy-start = (f32[512,4096]{1,0:T(8,128)S(1)}, f32[512,4096]{1,0:T(8,128)}, u32[]{:S(2)}) copy-start(f32[512,4096]{1,0:T(8,128)} %refs_0_.1) | copy-start | bytes 25165828
  17.2 1.3 %copy-start.2 = (f32[128,2048]{1,0:T(8,128)S(1)}, f32[128,2048]{1,0:T(8,128)}, u32[]{:S(2)}) copy-start(f32[128,2048]{1,0:T(8,128)} %refs_5_.1) | copy-start | bytes 3145732
  17.2 1.3 %copy-start.4 = (s32[1,8]{1,0:T(1,128)S(1)}, s32[1,8]{1,0:T(1,128)}, u32[]{:S(2)}) copy-start(s32[1,8]{1,0:T(1,128)} %refs_4_.7) | copy-start | bytes 100
  20.7 11.7 %copy-start.3 = (f32[4096]{0:T(1024)S(1)}, f32[4096]{0:T(1024)}, u32[]{:S(2)}) copy-start(f32[4096]{0:T(1024)} %param.10) | copy-start | bytes 49156
  27.2 5.1 %collective-permute-start.8 = (f32[3200,128]{1,0:T(8,128)S(1)}, f32[3200,128]{1,0:T(8,128)S(1)}, u32[]{:S(2)}, u32[]{:S(2)}) collective-permute-start(f32[3200,128]{1,0:T(8,128)S(1)} %get-tuple-element.42.refs_5_), channel_id=1, source_target_pairs={{0,1},{1,0},{2,3},{3,2},{4,5},{5,4},{6,7},{7,6},{8,9},{9,8},{10,11... | collective-permute-start | bytes 4915208 | tf_op jit(solution)/shard_map/ppermute | solution.py:398
  27.3 20.3 %collective-permute-start.7 = (f32[1216,128]{1,0:T(8,128)S(1)}, f32[1216,128]{1,0:T(8,128)S(1)}, u32[]{:S(2)}, u32[]{:S(2)}) collective-permute-start(f32[1216,128]{1,0:T(8,128)S(1)} %get-tuple-element.41), channel_id=1, source_target_pairs={{0,2},{1,3},{2,0},{3,1},{4,6},{5,7},{6,4},{7,5},{8,10},{9,11},{10,... | collective-permute-start | bytes 1867784 | tf_op jit(solution)/shard_map/ppermute | solution.py:398
  29.0 18.6 %collective-permute-start.4 = (f32[960,128]{1,0:T(8,128)S(1)}, f32[960,128]{1,0:T(8,128)S(1)}, u32[]{:S(2)}, u32[]{:S(2)}) collective-permute-start(f32[960,128]{1,0:T(8,128)S(1)} %get-tuple-element.38.refs_1_), channel_id=1, source_target_pairs={{4,0},{5,1},{6,2},{7,3},{8,12},{9,13},{10,14},{11,15},{20,16},{21,... | collective-permute-start | bytes 1474568 | tf_op jit(solution)/shard_map/ppermute | solution.py:403
  30.3 17.3 %collective-permute-start.5 = (f32[704,128]{1,0:T(8,128)S(1)}, f32[704,128]{1,0:T(8,128)S(1)}, u32[]{:S(2)}, u32[]{:S(2)}) collective-permute-start(f32[704,128]{1,0:T(8,128)S(1)} %get-tuple-element.39), channel_id=1, source_target_pairs={{4,8},{5,9},{6,10},{7,11},{8,4},{9,5},{10,6},{11,7},{20,24},{21,25... | collective-permute-start | bytes 1081352 | tf_op jit(solution)/shard_map/ppermute | solution.py:403
  31.0 16.6 %collective-permute-start.6 = (f32[192,128]{1,0:T(8,128)S(1)}, f32[192,128]{1,0:T(8,128)S(1)}, u32[]{:S(2)}, u32[]{:S(2)}) collective-permute-start(f32[192,128]{1,0:T(8,128)S(1)} %get-tuple-element.40), channel_id=1, source_target_pairs={{4,12},{5,13},{6,14},{7,15},{8,0},{9,1},{10,2},{11,3},{20,28},{21,... | collective-permute-start | bytes 294920 | tf_op jit(solution)/shard_map/ppermute | solution.py:403
  47.8 3.0 %collective-permute-start.11 = (f32[2368,128]{1,0:T(8,128)S(1)}, f32[2368,128]{1,0:T(8,128)S(1)}, u32[]{:S(2)}, u32[]{:S(2)}) collective-permute-start(f32[2368,128]{1,0:T(8,128)S(1)} %get-tuple-element.48.refs_5_), channel_id=1, source_target_pairs={{0,1},{1,0},{2,3},{3,2},{4,5},{5,4},{6,7},{7,6},{8,9},{9,8},{10,11... | collective-permute-start | bytes 3637256 | tf_op jit(solution)/shard_map/ppermute | solution.py:398
  47.8 10.8 %collective-permute-start.9 = (f32[640,128]{1,0:T(8,128)S(1)}, f32[640,128]{1,0:T(8,128)S(1)}, u32[]{:S(2)}, u32[]{:S(2)}) collective-permute-start(f32[640,128]{1,0:T(8,128)S(1)} %get-tuple-element.46), channel_id=1, source_target_pairs={{0,2},{1,3},{2,0},{3,1},{4,6},{5,7},{6,4},{7,5},{8,10},{9,11},{10,... | collective-permute-start | bytes 983048 | tf_op jit(solution)/shard_map/ppermute | solution.py:398
  48.4 10.3 %collective-permute-start.10 = (f32[512,128]{1,0:T(8,128)S(1)}, f32[512,128]{1,0:T(8,128)S(1)}, u32[]{:S(2)}, u32[]{:S(2)}) collective-permute-start(f32[512,128]{1,0:T(8,128)S(1)} %get-tuple-element.47.refs_2_), channel_id=1, source_target_pairs={{4,0},{5,1},{6,2},{7,3},{8,12},{9,13},{10,14},{11,15},{20,16},{21,... | collective-permute-start | bytes 786440 | tf_op jit(solution)/shard_map/ppermute | solution.py:403
  58.7 2.1 %collective-permute-start.12 = (f32[1152,128]{1,0:T(8,128)S(1)}, f32[1152,128]{1,0:T(8,128)S(1)}, u32[]{:S(2)}, u32[]{:S(2)}) collective-permute-start(f32[1152,128]{1,0:T(8,128)S(1)} %turn_3.1.refs_5_), channel_id=1, source_target_pairs={{0,1},{1,0},{2,3},{3,2},{4,5},{5,4},{6,7},{7,6},{8,9},{9,8},{10,11... | collective-permute-start | bytes 1769480 | tf_op jit(solution)/shard_map/ppermute | solution.py:398

commit v6 on v5

--- a/solution.py
+++ b/solution.py
@@ -91,36 +91,58 @@
     return high, low
 
 
-def pack_kernel(sets, me_ref, rows_ref, *packed_refs):
+def pack_kernel(sets, me_ref, rows_ref, *refs):
+    packed_refs, pair_ref, half_ref, pair_sem, half_sem, sems = refs[: len(sets)], *refs[len(sets) :]
     me = me_ref[0]
 
     def tile(q):
-        return rows_ref[:, pl.ds(pl.multiple_of(q * TILE, TILE), TILE)]
-
-    diagonal, pair = tile(me), tile(me ^ 1)
-    half = jnp.where(me % 2 == 0, pair[:HALF, :], pair.T[HALF:, :])
+        return rows_ref.at[:, pl.ds(pl.multiple_of(q * TILE, TILE), TILE)]
+
+    pair = pltpu.make_async_copy(tile(me ^ 1), pair_ref, pair_sem)
+    pair.start()
+    copies, halves = [], []
     for names, packed_ref in zip(sets, packed_refs, strict=True):
         row = 0
         for name in names:
             owner, own, classes = PIECES[name]
             receiver = device_of(owner, me, 0) if owner < 4 else me ^ 12
+            columns = [device_of(column, receiver, core) for column in classes for core in range(2)]
             if own:
-                packed_ref[row : row + TILE, :] = diagonal
-                packed_ref[row + TILE : row + TILE + HALF, :] = half
+                copies.append((tile(me), packed_ref.at[pl.ds(row, TILE), :]))
+                halves.append((half_ref, packed_ref.at[pl.ds(row + TILE, HALF), :]))
                 row += TILE + HALF
-            for column in classes:
-                for core in range(2):
-                    packed_ref[row : row + TILE, :] = tile(device_of(column, receiver, core))
-                    row += TILE
+            for q in columns:
+                copies.append((tile(q), packed_ref.at[pl.ds(row, TILE), :]))
+                row += TILE
+    copies = [pltpu.make_async_copy(*ends, sems.at[i]) for i, ends in enumerate(copies)]
+    halves = [pltpu.make_async_copy(*ends, half_sem.at[i]) for i, ends in enumerate(halves)]
+    for copy in copies:
+        copy.start()
+    pair.wait()
+    half_ref[...] = jnp.where(me % 2 == 0, pair_ref[:HALF, :], pair_ref[...].T[HALF:, :])
+    for copy in halves:
+        copy.start()
+    for copy in (*copies, *halves):
+        copy.wait()
 
 
 def pack(sets, me, sep_rows):
+    names = [name for names in sets for name in names]
+    tiles = sum(PIECES[name][1] + 2 * len(PIECES[name][2]) for name in names)
+    anywhere = pl.BlockSpec(memory_space=pl.ANY)
     return call(
         functools.partial(pack_kernel, sets),
         "pack",
-        [("smem", me), ("vmem", sep_rows)],
-        [pltpu.VMEM((piece_rows(*names), TILE), jnp.float32) for names in sets],
-        [VMEM] * len(sets),
+        [("smem", me), ("any", sep_rows)],
+        [jax.ShapeDtypeStruct((piece_rows(*names), TILE), jnp.float32) for names in sets],
+        [anywhere] * len(sets),
+        scratch_shapes=[
+            pltpu.VMEM((TILE, TILE), jnp.float32),
+            pltpu.VMEM((HALF, TILE), jnp.float32),
+            pltpu.SemaphoreType.DMA(()),
+            pltpu.SemaphoreType.DMA((len(names),)),
+            pltpu.SemaphoreType.DMA((tiles,)),
+        ],
     )
 
 
@@ -432,13 +454,12 @@
     return row + count
 
 
-def turn_1(inner, near_ref, side_ref, part_ref, held_ref, far_ref, far_first_ref):
+def turn_1(inner, near_ref, side_ref, part_ref, held_ref, far_ref):
     copy_rows(part_ref, 0, near_ref, 0, part_ref.shape[0])
     copy_rows(held_ref, copy_rows(held_ref, 0, near_ref), side_ref)
     first, rest = piece_rows("far"), piece_rows("far_rest")
     copy_rows(far_ref, 0, near_ref, 0, first)
     copy_rows(far_ref, first, near_ref, near_ref.shape[0] - rest, rest)
-    copy_rows(far_first_ref, 0, near_ref, 0, first)
 
 
 def turn_2(inner, mid_ref, mid_outer_ref, far_ref, far_outer_ref, side_near_ref, part_ref, held_ref, rest_ref):
@@ -467,20 +488,20 @@
 
 def planned(sep_inv, factor, widths, patterns, dinv):
     me = lax.axis_index("pr").astype(jnp.int32).reshape(1)
-    between_inner, outward, across = {1: 2, 2: 1}, {1: 0, 2: 3}, {1: 3, 2: 0}
-
-    near, side, mid = pack((("near",), ("side",), ("mid",)), me, sep_inv)
+    between_inner, between_outer, outward = {1: 2, 2: 1}, {0: 3, 3: 0}, {1: 0, 2: 3}
+
+    near, side, mid, first = pack((("near",), ("side",), ("mid",), ("far",)), me, sep_inv)
     rows_other = swap(sep_inv, 1)
     near, side, mid = swap(near, 4), swap(side, 2), move(mid, between_inner)
     plan = plan_jobs(me, patterns, (rows_other,))
     factors = factor_halves(factor, plan[1:2])
     do = functools.partial(work, me, plan, widths, patterns.shape[1])
     blocks = do((), (("rows",),), (sep_inv, rows_other), after=factors[:1])
-    rows = (piece_rows("side_near"), piece_rows(*ROUNDS[0]), piece_rows("far", "far_rest"), piece_rows("far"))
-    part, held, far, far_first, mid = turn("turn_1", turn_1, me, (near, side), rows, (mid,), blocks[:1])
+    rows = (piece_rows("side_near"), piece_rows(*ROUNDS[0]), piece_rows("far", "far_rest"))
+    part, held, far, mid = turn("turn_1", turn_1, me, (near, side), rows, (mid,), blocks[:1])
 
     side_near, mid_outer = swap(part, 2), move(mid, outward)
-    far, far_outer = move(far, between_inner), move(far_first, across)
+    far, far_outer = move(far, between_inner), move(first, between_outer)
     *blocks, marg, out = do(blocks, ROUNDS[:1], (held, swap(held, 1)), 0, factors, dinv)
     rows = (piece_rows("side_mid", "side_far"), piece_rows(*ROUNDS[1]), piece_rows("far_rest"))
     part, held, rest = turn("turn_2", turn_2, me, (mid, mid_outer, far, far_outer, side_near), rows, (), (marg,))

time: 68.7 us -> 67.3 us (0.980)
  waiting for transfers between devices: 17.1 us -> 11.1 us
  starting transfers between devices: 12.4 us -> 16.5 us
    ppermute x5, waiting for transfers between devices: 7.71 us -> 1.53 us  [move(): return lax.ppermute(value, 'pr', pairs)]
    ppermute x5, starting transfers between devices: 5.22 us -> 9.43 us  [move(): return lax.ppermute(value, 'pr', pairs)]
  transfers between devices with their start and end apart: 13 -> 13, of which waited for: 6 -> 6; matrix products, arithmetic and copies ran while one was open for 1% -> 1% of each run, Pallas kernels for 35% -> 37%
where the time goes in v6:
time: 67.3 us; the launch traced here: 66.8 us
  Pallas kernels  32.1 us (48%)
  starting transfers between devices  16.5 us (25%)
  waiting for transfers between devices  11.1 us (16%)
  local copies, waits for them, and re-layouts  6.03 us (9%)
  between operations  1.04 us (2%)
    pallas_call x10, Pallas kernels, call(): pl.pallas_call(body, out_shape=out_shape, in_specs=[pl.BlockSpec(memory_s...  32.1 us
    ppermute x8, waiting for transfers between devices, swap(): return lax.ppermute(value, 'pr', [(i, i ^ mask) for i in range(DEVICES)])  9.54 us
    ppermute x5, starting transfers between devices, move(): return lax.ppermute(value, 'pr', pairs)  9.43 us
    ppermute x8, starting transfers between devices, swap(): return lax.ppermute(value, 'pr', [(i, i ^ mask) for i in range(DEVICES)])  7.06 us
    unnamed x13, local copies, waits for them, and re-layouts  6.03 us
    ppermute x5, waiting for transfers between devices, move(): return lax.ppermute(value, 'pr', pairs)  1.53 us
  transfers between devices with their start and end apart: 13, of which 6 were waited for; matrix products, arithmetic and copies ran while one was open for 1% of the time, Pallas kernels for 37%

profile of v6, /device:TPU:0, one launch (start us, length us, event | category | flops | bytes accessed | tf_op | source)
XLA Modules:
  0.0 66.8 jit_solution(18170704218174614480)
XLA Ops:
  1.1 1.2 %copy-done.1 = f32[128,2048]{1,0:T(8,128)S(1)} copy-done((f32[128,2048]{1,0:T(8,128)S(1)}, f32[128,2048]{1,0:T(8,128)}, u32[]{:S(2)}) %copy-start.1) | copy-done | bytes 1048600
  2.4 1.6 %pack.1 = (f32[1728,128]{1,0:T(8,128)}, f32[1472,128]{1,0:T(8,128)}, f32[960,128]{1,0:T(8,128)}, f32[192,128]{1,0:T(8,128)S(1)}) custom-call(s32[1]{0:T(128)} %bitcast.refs_0_, f32[128,2048]{1,0:T(8,128)S(1)} %copy-done.1), custom_call_target="tpu_custom_call" | custom-call | tf_op jit(solution)/shard_map/pack/pallas_call | solution.py:71
  4.0 2.7 %collective-permute-start.1 = (f32[1728,128]{1,0:T(8,128)}, f32[1728,128]{1,0:T(8,128)S(1)}, u32[]{:S(2)}, u32[]{:S(2)}) collective-permute-start(f32[1728,128]{1,0:T(8,128)} %get-tuple-element.33), channel_id=1, source_target_pairs={{0,4},{1,5},{2,6},{3,7},{4,0},{5,1},{6,2},{7,3},{8,12},{9,13},{10,... | collective-permute-start | bytes 2654216 | tf_op jit(solution)/shard_map/ppermute | solution.py:420
  6.7 1.5 %collective-permute-start.2 = (f32[1472,128]{1,0:T(8,128)}, f32[1472,128]{1,0:T(8,128)S(1)}, u32[]{:S(2)}, u32[]{:S(2)}) collective-permute-start(f32[1472,128]{1,0:T(8,128)} %get-tuple-element.34), channel_id=1, source_target_pairs={{0,2},{1,3},{2,0},{3,1},{4,6},{5,7},{6,4},{7,5},{8,10},{9,11},{10,... | collective-permute-start | bytes 2261000 | tf_op jit(solution)/shard_map/ppermute | solution.py:420
  8.2 0.7 %collective-permute-start.3 = (f32[960,128]{1,0:T(8,128)}, f32[960,128]{1,0:T(8,128)S(1)}, u32[]{:S(2)}, u32[]{:S(2)}) collective-permute-start(f32[960,128]{1,0:T(8,128)} %get-tuple-element.35), channel_id=1, source_target_pairs={{4,8},{5,9},{6,10},{7,11},{8,4},{9,5},{10,6},{11,7},{20,24},{21,25... | collective-permute-start | bytes 1474568 | tf_op jit(solution)/shard_map/ppermute | solution.py:425
  8.9 0.8 %copy.17.refs_2_ = s32[8,4]{1,0:T(8,128)S(1)} copy(s32[8,4]{0,1:T(4,128)} %param.9) | data formatting | bytes 256 | tf_op args[3]
  9.6 0.7 copy-done.5
  10.3 3.7 %plan_jobs.1 = (s32[54,32]{1,0:T(8,128)S(1)}, s32[54]{0:T(128)S(1)}, s32[5,32]{1,0:T(8,128)S(1)}) custom-call(s32[1]{0:T(128)} %bitcast.refs_0_, s32[64]{0:T(128)S(1)} %copy-done.5, s32[8,4]{1,0:T(8,128)S(1)} %copy.17.refs_2_, f32[128,2048]{1,0:T(8,128)S(1)} %collective-permute-done.refs_3_.refs_6_), custom_call_target="tpu_custom_call" | custom-call | tf_op jit(solution)/shard_map/plan_jobs/pallas_call | solution.py:71
  14.0 3.4 %copy-done = f32[512,4096]{1,0:T(8,128)S(1)} copy-done((f32[512,4096]{1,0:T(8,128)S(1)}, f32[512,4096]{1,0:T(8,128)}, u32[]{:S(2)}) %copy-start) | copy-done | bytes 8388632
  17.4 1.3 %factor_halves.1 = (bf16[512,4096]{1,0:T(8,128)(2,1)S(1)}, bf16[512,4096]{1,0:T(8,128)(2,1)S(1)}) custom-call(f32[512,4096]{1,0:T(8,128)S(1)} %copy-done, s32[54]{0:T(128)S(1)} %get-tuple-element.31.refs_1_.refs_2_), custom_call_target="tpu_custom_call" | custom-call | tf_op jit(solution)/shard_map/factor_halves/pallas_call | solution.py:71
  18.7 2.1 %put_rows.1 = (bf16[8,512,512]{2,1,0:T(8,128)(2,1)S(1)}, bf16[8,512,512]{2,1,0:T(8,128)(2,1)S(1)}) custom-call(s32[1]{0:T(128)} %bitcast.refs_0_, s32[54,32]{1,0:T(8,128)S(1)} %get-tuple-element.30.refs_1_, s32[54]{0:T(128)S(1)} %get-tuple-element.31.refs_1_.refs_2_, s32[5,32]{1,0:T(8,128)S(1)} %get-tuple-element.32.refs_3_, s32[1,8]{1,0:T(1,128)S(1)} %copy-done.4, ...), custom_call_target="tpu_custom_call" | custom-call | tf_op jit(solution)/shard_map/put_rows/pallas_call | solution.py:71
  20.8 5.0 %collective-permute-done.2.refs_2_ = f32[1472,128]{1,0:T(8,128)S(1)} collective-permute-done((f32[1472,128]{1,0:T(8,128)}, f32[1472,128]{1,0:T(8,128)S(1)}, u32[]{:S(2)}, u32[]{:S(2)}) %collective-permute-start.2) | collective-permute-done | bytes 753696 | tf_op jit(solution)/shard_map/ppermute | solution.py:420
  25.8 1.3 %collective-permute-done.1.refs_1_ = f32[1728,128]{1,0:T(8,128)S(1)} collective-permute-done((f32[1728,128]{1,0:T(8,128)}, f32[1728,128]{1,0:T(8,128)S(1)}, u32[]{:S(2)}, u32[]{:S(2)}) %collective-permute-start.1) | collective-permute-done | bytes 884768 | tf_op jit(solution)/shard_map/ppermute | solution.py:420
  27.4 1.7 %collective-permute-start.7 = (f32[1216,128]{1,0:T(8,128)S(1)}, f32[1216,128]{1,0:T(8,128)S(1)}, u32[]{:S(2)}, u32[]{:S(2)}) collective-permute-start(f32[1216,128]{1,0:T(8,128)S(1)} %get-tuple-element.41), channel_id=1, source_target_pairs={{0,2},{1,3},{2,0},{3,1},{4,6},{5,7},{6,4},{7,5},{8,10},{9,11},{10,... | collective-permute-start | bytes 1867784 | tf_op jit(solution)/shard_map/ppermute | solution.py:420
  29.2 1.3 %collective-permute-start.4 = (f32[960,128]{1,0:T(8,128)S(1)}, f32[960,128]{1,0:T(8,128)S(1)}, u32[]{:S(2)}, u32[]{:S(2)}) collective-permute-start(f32[960,128]{1,0:T(8,128)S(1)} %get-tuple-element.38.refs_1_), channel_id=1, source_target_pairs={{4,0},{5,1},{6,2},{7,3},{8,12},{9,13},{10,14},{11,15},{20,16},{21,... | collective-permute-start | bytes 1474568 | tf_op jit(solution)/shard_map/ppermute | solution.py:425
  30.5 0.7 %collective-permute-start.5 = (f32[704,128]{1,0:T(8,128)S(1)}, f32[704,128]{1,0:T(8,128)S(1)}, u32[]{:S(2)}, u32[]{:S(2)}) collective-permute-start(f32[704,128]{1,0:T(8,128)S(1)} %get-tuple-element.39), channel_id=1, source_target_pairs={{4,8},{5,9},{6,10},{7,11},{8,4},{9,5},{10,6},{11,7},{20,24},{21,25... | collective-permute-start | bytes 1081352 | tf_op jit(solution)/shard_map/ppermute | solution.py:425
  31.2 5.5 %collective-permute-start.6 = (f32[192,128]{1,0:T(8,128)S(1)}, f32[192,128]{1,0:T(8,128)S(1)}, u32[]{:S(2)}, u32[]{:S(2)}) collective-permute-start(f32[192,128]{1,0:T(8,128)S(1)} %get-tuple-element.40), channel_id=1, source_target_pairs={{0,12},{1,13},{2,14},{3,15},{12,0},{13,1},{14,2},{15,3},{16,28},{1... | collective-permute-start | bytes 294920 | tf_op jit(solution)/shard_map/ppermute | solution.py:425
  36.7 8.8 %put_near_multiply_0.1 = (bf16[8,512,512]{2,1,0:T(8,128)(2,1)S(1)}, bf16[8,512,512]{2,1,0:T(8,128)(2,1)S(1)}, f32[32,128]{1,0:T(8,128)S(1)}, f32[512,4096]{1,0:T(8,128)}) custom-call(s32[1]{0:T(128)} %bitcast.refs_0_, s32[54,32]{1,0:T(8,128)S(1)} %get-tuple-element.30.refs_1_, ...), custom_call_target="tpu_custom_call", output_to_operand_aliasing={{0}: (10, {}), {1}: (11, {})} | custom-call | tf_op jit(solution)/shard_map/put_near_multiply_0/pallas_call | solution.py:71
  45.5 0.9 %collective-permute-done.4.refs_2_ = f32[960,128]{1,0:T(8,128)S(1)} collective-permute-done((f32[960,128]{1,0:T(8,128)S(1)}, f32[960,128]{1,0:T(8,128)S(1)}, u32[]{:S(2)}, u32[]{:S(2)}) %collective-permute-start.4) | collective-permute-done | bytes 491552 | tf_op jit(solution)/shard_map/ppermute | solution.py:425
  47.1 1.3 %collective-permute-start.10 = (f32[512,128]{1,0:T(8,128)S(1)}, f32[512,128]{1,0:T(8,128)S(1)}, u32[]{:S(2)}, u32[]{:S(2)}) collective-permute-start(f32[512,128]{1,0:T(8,128)S(1)} %get-tuple-element.47.refs_2_), channel_id=1, source_target_pairs={{4,0},{5,1},{6,2},{7,3},{8,12},{9,13},{10,14},{11,15},{20,16},{21,... | collective-permute-start | bytes 786440 | tf_op jit(solution)/shard_map/ppermute | solution.py:425
  48.4 1.2 %collective-permute-done.11.refs_6_ = f32[2368,128]{1,0:T(8,128)S(1)} collective-permute-done((f32[2368,128]{1,0:T(8,128)S(1)}, f32[2368,128]{1,0:T(8,128)S(1)}, u32[]{:S(2)}, u32[]{:S(2)}) %collective-permute-start.11) | collective-permute-done | bytes 1212448 | tf_op jit(solution)/shard_map/ppermute | solution.py:420
  49.5 7.2 %put_mid_multiply_1.1 = (bf16[8,512,512]{2,1,0:T(8,128)(2,1)S(1)}, bf16[8,512,512]{2,1,0:T(8,128)(2,1)S(1)}, f32[32,128]{1,0:T(8,128)S(1)}, f32[512,4096]{1,0:T(8,128)}) custom-call(s32[1]{0:T(128)} %bitcast.refs_0_, s32[54,32]{1,0:T(8,128)S(1)} %get-tuple-element.30.refs_1_, ...), custom_call_target="tpu_custom_call", output_to_operand_aliasing={{0}: (10, {}), {1}: (11, {}), {3}: (12, {})} | custom-call | tf_op jit(solution)/shard_map/put_mid_multiply_1/pallas_call | solution.py:71
  57.5 2.0 %collective-permute-done.12.refs_6_ = f32[1152,128]{1,0:T(8,128)S(1)} collective-permute-done((f32[1152,128]{1,0:T(8,128)S(1)}, f32[1152,128]{1,0:T(8,128)S(1)}, u32[]{:S(2)}, u32[]{:S(2)}) %collective-permute-start.12) | collective-permute-done | bytes 589856 | tf_op jit(solution)/shard_map/ppermute | solution.py:420
  59.4 7.1 %put_side_mid_multiply_2.1 = (bf16[8,512,512]{2,1,0:T(8,128)(2,1)S(1)}, bf16[8,512,512]{2,1,0:T(8,128)(2,1)S(1)}, f32[32,128]{1,0:T(8,128)}, f32[512,4096]{1,0:T(8,128)}) custom-call(s32[1]{0:T(128)} %bitcast.refs_0_, s32[54,32]{1,0:T(8,128)S(1)} %get-tuple-element.30.refs_1_, ...), custom_call_target="tpu_custom_call", output_to_operand_aliasing={{0}: (10, {}), {1}: (11, {}), {3}: (12, {})} | custom-call | tf_op jit(solution)/shard_map/put_side_mid_multiply_2/pallas_call | solution.py:71
  (25 shorter events, 2.1 us)
Async XLA Ops:
  0.6 9.0 %collective-permute-start = (f32[128,2048]{1,0:T(8,128)}, f32[128,2048]{1,0:T(8,128)S(1)}, u32[]{:S(2)}, u32[]{:S(2)}) collective-permute-start(f32[128,2048]{1,0:T(8,128)} %refs_5_.1), channel_id=1, source_target_pairs={{0,1},{1,0},{2,3},{3,2},{4,5},{5,4},{6,7},{7,6},{8,9},{9,8},{10,11... | collective-permute-start | bytes 3145736 | tf_op jit(solution)/shard_map/ppermute | solution.py:420
  1.1 1.2 %copy-start.1 = (f32[128,2048]{1,0:T(8,128)S(1)}, f32[128,2048]{1,0:T(8,128)}, u32[]{:S(2)}) copy-start(f32[128,2048]{1,0:T(8,128)} %refs_5_.1) | copy-start | bytes 3145732
  4.0 23.2 %collective-permute-start.1 = (f32[1728,128]{1,0:T(8,128)}, f32[1728,128]{1,0:T(8,128)S(1)}, u32[]{:S(2)}, u32[]{:S(2)}) collective-permute-start(f32[1728,128]{1,0:T(8,128)} %get-tuple-element.33), channel_id=1, source_target_pairs={{0,4},{1,5},{2,6},{3,7},{4,0},{5,1},{6,2},{7,3},{8,12},{9,13},{10,... | collective-permute-start | bytes 2654216 | tf_op jit(solution)/shard_map/ppermute | solution.py:420
  6.7 19.2 %collective-permute-start.2 = (f32[1472,128]{1,0:T(8,128)}, f32[1472,128]{1,0:T(8,128)S(1)}, u32[]{:S(2)}, u32[]{:S(2)}) collective-permute-start(f32[1472,128]{1,0:T(8,128)} %get-tuple-element.34), channel_id=1, source_target_pairs={{0,2},{1,3},{2,0},{3,1},{4,6},{5,7},{6,4},{7,5},{8,10},{9,11},{10,... | collective-permute-start | bytes 2261000 | tf_op jit(solution)/shard_map/ppermute | solution.py:420
  8.2 12.6 %collective-permute-start.3 = (f32[960,128]{1,0:T(8,128)}, f32[960,128]{1,0:T(8,128)S(1)}, u32[]{:S(2)}, u32[]{:S(2)}) collective-permute-start(f32[960,128]{1,0:T(8,128)} %get-tuple-element.35), channel_id=1, source_target_pairs={{4,8},{5,9},{6,10},{7,11},{8,4},{9,5},{10,6},{11,7},{20,24},{21,25... | collective-permute-start | bytes 1474568 | tf_op jit(solution)/shard_map/ppermute | solution.py:425
  9.6 0.7 copy-start.5
  14.0 3.4 %copy-start = (f32[512,4096]{1,0:T(8,128)S(1)}, f32[512,4096]{1,0:T(8,128)}, u32[]{:S(2)}) copy-start(f32[512,4096]{1,0:T(8,128)} %refs_0_.1) | copy-start | bytes 25165828
  17.4 1.3 %copy-start.2 = (f32[128,2048]{1,0:T(8,128)S(1)}, f32[128,2048]{1,0:T(8,128)}, u32[]{:S(2)}) copy-start(f32[128,2048]{1,0:T(8,128)} %refs_5_.1) | copy-start | bytes 3145732
  17.4 1.3 %copy-start.4 = (s32[1,8]{1,0:T(1,128)S(1)}, s32[1,8]{1,0:T(1,128)}, u32[]{:S(2)}) copy-start(s32[1,8]{1,0:T(1,128)} %refs_4_.7) | copy-start | bytes 100
  20.8 15.9 %copy-start.3 = (f32[4096]{0:T(1024)S(1)}, f32[4096]{0:T(1024)}, u32[]{:S(2)}) copy-start(f32[4096]{0:T(1024)} %param.10) | copy-start | bytes 49156
  27.3 9.3 %collective-permute-start.8 = (f32[3200,128]{1,0:T(8,128)S(1)}, f32[3200,128]{1,0:T(8,128)S(1)}, u32[]{:S(2)}, u32[]{:S(2)}) collective-permute-start(f32[3200,128]{1,0:T(8,128)S(1)} %get-tuple-element.42.refs_5_), channel_id=1, source_target_pairs={{0,1},{1,0},{2,3},{3,2},{4,5},{5,4},{6,7},{7,6},{8,9},{9,8},{10,11... | collective-permute-start | bytes 4915208 | tf_op jit(solution)/shard_map/ppermute | solution.py:420
  27.4 19.0 %collective-permute-start.7 = (f32[1216,128]{1,0:T(8,128)S(1)}, f32[1216,128]{1,0:T(8,128)S(1)}, u32[]{:S(2)}, u32[]{:S(2)}) collective-permute-start(f32[1216,128]{1,0:T(8,128)S(1)} %get-tuple-element.41), channel_id=1, source_target_pairs={{0,2},{1,3},{2,0},{3,1},{4,6},{5,7},{6,4},{7,5},{8,10},{9,11},{10,... | collective-permute-start | bytes 1867784 | tf_op jit(solution)/shard_map/ppermute | solution.py:420
  29.2 17.3 %collective-permute-start.4 = (f32[960,128]{1,0:T(8,128)S(1)}, f32[960,128]{1,0:T(8,128)S(1)}, u32[]{:S(2)}, u32[]{:S(2)}) collective-permute-start(f32[960,128]{1,0:T(8,128)S(1)} %get-tuple-element.38.refs_1_), channel_id=1, source_target_pairs={{4,0},{5,1},{6,2},{7,3},{8,12},{9,13},{10,14},{11,15},{20,16},{21,... | collective-permute-start | bytes 1474568 | tf_op jit(solution)/shard_map/ppermute | solution.py:425
  30.5 15.1 %collective-permute-start.5 = (f32[704,128]{1,0:T(8,128)S(1)}, f32[704,128]{1,0:T(8,128)S(1)}, u32[]{:S(2)}, u32[]{:S(2)}) collective-permute-start(f32[704,128]{1,0:T(8,128)S(1)} %get-tuple-element.39), channel_id=1, source_target_pairs={{4,8},{5,9},{6,10},{7,11},{8,4},{9,5},{10,6},{11,7},{20,24},{21,25... | collective-permute-start | bytes 1081352 | tf_op jit(solution)/shard_map/ppermute | solution.py:425
  31.2 14.4 %collective-permute-start.6 = (f32[192,128]{1,0:T(8,128)S(1)}, f32[192,128]{1,0:T(8,128)S(1)}, u32[]{:S(2)}, u32[]{:S(2)}) collective-permute-start(f32[192,128]{1,0:T(8,128)S(1)} %get-tuple-element.40), channel_id=1, source_target_pairs={{0,12},{1,13},{2,14},{3,15},{12,0},{13,1},{14,2},{15,3},{16,28},{1... | collective-permute-start | bytes 294920 | tf_op jit(solution)/shard_map/ppermute | solution.py:425
  46.6 3.0 %collective-permute-start.11 = (f32[2368,128]{1,0:T(8,128)S(1)}, f32[2368,128]{1,0:T(8,128)S(1)}, u32[]{:S(2)}, u32[]{:S(2)}) collective-permute-start(f32[2368,128]{1,0:T(8,128)S(1)} %get-tuple-element.48.refs_5_), channel_id=1, source_target_pairs={{0,1},{1,0},{2,3},{3,2},{4,5},{5,4},{6,7},{7,6},{8,9},{9,8},{10,11... | collective-permute-start | bytes 3637256 | tf_op jit(solution)/shard_map/ppermute | solution.py:420
  46.7 10.7 %collective-permute-start.9 = (f32[640,128]{1,0:T(8,128)S(1)}, f32[640,128]{1,0:T(8,128)S(1)}, u32[]{:S(2)}, u32[]{:S(2)}) collective-permute-start(f32[640,128]{1,0:T(8,128)S(1)} %get-tuple-element.46), channel_id=1, source_target_pairs={{0,2},{1,3},{2,0},{3,1},{4,6},{5,7},{6,4},{7,5},{8,10},{9,11},{10,... | collective-permute-start | bytes 983048 | tf_op jit(solution)/shard_map/ppermute | solution.py:420
  47.1 10.3 %collective-permute-start.10 = (f32[512,128]{1,0:T(8,128)S(1)}, f32[512,128]{1,0:T(8,128)S(1)}, u32[]{:S(2)}, u32[]{:S(2)}) collective-permute-start(f32[512,128]{1,0:T(8,128)S(1)} %get-tuple-element.47.refs_2_), channel_id=1, source_target_pairs={{4,0},{5,1},{6,2},{7,3},{8,12},{9,13},{10,14},{11,15},{20,16},{21,... | collective-permute-start | bytes 786440 | tf_op jit(solution)/shard_map/ppermute | solution.py:425
  57.4 2.1 %collective-permute-start.12 = (f32[1152,128]{1,0:T(8,128)S(1)}, f32[1152,128]{1,0:T(8,128)S(1)}, u32[]{:S(2)}, u32[]{:S(2)}) collective-permute-start(f32[1152,128]{1,0:T(8,128)S(1)} %turn_3.1.refs_5_), channel_id=1, source_target_pairs={{0,1},{1,0},{2,3},{3,2},{4,5},{5,4},{6,7},{7,6},{8,9},{9,8},{10,11... | collective-permute-start | bytes 1769480 | tf_op jit(solution)/shard_map/ppermute | solution.py:420

commit v7 on v6

--- a/solution.py
+++ b/solution.py
@@ -9,6 +9,8 @@
 
 TILE = 128
 HALF = TILE // 2
+QUARTER = TILE // 4
+FOLD, PAIR, FIRST = HALF, HALF + QUARTER, TILE + QUARTER
 MIB = 1024 * 1024
 
 ORDER = (0, 2, 1, 3, 4, 6, 5, 7)
@@ -45,8 +47,16 @@
     return 4 * place + 2 * (((seen_from >> 1) & 1) ^ (column & 1)) + core
 
 
+def diagonal_rows(name):
+    return TILE if name in ROUNDS[-1] else PAIR
+
+
+def first_rows(name):
+    return diagonal_rows(name) + HALF if PIECES[name][1] else 0
+
+
 def piece_rows(*names):
-    return sum((TILE + HALF if PIECES[name][1] else 0) + 2 * TILE * len(PIECES[name][2]) for name in names)
+    return sum(first_rows(name) + 2 * TILE * len(PIECES[name][2]) for name in names)
 
 
 def piece_table():
@@ -54,9 +64,9 @@
     for name, (owner, own, classes) in PIECES.items():
         kind = KINDS.index(name)
         for place, column in enumerate(classes):
-            table[owner * CLASSES + column] = kind * 64 + (3 if own else 0) + 4 * place
+            table[owner * CLASSES + column] = kind * 64 + first_rows(name) // QUARTER + 8 * place
         if own:
-            table[owner * CLASSES + owner] = kind * 64 + 2
+            table[owner * CLASSES + owner] = kind * 64 + diagonal_rows(name) // QUARTER
     return jnp.array(table, jnp.int32)
 
 
@@ -92,56 +102,61 @@
 
 
 def pack_kernel(sets, me_ref, rows_ref, *refs):
-    packed_refs, pair_ref, half_ref, pair_sem, half_sem, sems = refs[: len(sets)], *refs[len(sets) :]
+    packed_refs, own_ref, first_sems, sems = refs[: len(sets)], *refs[len(sets) :]
     me = me_ref[0]
 
     def tile(q):
         return rows_ref.at[:, pl.ds(pl.multiple_of(q * TILE, TILE), TILE)]
 
-    pair = pltpu.make_async_copy(tile(me ^ 1), pair_ref, pair_sem)
-    pair.start()
-    copies, halves = [], []
+    copies, firsts = [], []
     for names, packed_ref in zip(sets, packed_refs, strict=True):
         row = 0
         for name in names:
             owner, own, classes = PIECES[name]
             receiver = device_of(owner, me, 0) if owner < 4 else me ^ 12
-            columns = [device_of(column, receiver, core) for column in classes for core in range(2)]
             if own:
-                copies.append((tile(me), packed_ref.at[pl.ds(row, TILE), :]))
-                halves.append((half_ref, packed_ref.at[pl.ds(row + TILE, HALF), :]))
-                row += TILE + HALF
-            for q in columns:
+                firsts.append((own_ref, packed_ref.at[pl.ds(row, FIRST), :]))
+                row += FIRST
+            for q in [device_of(column, receiver, core) for column in classes for core in range(2)]:
                 copies.append((tile(q), packed_ref.at[pl.ds(row, TILE), :]))
                 row += TILE
     copies = [pltpu.make_async_copy(*ends, sems.at[i]) for i, ends in enumerate(copies)]
-    halves = [pltpu.make_async_copy(*ends, half_sem.at[i]) for i, ends in enumerate(halves)]
+    firsts = [pltpu.make_async_copy(*ends, first_sems.at[i]) for i, ends in enumerate(firsts)]
     for copy in copies:
         copy.start()
-    pair.wait()
-    half_ref[...] = jnp.where(me % 2 == 0, pair_ref[:HALF, :], pair_ref[...].T[HALF:, :])
-    for copy in halves:
+    diagonal, pair = tile(me)[...], tile(me ^ 1)[...]
+    own_ref[:FOLD, :] = diagonal[:HALF, :]
+    first, second = diagonal[HALF : HALF + QUARTER, :], diagonal[HALF + QUARTER :, :]
+    left = lax.broadcasted_iota(jnp.int32, first.shape, 1) < HALF
+    own_ref[FOLD:PAIR, :] = jnp.where(left, pltpu.roll(first, HALF, 1), second)
+    own_ref[PAIR:FIRST, :] = jnp.where(me % 2 == 0, pair[:HALF, :], pair.T[HALF:, :])
+    for copy in firsts:
         copy.start()
-    for copy in (*copies, *halves):
+    for copy in (*copies, *firsts):
         copy.wait()
 
 
-def pack(sets, me, sep_rows):
+def unfold(value):
+    top, fold = value[:HALF, :], value[FOLD:PAIR, :]
+    upper = jnp.concatenate([top, pltpu.roll(fold, HALF, 1), fold], axis=0)
+    row, column = (lax.broadcasted_iota(jnp.int32, upper.shape, k) for k in range(2))
+    return jnp.where((row >= HALF) & (column < HALF), upper.T, upper)
+
+
+def pack(sets, me, sep_rows, after=()):
     names = [name for names in sets for name in names]
-    tiles = sum(PIECES[name][1] + 2 * len(PIECES[name][2]) for name in names)
-    anywhere = pl.BlockSpec(memory_space=pl.ANY)
+    tiles = sum(2 * len(PIECES[name][2]) for name in names)
     return call(
         functools.partial(pack_kernel, sets),
-        "pack",
-        [("smem", me), ("any", sep_rows)],
-        [jax.ShapeDtypeStruct((piece_rows(*names), TILE), jnp.float32) for names in sets],
-        [anywhere] * len(sets),
+        "pack_" + names[0],
+        [("smem", me), ("vmem", sep_rows)],
+        [pltpu.HBM((piece_rows(*names), TILE), jnp.float32) for names in sets],
+        [pl.BlockSpec(memory_space=pltpu.HBM)] * len(sets),
+        after,
         scratch_shapes=[
-            pltpu.VMEM((TILE, TILE), jnp.float32),
-            pltpu.VMEM((HALF, TILE), jnp.float32),
-            pltpu.SemaphoreType.DMA(()),
+            pltpu.VMEM((FIRST, TILE), jnp.float32),
             pltpu.SemaphoreType.DMA((len(names),)),
-            pltpu.SemaphoreType.DMA((tiles,)),
+            pltpu.SemaphoreType.DMA((max(tiles, 1),)),
         ],
     )
 
@@ -192,7 +207,7 @@
                 i, j = jnp.where(turned, b, a), jnp.where(turned, a, b)
                 entry = table_ref[c * CLASSES + d]
                 halved = (c == d) & (c != 0)
-                first = (entry & 63) + jnp.where(halved, 0, 2 * (q & 1))
+                first = (entry & 63) + jnp.where(halved, 0, 4 * (q & 1))
                 first = jnp.where(c == 0, q, first)
                 which = ((entry >> 6) * 2 + jnp.where(halved, 0, (r ^ me) & 1)) * 3 + jnp.where(halved, 2, 0)
                 add(which, first, i, j)
@@ -223,11 +238,13 @@
             if name == "rows":
                 value = pair[other][:, pl.ds(pl.multiple_of(code * TILE, TILE), TILE)]
             elif sort == 2:
-                rows = pl.ds(pl.multiple_of(start + code * HALF, HALF), HALF)
+                rows = pl.ds(pl.multiple_of(start + code * QUARTER, QUARTER), HALF)
                 mine, theirs = pair[0][rows, :], pair[1][rows, :]
                 value = jnp.concatenate([jnp.where(even, mine, theirs), jnp.where(even, theirs, mine)], axis=0)
             else:
-                value = pair[other][pl.ds(pl.multiple_of(start + code * HALF, HALF), TILE), :]
+                length = diagonal_rows(name) if sort == 1 else TILE
+                value = pair[other][pl.ds(pl.multiple_of(start + code * QUARTER, QUARTER), length), :]
+                value = unfold(value) if length == PAIR else value
             return node, i, j, slot_i, slot_j, value
 
         def put(sort, node, i, j, slot_i, slot_j, value):
@@ -466,7 +483,9 @@
     mid, far, onward = piece_rows("mid"), piece_rows("far"), piece_rows("side_mid")
 
     def take(m_ref, f_ref):
-        copy_rows(part_ref, copy_rows(part_ref, 0, m_ref, 0, onward), f_ref, 0, far)
+        for row, ref, count in ((0, m_ref, onward), (onward, f_ref, piece_rows("side_far"))):
+            part_ref[row : row + TILE, :] = unfold(ref[:PAIR, :])
+            copy_rows(part_ref, row + TILE, ref, PAIR, count - TILE)
         copy_rows(held_ref, 0, m_ref)
         copy_rows(held_ref, mid + side_near_ref.shape[0], f_ref, 0, far)
 
@@ -490,7 +509,8 @@
     me = lax.axis_index("pr").astype(jnp.int32).reshape(1)
     between_inner, between_outer, outward = {1: 2, 2: 1}, {0: 3, 3: 0}, {1: 0, 2: 3}
 
-    near, side, mid, first = pack((("near",), ("side",), ("mid",), ("far",)), me, sep_inv)
+    near, side = pack((("near",), ("side",)), me, sep_inv)
+    mid, first = pack((("mid",), ("far",)), me, sep_inv, (near,))
     rows_other = swap(sep_inv, 1)
     near, side, mid = swap(near, 4), swap(side, 2), move(mid, between_inner)
     plan = plan_jobs(me, patterns, (rows_other,))

time: 67.3 us -> 66.7 us (level)
  waiting for transfers between devices: 11.1 us -> 7.18 us
  Pallas kernels: 32.1 us -> 34.1 us
  local copies, waits for them, and re-layouts: 6.03 us -> 7.19 us
    ppermute x8, waiting for transfers between devices: 9.54 us -> 6.42 us  [swap(): return lax.ppermute(value, 'pr', [(i, i ^ mask) for i in range(DEVICES)])]
    pallas_call x10 -> x11, Pallas kernels: 32.1 us -> 34.1 us  [call(): pl.pallas_call(body, out_shape=out_shape, in_specs=[pl.BlockSpec(memory_s...]
    unnamed x13 -> x17, local copies, waits for them, and re-layouts: 6.03 us -> 7.19 us
    ppermute x5, waiting for transfers between devices: 1.53 us -> 0.76 us  [move(): return lax.ppermute(value, 'pr', pairs)]
  transfers between devices with their start and end apart: 13 -> 13, of which waited for: 6 -> 6; matrix products, arithmetic and copies ran while one was open for 1% -> 1% of each run, Pallas kernels for 37% -> 39%
where the time goes in v7:
time: 66.7 us
  Pallas kernels  34.1 us (51%)
  starting transfers between devices  17.1 us (26%)
  local copies, waits for them, and re-layouts  7.19 us (11%)
  waiting for transfers between devices  7.18 us (11%)
  between operations  1.06 us (2%)
    pallas_call x11, Pallas kernels, call(): pl.pallas_call(body, out_shape=out_shape, in_specs=[pl.BlockSpec(memory_s...  34.1 us
    ppermute x5, starting transfers between devices, move(): return lax.ppermute(value, 'pr', pairs)  9.44 us
    ppermute x8, starting transfers between devices, swap(): return lax.ppermute(value, 'pr', [(i, i ^ mask) for i in range(DEVICES)])  7.67 us
    unnamed x17, local copies, waits for them, and re-layouts  7.19 us
    ppermute x8, waiting for transfers between devices, swap(): return lax.ppermute(value, 'pr', [(i, i ^ mask) for i in range(DEVICES)])  6.42 us
  transfers between devices with their start and end apart: 13, of which 6 were waited for; matrix products, arithmetic and copies ran while one was open for 1% of the time, Pallas kernels for 39%

profile of v7, /device:TPU:0, one launch (start us, length us, event | category | flops | bytes accessed | tf_op | source)
XLA Modules:
  0.0 66.7 jit_solution(7113902063823261353)
XLA Ops:
  1.1 1.2 %copy-done = f32[128,2048]{1,0:T(8,128)S(1)} copy-done((f32[128,2048]{1,0:T(8,128)S(1)}, f32[128,2048]{1,0:T(8,128)}, u32[]{:S(2)}) %copy-start) | copy-done | bytes 1048600
  2.4 1.4 %pack_near.1 = (f32[1696,128]{1,0:T(8,128)}, f32[1440,128]{1,0:T(8,128)}) custom-call(s32[1]{0:T(128)} %bitcast.refs_0_, f32[128,2048]{1,0:T(8,128)S(1)} %copy-done), custom_call_target="tpu_custom_call" | custom-call | tf_op jit(solution)/shard_map/pack_near/pallas_call | solution.py:81
  3.7 2.7 %collective-permute-start.1 = (f32[1696,128]{1,0:T(8,128)}, f32[1696,128]{1,0:T(8,128)S(1)}, u32[]{:S(2)}, u32[]{:S(2)}) collective-permute-start(f32[1696,128]{1,0:T(8,128)} %get-tuple-element.33.refs_2_), channel_id=1, source_target_pairs={{0,4},{1,5},{2,6},{3,7},{4,0},{5,1},{6,2},{7,3},{8,12},{9,13},{10,... | collective-permute-start | bytes 2605064 | tf_op jit(solution)/shard_map/ppermute | solution.py:437
  6.4 1.5 %collective-permute-start.2 = (f32[1440,128]{1,0:T(8,128)}, f32[1440,128]{1,0:T(8,128)S(1)}, u32[]{:S(2)}, u32[]{:S(2)}) collective-permute-start(f32[1440,128]{1,0:T(8,128)} %get-tuple-element.34), channel_id=1, source_target_pairs={{0,2},{1,3},{2,0},{3,1},{4,6},{5,7},{6,4},{7,5},{8,10},{9,11},{10,... | collective-permute-start | bytes 2211848 | tf_op jit(solution)/shard_map/ppermute | solution.py:437
  7.9 1.2 %copy-done.3 = f32[1696,128]{1,0:T(8,128)S(1)} copy-done((f32[1696,128]{1,0:T(8,128)S(1)}, f32[1696,128]{1,0:T(8,128)}, u32[]{:S(2)}) %copy-start.3) | copy-done | bytes 868376
  9.1 0.9 %pack_mid.1 = (f32[928,128]{1,0:T(8,128)}, f32[160,128]{1,0:T(8,128)}) custom-call(s32[1]{0:T(128)} %bitcast.refs_0_, f32[128,2048]{1,0:T(8,128)S(1)} %copy-done, f32[1696,128]{1,0:T(8,128)S(1)} %copy-done.3), custom_call_target="tpu_custom_call" | custom-call | tf_op jit(solution)/shard_map/pack_mid/pallas_call | solution.py:81
  10.0 0.7 %collective-permute-start.3 = (f32[928,128]{1,0:T(8,128)}, f32[928,128]{1,0:T(8,128)S(1)}, u32[]{:S(2)}, u32[]{:S(2)}) collective-permute-start(f32[928,128]{1,0:T(8,128)} %get-tuple-element.35), channel_id=1, source_target_pairs={{4,8},{5,9},{6,10},{7,11},{8,4},{9,5},{10,6},{11,7},{20,24},{21,25... | collective-permute-start | bytes 1425416 | tf_op jit(solution)/shard_map/ppermute | solution.py:442
  10.7 0.8 %copy.17.refs_2_ = s32[8,4]{1,0:T(8,128)S(1)} copy(s32[8,4]{0,1:T(4,128)} %param.9) | data formatting | bytes 256 | tf_op args[3]
  12.1 3.7 %plan_jobs.1 = (s32[54,32]{1,0:T(8,128)S(1)}, s32[54]{0:T(128)S(1)}, s32[5,32]{1,0:T(8,128)S(1)}) custom-call(s32[1]{0:T(128)} %bitcast.refs_0_, s32[64]{0:T(128)S(1)} %copy-done.6, s32[8,4]{1,0:T(8,128)S(1)} %copy.17.refs_2_, f32[128,2048]{1,0:T(8,128)S(1)} %collective-permute-done.refs_3_.refs_6_), custom_call_target="tpu_custom_call" | custom-call | tf_op jit(solution)/shard_map/plan_jobs/pallas_call | solution.py:81
  15.8 3.4 %copy-done.2 = f32[512,4096]{1,0:T(8,128)S(1)} copy-done((f32[512,4096]{1,0:T(8,128)S(1)}, f32[512,4096]{1,0:T(8,128)}, u32[]{:S(2)}) %copy-start.2) | copy-done | bytes 8388632
  19.2 1.3 %factor_halves.1 = (bf16[512,4096]{1,0:T(8,128)(2,1)S(1)}, bf16[512,4096]{1,0:T(8,128)(2,1)S(1)}) custom-call(f32[512,4096]{1,0:T(8,128)S(1)} %copy-done.2, s32[54]{0:T(128)S(1)} %get-tuple-element.31.refs_1_.refs_2_), custom_call_target="tpu_custom_call" | custom-call | tf_op jit(solution)/shard_map/factor_halves/pallas_call | solution.py:81
  20.5 2.1 %put_rows.1 = (bf16[8,512,512]{2,1,0:T(8,128)(2,1)S(1)}, bf16[8,512,512]{2,1,0:T(8,128)(2,1)S(1)}) custom-call(s32[1]{0:T(128)} %bitcast.refs_0_, s32[54,32]{1,0:T(8,128)S(1)} %get-tuple-element.30.refs_1_, s32[54]{0:T(128)S(1)} %get-tuple-element.31.refs_1_.refs_2_, s32[5,32]{1,0:T(8,128)S(1)} %get-tuple-element.32.refs_3_, s32[1,8]{1,0:T(1,128)S(1)} %copy-done.5, ...), custom_call_target="tpu_custom_call" | custom-call | tf_op jit(solution)/shard_map/put_rows/pallas_call | solution.py:81
  22.6 2.6 %collective-permute-done.2.refs_2_ = f32[1440,128]{1,0:T(8,128)S(1)} collective-permute-done((f32[1440,128]{1,0:T(8,128)}, f32[1440,128]{1,0:T(8,128)S(1)}, u32[]{:S(2)}, u32[]{:S(2)}) %collective-permute-start.2) | collective-permute-done | bytes 737312 | tf_op jit(solution)/shard_map/ppermute | solution.py:437
  25.2 1.3 %collective-permute-done.1.refs_1_ = f32[1696,128]{1,0:T(8,128)S(1)} collective-permute-done((f32[1696,128]{1,0:T(8,128)}, f32[1696,128]{1,0:T(8,128)S(1)}, u32[]{:S(2)}, u32[]{:S(2)}) %collective-permute-start.1) | collective-permute-done | bytes 868384 | tf_op jit(solution)/shard_map/ppermute | solution.py:437
  26.8 1.7 %collective-permute-start.7 = (f32[1184,128]{1,0:T(8,128)S(1)}, f32[1184,128]{1,0:T(8,128)S(1)}, u32[]{:S(2)}, u32[]{:S(2)}) collective-permute-start(f32[1184,128]{1,0:T(8,128)S(1)} %get-tuple-element.41), channel_id=1, source_target_pairs={{0,2},{1,3},{2,0},{3,1},{4,6},{5,7},{6,4},{7,5},{8,10},{9,11},{10,... | collective-permute-start | bytes 1818632 | tf_op jit(solution)/shard_map/ppermute | solution.py:437
  28.5 1.3 %collective-permute-start.4 = (f32[928,128]{1,0:T(8,128)S(1)}, f32[928,128]{1,0:T(8,128)S(1)}, u32[]{:S(2)}, u32[]{:S(2)}) collective-permute-start(f32[928,128]{1,0:T(8,128)S(1)} %get-tuple-element.38.refs_1_), channel_id=1, source_target_pairs={{4,0},{5,1},{6,2},{7,3},{8,12},{9,13},{10,14},{11,15},{20,16},{21,... | collective-permute-start | bytes 1425416 | tf_op jit(solution)/shard_map/ppermute | solution.py:442
  29.8 0.7 %collective-permute-start.5 = (f32[672,128]{1,0:T(8,128)S(1)}, f32[672,128]{1,0:T(8,128)S(1)}, u32[]{:S(2)}, u32[]{:S(2)}) collective-permute-start(f32[672,128]{1,0:T(8,128)S(1)} %get-tuple-element.39), channel_id=1, source_target_pairs={{4,8},{5,9},{6,10},{7,11},{8,4},{9,5},{10,6},{11,7},{20,24},{21,25... | collective-permute-start | bytes 1032200 | tf_op jit(solution)/shard_map/ppermute | solution.py:442
  30.5 5.5 %collective-permute-start.6 = (f32[160,128]{1,0:T(8,128)S(1)}, f32[160,128]{1,0:T(8,128)S(1)}, u32[]{:S(2)}, u32[]{:S(2)}) collective-permute-start(f32[160,128]{1,0:T(8,128)S(1)} %copy-done.7), channel_id=1, source_target_pairs={{0,12},{1,13},{2,14},{3,15},{12,0},{13,1},{14,2},{15,3},{16,28},{1... | collective-permute-start | bytes 245768 | tf_op jit(solution)/shard_map/ppermute | solution.py:442
  36.1 8.8 %put_near_multiply_0.1 = (bf16[8,512,512]{2,1,0:T(8,128)(2,1)S(1)}, bf16[8,512,512]{2,1,0:T(8,128)(2,1)S(1)}, f32[32,128]{1,0:T(8,128)S(1)}, f32[512,4096]{1,0:T(8,128)}) custom-call(s32[1]{0:T(128)} %bitcast.refs_0_, s32[54,32]{1,0:T(8,128)S(1)} %get-tuple-element.30.refs_1_, ...), custom_call_target="tpu_custom_call", output_to_operand_aliasing={{0}: (10, {}), {1}: (11, {})} | custom-call | tf_op jit(solution)/shard_map/put_near_multiply_0/pallas_call | solution.py:81
  45.6 0.8 %collective-permute-start.9 = (f32[640,128]{1,0:T(8,128)S(1)}, f32[640,128]{1,0:T(8,128)S(1)}, u32[]{:S(2)}, u32[]{:S(2)}) collective-permute-start(f32[640,128]{1,0:T(8,128)S(1)} %get-tuple-element.46), channel_id=1, source_target_pairs={{0,2},{1,3},{2,0},{3,1},{4,6},{5,7},{6,4},{7,5},{8,10},{9,11},{10,... | collective-permute-start | bytes 983048 | tf_op jit(solution)/shard_map/ppermute | solution.py:437
  46.4 1.3 %collective-permute-start.10 = (f32[512,128]{1,0:T(8,128)S(1)}, f32[512,128]{1,0:T(8,128)S(1)}, u32[]{:S(2)}, u32[]{:S(2)}) collective-permute-start(f32[512,128]{1,0:T(8,128)S(1)} %get-tuple-element.47.refs_2_), channel_id=1, source_target_pairs={{4,0},{5,1},{6,2},{7,3},{8,12},{9,13},{10,14},{11,15},{20,16},{21,... | collective-permute-start | bytes 786440 | tf_op jit(solution)/shard_map/ppermute | solution.py:442
  48.2 7.9 %put_mid_multiply_1.1 = (bf16[8,512,512]{2,1,0:T(8,128)(2,1)S(1)}, bf16[8,512,512]{2,1,0:T(8,128)(2,1)S(1)}, f32[32,128]{1,0:T(8,128)S(1)}, f32[512,4096]{1,0:T(8,128)}) custom-call(s32[1]{0:T(128)} %bitcast.refs_0_, s32[54,32]{1,0:T(8,128)S(1)} %get-tuple-element.30.refs_1_, ...), custom_call_target="tpu_custom_call", output_to_operand_aliasing={{0}: (10, {}), {1}: (11, {}), {3}: (12, {})} | custom-call | tf_op jit(solution)/shard_map/put_mid_multiply_1/pallas_call | solution.py:81
  56.8 2.0 %collective-permute-done.12.refs_6_ = f32[1152,128]{1,0:T(8,128)S(1)} collective-permute-done((f32[1152,128]{1,0:T(8,128)S(1)}, f32[1152,128]{1,0:T(8,128)S(1)}, u32[]{:S(2)}, u32[]{:S(2)}) %collective-permute-start.12) | collective-permute-done | bytes 589856 | tf_op jit(solution)/shard_map/ppermute | solution.py:437
  58.8 7.6 %put_side_mid_multiply_2.1 = (bf16[8,512,512]{2,1,0:T(8,128)(2,1)S(1)}, bf16[8,512,512]{2,1,0:T(8,128)(2,1)S(1)}, f32[32,128]{1,0:T(8,128)}, f32[512,4096]{1,0:T(8,128)}) custom-call(s32[1]{0:T(128)} %bitcast.refs_0_, s32[54,32]{1,0:T(8,128)S(1)} %get-tuple-element.30.refs_1_, ...), custom_call_target="tpu_custom_call", output_to_operand_aliasing={{0}: (10, {}), {1}: (11, {}), {3}: (12, {})} | custom-call | tf_op jit(solution)/shard_map/put_side_mid_multiply_2/pallas_call | solution.py:81
  (30 shorter events, 3.3 us)
Async XLA Ops:
  0.6 10.8 %collective-permute-start = (f32[128,2048]{1,0:T(8,128)}, f32[128,2048]{1,0:T(8,128)S(1)}, u32[]{:S(2)}, u32[]{:S(2)}) collective-permute-start(f32[128,2048]{1,0:T(8,128)} %refs_5_.1), channel_id=1, source_target_pairs={{0,1},{1,0},{2,3},{3,2},{4,5},{5,4},{6,7},{7,6},{8,9},{9,8},{10,11... | collective-permute-start | bytes 3145736 | tf_op jit(solution)/shard_map/ppermute | solution.py:437
  1.1 1.2 %copy-start = (f32[128,2048]{1,0:T(8,128)S(1)}, f32[128,2048]{1,0:T(8,128)}, u32[]{:S(2)}) copy-start(f32[128,2048]{1,0:T(8,128)} %refs_5_.1) | copy-start | bytes 3145732
  3.7 22.8 %collective-permute-start.1 = (f32[1696,128]{1,0:T(8,128)}, f32[1696,128]{1,0:T(8,128)S(1)}, u32[]{:S(2)}, u32[]{:S(2)}) collective-permute-start(f32[1696,128]{1,0:T(8,128)} %get-tuple-element.33.refs_2_), channel_id=1, source_target_pairs={{0,4},{1,5},{2,6},{3,7},{4,0},{5,1},{6,2},{7,3},{8,12},{9,13},{10,... | collective-permute-start | bytes 2605064 | tf_op jit(solution)/shard_map/ppermute | solution.py:437
  6.4 18.8 %collective-permute-start.2 = (f32[1440,128]{1,0:T(8,128)}, f32[1440,128]{1,0:T(8,128)S(1)}, u32[]{:S(2)}, u32[]{:S(2)}) collective-permute-start(f32[1440,128]{1,0:T(8,128)} %get-tuple-element.34), channel_id=1, source_target_pairs={{0,2},{1,3},{2,0},{3,1},{4,6},{5,7},{6,4},{7,5},{8,10},{9,11},{10,... | collective-permute-start | bytes 2211848 | tf_op jit(solution)/shard_map/ppermute | solution.py:437
  7.9 1.2 %copy-start.3 = (f32[1696,128]{1,0:T(8,128)S(1)}, f32[1696,128]{1,0:T(8,128)}, u32[]{:S(2)}) copy-start(f32[1696,128]{1,0:T(8,128)} %get-tuple-element.33.refs_2_) | copy-start | bytes 2605060
  10.0 12.7 %collective-permute-start.3 = (f32[928,128]{1,0:T(8,128)}, f32[928,128]{1,0:T(8,128)S(1)}, u32[]{:S(2)}, u32[]{:S(2)}) collective-permute-start(f32[928,128]{1,0:T(8,128)} %get-tuple-element.35), channel_id=1, source_target_pairs={{4,8},{5,9},{6,10},{7,11},{8,4},{9,5},{10,6},{11,7},{20,24},{21,25... | collective-permute-start | bytes 1425416 | tf_op jit(solution)/shard_map/ppermute | solution.py:442
  11.4 0.7 copy-start.6
  15.8 3.4 %copy-start.2 = (f32[512,4096]{1,0:T(8,128)S(1)}, f32[512,4096]{1,0:T(8,128)}, u32[]{:S(2)}) copy-start(f32[512,4096]{1,0:T(8,128)} %refs_0_.1) | copy-start | bytes 25165828
  19.2 1.3 %copy-start.1 = (f32[128,2048]{1,0:T(8,128)S(1)}, f32[128,2048]{1,0:T(8,128)}, u32[]{:S(2)}) copy-start(f32[128,2048]{1,0:T(8,128)} %refs_5_.1) | copy-start | bytes 3145732
  19.2 1.3 %copy-start.5 = (s32[1,8]{1,0:T(1,128)S(1)}, s32[1,8]{1,0:T(1,128)}, u32[]{:S(2)}) copy-start(s32[1,8]{1,0:T(1,128)} %refs_4_.7) | copy-start | bytes 100
  22.6 7.9 %copy-start.7 = (f32[160,128]{1,0:T(8,128)S(1)}, f32[160,128]{1,0:T(8,128)}, u32[]{:S(2)}) copy-start(f32[160,128]{1,0:T(8,128)} %get-tuple-element.40) | copy-start | bytes 245764
  22.6 13.4 %copy-start.4 = (f32[4096]{0:T(1024)S(1)}, f32[4096]{0:T(1024)}, u32[]{:S(2)}) copy-start(f32[4096]{0:T(1024)} %param.10) | copy-start | bytes 49156
  26.7 9.3 %collective-permute-start.8 = (f32[3136,128]{1,0:T(8,128)S(1)}, f32[3136,128]{1,0:T(8,128)S(1)}, u32[]{:S(2)}, u32[]{:S(2)}) collective-permute-start(f32[3136,128]{1,0:T(8,128)S(1)} %get-tuple-element.42.refs_5_), channel_id=1, source_target_pairs={{0,1},{1,0},{2,3},{3,2},{4,5},{5,4},{6,7},{7,6},{8,9},{9,8},{10,11... | collective-permute-start | bytes 4816904 | tf_op jit(solution)/shard_map/ppermute | solution.py:437
  26.8 18.3 %collective-permute-start.7 = (f32[1184,128]{1,0:T(8,128)S(1)}, f32[1184,128]{1,0:T(8,128)S(1)}, u32[]{:S(2)}, u32[]{:S(2)}) collective-permute-start(f32[1184,128]{1,0:T(8,128)S(1)} %get-tuple-element.41), channel_id=1, source_target_pairs={{0,2},{1,3},{2,0},{3,1},{4,6},{5,7},{6,4},{7,5},{8,10},{9,11},{10,... | collective-permute-start | bytes 1818632 | tf_op jit(solution)/shard_map/ppermute | solution.py:437
  28.5 16.6 %collective-permute-start.4 = (f32[928,128]{1,0:T(8,128)S(1)}, f32[928,128]{1,0:T(8,128)S(1)}, u32[]{:S(2)}, u32[]{:S(2)}) collective-permute-start(f32[928,128]{1,0:T(8,128)S(1)} %get-tuple-element.38.refs_1_), channel_id=1, source_target_pairs={{4,0},{5,1},{6,2},{7,3},{8,12},{9,13},{10,14},{11,15},{20,16},{21,... | collective-permute-start | bytes 1425416 | tf_op jit(solution)/shard_map/ppermute | solution.py:442
  29.8 15.0 %collective-permute-start.5 = (f32[672,128]{1,0:T(8,128)S(1)}, f32[672,128]{1,0:T(8,128)S(1)}, u32[]{:S(2)}, u32[]{:S(2)}) collective-permute-start(f32[672,128]{1,0:T(8,128)S(1)} %get-tuple-element.39), channel_id=1, source_target_pairs={{4,8},{5,9},{6,10},{7,11},{8,4},{9,5},{10,6},{11,7},{20,24},{21,25... | collective-permute-start | bytes 1032200 | tf_op jit(solution)/shard_map/ppermute | solution.py:442
  30.5 14.3 %collective-permute-start.6 = (f32[160,128]{1,0:T(8,128)S(1)}, f32[160,128]{1,0:T(8,128)S(1)}, u32[]{:S(2)}, u32[]{:S(2)}) collective-permute-start(f32[160,128]{1,0:T(8,128)S(1)} %copy-done.7), channel_id=1, source_target_pairs={{0,12},{1,13},{2,14},{3,15},{12,0},{13,1},{14,2},{15,3},{16,28},{1... | collective-permute-start | bytes 245768 | tf_op jit(solution)/shard_map/ppermute | solution.py:442
  45.3 2.9 %collective-permute-start.11 = (f32[2272,128]{1,0:T(8,128)S(1)}, f32[2272,128]{1,0:T(8,128)S(1)}, u32[]{:S(2)}, u32[]{:S(2)}) collective-permute-start(f32[2272,128]{1,0:T(8,128)S(1)} %get-tuple-element.48.refs_5_), channel_id=1, source_target_pairs={{0,1},{1,0},{2,3},{3,2},{4,5},{5,4},{6,7},{7,6},{8,9},{9,8},{10,11... | collective-permute-start | bytes 3489800 | tf_op jit(solution)/shard_map/ppermute | solution.py:437
  45.6 11.1 %collective-permute-start.9 = (f32[640,128]{1,0:T(8,128)S(1)}, f32[640,128]{1,0:T(8,128)S(1)}, u32[]{:S(2)}, u32[]{:S(2)}) collective-permute-start(f32[640,128]{1,0:T(8,128)S(1)} %get-tuple-element.46), channel_id=1, source_target_pairs={{0,2},{1,3},{2,0},{3,1},{4,6},{5,7},{6,4},{7,5},{8,10},{9,11},{10,... | collective-permute-start | bytes 983048 | tf_op jit(solution)/shard_map/ppermute | solution.py:437
  46.4 10.3 %collective-permute-start.10 = (f32[512,128]{1,0:T(8,128)S(1)}, f32[512,128]{1,0:T(8,128)S(1)}, u32[]{:S(2)}, u32[]{:S(2)}) collective-permute-start(f32[512,128]{1,0:T(8,128)S(1)} %get-tuple-element.47.refs_2_), channel_id=1, source_target_pairs={{4,0},{5,1},{6,2},{7,3},{8,12},{9,13},{10,14},{11,15},{20,16},{21,... | collective-permute-start | bytes 786440 | tf_op jit(solution)/shard_map/ppermute | solution.py:442
  56.7 2.1 %collective-permute-start.12 = (f32[1152,128]{1,0:T(8,128)S(1)}, f32[1152,128]{1,0:T(8,128)S(1)}, u32[]{:S(2)}, u32[]{:S(2)}) collective-permute-start(f32[1152,128]{1,0:T(8,128)S(1)} %turn_3.1.refs_5_), channel_id=1, source_target_pairs={{0,1},{1,0},{2,3},{3,2},{4,5},{5,4},{6,7},{7,6},{8,9},{9,8},{10,11... | collective-permute-start | bytes 1769480 | tf_op jit(solution)/shard_map/ppermute | solution.py:437

commit v8 on v7

--- a/solution.py
+++ b/solution.py
@@ -252,26 +252,54 @@
             if sort != 1:
                 place(high_ref, low_ref, node, slot_j, i, value.T)
 
+        def put_all(jobs):
+            for sort, job in jobs:
+                put(sort, *job)
+
+        def list_of(other, sort):
+            return (KINDS.index(name) * 2 + other) * 3 + sort
+
+        def diagonals():
+            lists = [list_of(other, 1) for other in range(2)]
+            numbers = [count_ref[which] for which in lists]
+            both = (numbers[0] > 0) & (numbers[1] > 0)
+
+            def some(chosen):
+                def step(i, _):
+                    jobs = []
+                    for k in chosen:
+                        for at in (2 * i, 2 * i + 1):
+                            jobs.append((1, read(lists[k], 1, jnp.minimum(at, numbers[k] - 1))))
+                    put_all(jobs)
+                    return 0
+
+                return step
+
+            most = jnp.maximum(numbers[0], numbers[1])
+            lax.fori_loop(0, jnp.where(both, lax.div(most + 1, 2), 0), some((0, 1)), 0)
+            for k in range(2):
+                lax.fori_loop(0, jnp.where(both, 0, lax.div(numbers[k] + 1, 2)), some((k,)), 0)
+
+        if name != "far_rest":
+            diagonals()
         for other in range(2):
-            for sort in range(3):
-                which = (KINDS.index(name) * 2 + other) * 3 + sort
-                if sort == 2 and (other == 1 or name == "rows" or not PIECES[name][1]) or sort == 1 and name == "far_rest":
+            for sort in (0, 2):
+                which = list_of(other, sort)
+                if sort == 2 and (other == 1 or name == "rows" or not PIECES[name][1]):
                     continue
                 if sort == 0 and name != "rows" and not PIECES[name][2]:
                     continue
                 number = count_ref[which]
 
                 def two(i, _):
-                    first, second = read(which, sort, 2 * i), read(which, sort, 2 * i + 1)
-                    put(sort, *first)
-                    put(sort, *second)
+                    put_all([(sort, read(which, sort, 2 * i)), (sort, read(which, sort, 2 * i + 1))])
                     return 0
 
                 lax.fori_loop(0, lax.div(number, 2), two, 0)
 
                 @pl.when(lax.rem(number, 2) == 1)
                 def _():
-                    put(sort, *read(which, sort, number - 1))
+                    put_all([(sort, read(which, sort, number - 1))])
 
     at = 0
     for names in sets:

time: 66.7 us -> 66.5 us (level)
  transfers between devices with their start and end apart: 13 -> 13, of which waited for: 6 -> 5; matrix products, arithmetic and copies ran while one was open for 1% -> 1% of each run, Pallas kernels for 39% -> 39%
where the time goes in v8:
time: 66.5 us; the launch traced here: 66.2 us
  Pallas kernels  33.9 us (51%)
  starting transfers between devices  16.8 us (25%)
  waiting for transfers between devices  7.25 us (11%)
  local copies, waits for them, and re-layouts  7.19 us (11%)
  between operations  1.06 us (2%)
    pallas_call x11, Pallas kernels, call(): pl.pallas_call(body, out_shape=out_shape, in_specs=[pl.BlockSpec(memory_s...  33.9 us
    ppermute x5, starting transfers between devices, move(): return lax.ppermute(value, 'pr', pairs)  9.44 us
    ppermute x8, starting transfers between devices, swap(): return lax.ppermute(value, 'pr', [(i, i ^ mask) for i in range(DEVICES)])  7.33 us
    unnamed x17, local copies, waits for them, and re-layouts  7.19 us
    ppermute x8, waiting for transfers between devices, swap(): return lax.ppermute(value, 'pr', [(i, i ^ mask) for i in range(DEVICES)])  6.75 us
  transfers between devices with their start and end apart: 13, of which 5 were waited for; matrix products, arithmetic and copies ran while one was open for 1% of the time, Pallas kernels for 39%

profile of v8, /device:TPU:0, one launch (start us, length us, event | category | flops | bytes accessed | tf_op | source)
XLA Modules:
  0.0 66.2 jit_solution(5046127306334022462)
XLA Ops:
  1.1 1.2 %copy-done = f32[128,2048]{1,0:T(8,128)S(1)} copy-done((f32[128,2048]{1,0:T(8,128)S(1)}, f32[128,2048]{1,0:T(8,128)}, u32[]{:S(2)}) %copy-start) | copy-done | bytes 1048600
  2.4 1.4 %pack_near.1 = (f32[1696,128]{1,0:T(8,128)}, f32[1440,128]{1,0:T(8,128)}) custom-call(s32[1]{0:T(128)} %bitcast.refs_0_, f32[128,2048]{1,0:T(8,128)S(1)} %copy-done), custom_call_target="tpu_custom_call" | custom-call | tf_op jit(solution)/shard_map/pack_near/pallas_call | solution.py:81
  3.7 2.7 %collective-permute-start.1 = (f32[1696,128]{1,0:T(8,128)}, f32[1696,128]{1,0:T(8,128)S(1)}, u32[]{:S(2)}, u32[]{:S(2)}) collective-permute-start(f32[1696,128]{1,0:T(8,128)} %get-tuple-element.33.refs_2_), channel_id=1, source_target_pairs={{0,4},{1,5},{2,6},{3,7},{4,0},{5,1},{6,2},{7,3},{8,12},{9,13},{10,... | collective-permute-start | bytes 2605064 | tf_op jit(solution)/shard_map/ppermute | solution.py:465
  6.4 1.5 %collective-permute-start.2 = (f32[1440,128]{1,0:T(8,128)}, f32[1440,128]{1,0:T(8,128)S(1)}, u32[]{:S(2)}, u32[]{:S(2)}) collective-permute-start(f32[1440,128]{1,0:T(8,128)} %get-tuple-element.34), channel_id=1, source_target_pairs={{0,2},{1,3},{2,0},{3,1},{4,6},{5,7},{6,4},{7,5},{8,10},{9,11},{10,... | collective-permute-start | bytes 2211848 | tf_op jit(solution)/shard_map/ppermute | solution.py:465
  7.9 1.2 %copy-done.3 = f32[1696,128]{1,0:T(8,128)S(1)} copy-done((f32[1696,128]{1,0:T(8,128)S(1)}, f32[1696,128]{1,0:T(8,128)}, u32[]{:S(2)}) %copy-start.3) | copy-done | bytes 868376
  9.1 0.9 %pack_mid.1 = (f32[928,128]{1,0:T(8,128)}, f32[160,128]{1,0:T(8,128)}) custom-call(s32[1]{0:T(128)} %bitcast.refs_0_, f32[128,2048]{1,0:T(8,128)S(1)} %copy-done, f32[1696,128]{1,0:T(8,128)S(1)} %copy-done.3), custom_call_target="tpu_custom_call" | custom-call | tf_op jit(solution)/shard_map/pack_mid/pallas_call | solution.py:81
  10.0 0.7 %collective-permute-start.3 = (f32[928,128]{1,0:T(8,128)}, f32[928,128]{1,0:T(8,128)S(1)}, u32[]{:S(2)}, u32[]{:S(2)}) collective-permute-start(f32[928,128]{1,0:T(8,128)} %get-tuple-element.35), channel_id=1, source_target_pairs={{4,8},{5,9},{6,10},{7,11},{8,4},{9,5},{10,6},{11,7},{20,24},{21,25... | collective-permute-start | bytes 1425416 | tf_op jit(solution)/shard_map/ppermute | solution.py:470
  10.7 0.8 %copy.17.refs_2_ = s32[8,4]{1,0:T(8,128)S(1)} copy(s32[8,4]{0,1:T(4,128)} %param.9) | data formatting | bytes 256 | tf_op args[3]
  12.1 3.7 %plan_jobs.1 = (s32[54,32]{1,0:T(8,128)S(1)}, s32[54]{0:T(128)S(1)}, s32[5,32]{1,0:T(8,128)S(1)}) custom-call(s32[1]{0:T(128)} %bitcast.refs_0_, s32[64]{0:T(128)S(1)} %copy-done.6, s32[8,4]{1,0:T(8,128)S(1)} %copy.17.refs_2_, f32[128,2048]{1,0:T(8,128)S(1)} %collective-permute-done.refs_3_.refs_6_), custom_call_target="tpu_custom_call" | custom-call | tf_op jit(solution)/shard_map/plan_jobs/pallas_call | solution.py:81
  15.8 3.4 %copy-done.2 = f32[512,4096]{1,0:T(8,128)S(1)} copy-done((f32[512,4096]{1,0:T(8,128)S(1)}, f32[512,4096]{1,0:T(8,128)}, u32[]{:S(2)}) %copy-start.2) | copy-done | bytes 8388632
  19.2 1.3 %factor_halves.1 = (bf16[512,4096]{1,0:T(8,128)(2,1)S(1)}, bf16[512,4096]{1,0:T(8,128)(2,1)S(1)}) custom-call(f32[512,4096]{1,0:T(8,128)S(1)} %copy-done.2, s32[54]{0:T(128)S(1)} %get-tuple-element.31.refs_1_.refs_2_), custom_call_target="tpu_custom_call" | custom-call | tf_op jit(solution)/shard_map/factor_halves/pallas_call | solution.py:81
  20.5 2.1 %put_rows.1 = (bf16[8,512,512]{2,1,0:T(8,128)(2,1)S(1)}, bf16[8,512,512]{2,1,0:T(8,128)(2,1)S(1)}) custom-call(s32[1]{0:T(128)} %bitcast.refs_0_, s32[54,32]{1,0:T(8,128)S(1)} %get-tuple-element.30.refs_1_, s32[54]{0:T(128)S(1)} %get-tuple-element.31.refs_1_.refs_2_, s32[5,32]{1,0:T(8,128)S(1)} %get-tuple-element.32.refs_3_, s32[1,8]{1,0:T(1,128)S(1)} %copy-done.5, ...), custom_call_target="tpu_custom_call" | custom-call | tf_op jit(solution)/shard_map/put_rows/pallas_call | solution.py:81
  22.7 2.5 %collective-permute-done.2.refs_2_ = f32[1440,128]{1,0:T(8,128)S(1)} collective-permute-done((f32[1440,128]{1,0:T(8,128)}, f32[1440,128]{1,0:T(8,128)S(1)}, u32[]{:S(2)}, u32[]{:S(2)}) %collective-permute-start.2) | collective-permute-done | bytes 737312 | tf_op jit(solution)/shard_map/ppermute | solution.py:465
  25.2 1.3 %collective-permute-done.1.refs_1_ = f32[1696,128]{1,0:T(8,128)S(1)} collective-permute-done((f32[1696,128]{1,0:T(8,128)}, f32[1696,128]{1,0:T(8,128)S(1)}, u32[]{:S(2)}, u32[]{:S(2)}) %collective-permute-start.1) | collective-permute-done | bytes 868384 | tf_op jit(solution)/shard_map/ppermute | solution.py:465
  26.8 1.7 %collective-permute-start.7 = (f32[1184,128]{1,0:T(8,128)S(1)}, f32[1184,128]{1,0:T(8,128)S(1)}, u32[]{:S(2)}, u32[]{:S(2)}) collective-permute-start(f32[1184,128]{1,0:T(8,128)S(1)} %get-tuple-element.41), channel_id=1, source_target_pairs={{0,2},{1,3},{2,0},{3,1},{4,6},{5,7},{6,4},{7,5},{8,10},{9,11},{10,... | collective-permute-start | bytes 1818632 | tf_op jit(solution)/shard_map/ppermute | solution.py:465
  28.5 1.3 %collective-permute-start.4 = (f32[928,128]{1,0:T(8,128)S(1)}, f32[928,128]{1,0:T(8,128)S(1)}, u32[]{:S(2)}, u32[]{:S(2)}) collective-permute-start(f32[928,128]{1,0:T(8,128)S(1)} %get-tuple-element.38.refs_1_), channel_id=1, source_target_pairs={{4,0},{5,1},{6,2},{7,3},{8,12},{9,13},{10,14},{11,15},{20,16},{21,... | collective-permute-start | bytes 1425416 | tf_op jit(solution)/shard_map/ppermute | solution.py:470
  29.8 0.7 %collective-permute-start.5 = (f32[672,128]{1,0:T(8,128)S(1)}, f32[672,128]{1,0:T(8,128)S(1)}, u32[]{:S(2)}, u32[]{:S(2)}) collective-permute-start(f32[672,128]{1,0:T(8,128)S(1)} %get-tuple-element.39), channel_id=1, source_target_pairs={{4,8},{5,9},{6,10},{7,11},{8,4},{9,5},{10,6},{11,7},{20,24},{21,25... | collective-permute-start | bytes 1032200 | tf_op jit(solution)/shard_map/ppermute | solution.py:470
  30.5 5.5 %collective-permute-start.6 = (f32[160,128]{1,0:T(8,128)S(1)}, f32[160,128]{1,0:T(8,128)S(1)}, u32[]{:S(2)}, u32[]{:S(2)}) collective-permute-start(f32[160,128]{1,0:T(8,128)S(1)} %copy-done.7), channel_id=1, source_target_pairs={{0,12},{1,13},{2,14},{3,15},{12,0},{13,1},{14,2},{15,3},{16,28},{1... | collective-permute-start | bytes 245768 | tf_op jit(solution)/shard_map/ppermute | solution.py:470
  36.1 9.0 %put_near_multiply_0.1 = (bf16[8,512,512]{2,1,0:T(8,128)(2,1)S(1)}, bf16[8,512,512]{2,1,0:T(8,128)(2,1)S(1)}, f32[32,128]{1,0:T(8,128)S(1)}, f32[512,4096]{1,0:T(8,128)}) custom-call(s32[1]{0:T(128)} %bitcast.refs_0_, s32[54,32]{1,0:T(8,128)S(1)} %get-tuple-element.30.refs_1_, ...), custom_call_target="tpu_custom_call", output_to_operand_aliasing={{0}: (10, {}), {1}: (11, {})} | custom-call | tf_op jit(solution)/shard_map/put_near_multiply_0/pallas_call | solution.py:81
  46.1 1.3 %collective-permute-start.10 = (f32[512,128]{1,0:T(8,128)S(1)}, f32[512,128]{1,0:T(8,128)S(1)}, u32[]{:S(2)}, u32[]{:S(2)}) collective-permute-start(f32[512,128]{1,0:T(8,128)S(1)} %get-tuple-element.47.refs_2_), channel_id=1, source_target_pairs={{4,0},{5,1},{6,2},{7,3},{8,12},{9,13},{10,14},{11,15},{20,16},{21,... | collective-permute-start | bytes 786440 | tf_op jit(solution)/shard_map/ppermute | solution.py:470
  47.4 0.9 %collective-permute-done.11.refs_6_ = f32[2272,128]{1,0:T(8,128)S(1)} collective-permute-done((f32[2272,128]{1,0:T(8,128)S(1)}, f32[2272,128]{1,0:T(8,128)S(1)}, u32[]{:S(2)}, u32[]{:S(2)}) %collective-permute-start.11) | collective-permute-done | bytes 1163296 | tf_op jit(solution)/shard_map/ppermute | solution.py:465
  48.2 7.7 %put_mid_multiply_1.1 = (bf16[8,512,512]{2,1,0:T(8,128)(2,1)S(1)}, bf16[8,512,512]{2,1,0:T(8,128)(2,1)S(1)}, f32[32,128]{1,0:T(8,128)S(1)}, f32[512,4096]{1,0:T(8,128)}) custom-call(s32[1]{0:T(128)} %bitcast.refs_0_, s32[54,32]{1,0:T(8,128)S(1)} %get-tuple-element.30.refs_1_, ...), custom_call_target="tpu_custom_call", output_to_operand_aliasing={{0}: (10, {}), {1}: (11, {}), {3}: (12, {})} | custom-call | tf_op jit(solution)/shard_map/put_mid_multiply_1/pallas_call | solution.py:81
  56.5 2.0 %collective-permute-done.12.refs_6_ = f32[1152,128]{1,0:T(8,128)S(1)} collective-permute-done((f32[1152,128]{1,0:T(8,128)S(1)}, f32[1152,128]{1,0:T(8,128)S(1)}, u32[]{:S(2)}, u32[]{:S(2)}) %collective-permute-start.12) | collective-permute-done | bytes 589856 | tf_op jit(solution)/shard_map/ppermute | solution.py:465
  58.5 7.5 %put_side_mid_multiply_2.1 = (bf16[8,512,512]{2,1,0:T(8,128)(2,1)S(1)}, bf16[8,512,512]{2,1,0:T(8,128)(2,1)S(1)}, f32[32,128]{1,0:T(8,128)}, f32[512,4096]{1,0:T(8,128)}) custom-call(s32[1]{0:T(128)} %bitcast.refs_0_, s32[54,32]{1,0:T(8,128)S(1)} %get-tuple-element.30.refs_1_, ...), custom_call_target="tpu_custom_call", output_to_operand_aliasing={{0}: (10, {}), {1}: (11, {}), {3}: (12, {})} | custom-call | tf_op jit(solution)/shard_map/put_side_mid_multiply_2/pallas_call | solution.py:81
  (30 shorter events, 3.0 us)
Async XLA Ops:
  0.6 10.8 %collective-permute-start = (f32[128,2048]{1,0:T(8,128)}, f32[128,2048]{1,0:T(8,128)S(1)}, u32[]{:S(2)}, u32[]{:S(2)}) collective-permute-start(f32[128,2048]{1,0:T(8,128)} %refs_5_.1), channel_id=1, source_target_pairs={{0,1},{1,0},{2,3},{3,2},{4,5},{5,4},{6,7},{7,6},{8,9},{9,8},{10,11... | collective-permute-start | bytes 3145736 | tf_op jit(solution)/shard_map/ppermute | solution.py:465
  1.1 1.2 %copy-start = (f32[128,2048]{1,0:T(8,128)S(1)}, f32[128,2048]{1,0:T(8,128)}, u32[]{:S(2)}) copy-start(f32[128,2048]{1,0:T(8,128)} %refs_5_.1) | copy-start | bytes 3145732
  3.7 22.8 %collective-permute-start.1 = (f32[1696,128]{1,0:T(8,128)}, f32[1696,128]{1,0:T(8,128)S(1)}, u32[]{:S(2)}, u32[]{:S(2)}) collective-permute-start(f32[1696,128]{1,0:T(8,128)} %get-tuple-element.33.refs_2_), channel_id=1, source_target_pairs={{0,4},{1,5},{2,6},{3,7},{4,0},{5,1},{6,2},{7,3},{8,12},{9,13},{10,... | collective-permute-start | bytes 2605064 | tf_op jit(solution)/shard_map/ppermute | solution.py:465
  6.4 18.8 %collective-permute-start.2 = (f32[1440,128]{1,0:T(8,128)}, f32[1440,128]{1,0:T(8,128)S(1)}, u32[]{:S(2)}, u32[]{:S(2)}) collective-permute-start(f32[1440,128]{1,0:T(8,128)} %get-tuple-element.34), channel_id=1, source_target_pairs={{0,2},{1,3},{2,0},{3,1},{4,6},{5,7},{6,4},{7,5},{8,10},{9,11},{10,... | collective-permute-start | bytes 2211848 | tf_op jit(solution)/shard_map/ppermute | solution.py:465
  7.9 1.2 %copy-start.3 = (f32[1696,128]{1,0:T(8,128)S(1)}, f32[1696,128]{1,0:T(8,128)}, u32[]{:S(2)}) copy-start(f32[1696,128]{1,0:T(8,128)} %get-tuple-element.33.refs_2_) | copy-start | bytes 2605060
  10.0 12.7 %collective-permute-start.3 = (f32[928,128]{1,0:T(8,128)}, f32[928,128]{1,0:T(8,128)S(1)}, u32[]{:S(2)}, u32[]{:S(2)}) collective-permute-start(f32[928,128]{1,0:T(8,128)} %get-tuple-element.35), channel_id=1, source_target_pairs={{4,8},{5,9},{6,10},{7,11},{8,4},{9,5},{10,6},{11,7},{20,24},{21,25... | collective-permute-start | bytes 1425416 | tf_op jit(solution)/shard_map/ppermute | solution.py:470
  11.4 0.7 copy-start.6
  15.8 3.4 %copy-start.2 = (f32[512,4096]{1,0:T(8,128)S(1)}, f32[512,4096]{1,0:T(8,128)}, u32[]{:S(2)}) copy-start(f32[512,4096]{1,0:T(8,128)} %refs_0_.1) | copy-start | bytes 25165828
  19.2 1.3 %copy-start.1 = (f32[128,2048]{1,0:T(8,128)S(1)}, f32[128,2048]{1,0:T(8,128)}, u32[]{:S(2)}) copy-start(f32[128,2048]{1,0:T(8,128)} %refs_5_.1) | copy-start | bytes 3145732
  19.2 1.3 %copy-start.5 = (s32[1,8]{1,0:T(1,128)S(1)}, s32[1,8]{1,0:T(1,128)}, u32[]{:S(2)}) copy-start(s32[1,8]{1,0:T(1,128)} %refs_4_.7) | copy-start | bytes 100
  22.6 7.9 %copy-start.7 = (f32[160,128]{1,0:T(8,128)S(1)}, f32[160,128]{1,0:T(8,128)}, u32[]{:S(2)}) copy-start(f32[160,128]{1,0:T(8,128)} %get-tuple-element.40) | copy-start | bytes 245764
  22.6 13.4 %copy-start.4 = (f32[4096]{0:T(1024)S(1)}, f32[4096]{0:T(1024)}, u32[]{:S(2)}) copy-start(f32[4096]{0:T(1024)} %param.10) | copy-start | bytes 49156
  26.7 9.3 %collective-permute-start.8 = (f32[3136,128]{1,0:T(8,128)S(1)}, f32[3136,128]{1,0:T(8,128)S(1)}, u32[]{:S(2)}, u32[]{:S(2)}) collective-permute-start(f32[3136,128]{1,0:T(8,128)S(1)} %get-tuple-element.42.refs_5_), channel_id=1, source_target_pairs={{0,1},{1,0},{2,3},{3,2},{4,5},{5,4},{6,7},{7,6},{8,9},{9,8},{10,11... | collective-permute-start | bytes 4816904 | tf_op jit(solution)/shard_map/ppermute | solution.py:465
  26.8 18.3 %collective-permute-start.7 = (f32[1184,128]{1,0:T(8,128)S(1)}, f32[1184,128]{1,0:T(8,128)S(1)}, u32[]{:S(2)}, u32[]{:S(2)}) collective-permute-start(f32[1184,128]{1,0:T(8,128)S(1)} %get-tuple-element.41), channel_id=1, source_target_pairs={{0,2},{1,3},{2,0},{3,1},{4,6},{5,7},{6,4},{7,5},{8,10},{9,11},{10,... | collective-permute-start | bytes 1818632 | tf_op jit(solution)/shard_map/ppermute | solution.py:465
  28.5 16.6 %collective-permute-start.4 = (f32[928,128]{1,0:T(8,128)S(1)}, f32[928,128]{1,0:T(8,128)S(1)}, u32[]{:S(2)}, u32[]{:S(2)}) collective-permute-start(f32[928,128]{1,0:T(8,128)S(1)} %get-tuple-element.38.refs_1_), channel_id=1, source_target_pairs={{4,0},{5,1},{6,2},{7,3},{8,12},{9,13},{10,14},{11,15},{20,16},{21,... | collective-permute-start | bytes 1425416 | tf_op jit(solution)/shard_map/ppermute | solution.py:470
  29.8 15.2 %collective-permute-start.5 = (f32[672,128]{1,0:T(8,128)S(1)}, f32[672,128]{1,0:T(8,128)S(1)}, u32[]{:S(2)}, u32[]{:S(2)}) collective-permute-start(f32[672,128]{1,0:T(8,128)S(1)} %get-tuple-element.39), channel_id=1, source_target_pairs={{4,8},{5,9},{6,10},{7,11},{8,4},{9,5},{10,6},{11,7},{20,24},{21,25... | collective-permute-start | bytes 1032200 | tf_op jit(solution)/shard_map/ppermute | solution.py:470
  30.5 14.5 %collective-permute-start.6 = (f32[160,128]{1,0:T(8,128)S(1)}, f32[160,128]{1,0:T(8,128)S(1)}, u32[]{:S(2)}, u32[]{:S(2)}) collective-permute-start(f32[160,128]{1,0:T(8,128)S(1)} %copy-done.7), channel_id=1, source_target_pairs={{0,12},{1,13},{2,14},{3,15},{12,0},{13,1},{14,2},{15,3},{16,28},{1... | collective-permute-start | bytes 245768 | tf_op jit(solution)/shard_map/ppermute | solution.py:470
  45.3 2.9 %collective-permute-start.11 = (f32[2272,128]{1,0:T(8,128)S(1)}, f32[2272,128]{1,0:T(8,128)S(1)}, u32[]{:S(2)}, u32[]{:S(2)}) collective-permute-start(f32[2272,128]{1,0:T(8,128)S(1)} %get-tuple-element.48.refs_5_), channel_id=1, source_target_pairs={{0,1},{1,0},{2,3},{3,2},{4,5},{5,4},{6,7},{7,6},{8,9},{9,8},{10,11... | collective-permute-start | bytes 3489800 | tf_op jit(solution)/shard_map/ppermute | solution.py:465
  45.4 10.9 %collective-permute-start.9 = (f32[640,128]{1,0:T(8,128)S(1)}, f32[640,128]{1,0:T(8,128)S(1)}, u32[]{:S(2)}, u32[]{:S(2)}) collective-permute-start(f32[640,128]{1,0:T(8,128)S(1)} %get-tuple-element.46), channel_id=1, source_target_pairs={{0,2},{1,3},{2,0},{3,1},{4,6},{5,7},{6,4},{7,5},{8,10},{9,11},{10,... | collective-permute-start | bytes 983048 | tf_op jit(solution)/shard_map/ppermute | solution.py:465
  46.1 10.3 %collective-permute-start.10 = (f32[512,128]{1,0:T(8,128)S(1)}, f32[512,128]{1,0:T(8,128)S(1)}, u32[]{:S(2)}, u32[]{:S(2)}) collective-permute-start(f32[512,128]{1,0:T(8,128)S(1)} %get-tuple-element.47.refs_2_), channel_id=1, source_target_pairs={{4,0},{5,1},{6,2},{7,3},{8,12},{9,13},{10,14},{11,15},{20,16},{21,... | collective-permute-start | bytes 786440 | tf_op jit(solution)/shard_map/ppermute | solution.py:470
  56.4 2.1 %collective-permute-start.12 = (f32[1152,128]{1,0:T(8,128)S(1)}, f32[1152,128]{1,0:T(8,128)S(1)}, u32[]{:S(2)}, u32[]{:S(2)}) collective-permute-start(f32[1152,128]{1,0:T(8,128)S(1)} %turn_3.1.refs_5_), channel_id=1, source_target_pairs={{0,1},{1,0},{2,3},{3,2},{4,5},{5,4},{6,7},{7,6},{8,9},{9,8},{10,11... | collective-permute-start | bytes 1769480 | tf_op jit(solution)/shard_map/ppermute | solution.py:465

commit v9 on v8

--- a/solution.py
+++ b/solution.py
@@ -259,8 +259,8 @@
         def list_of(other, sort):
             return (KINDS.index(name) * 2 + other) * 3 + sort
 
-        def diagonals():
-            lists = [list_of(other, 1) for other in range(2)]
+        def by_fours(sort):
+            lists = [list_of(other, sort) for other in range(2)]
             numbers = [count_ref[which] for which in lists]
             both = (numbers[0] > 0) & (numbers[1] > 0)
 
@@ -269,7 +269,7 @@
                     jobs = []
                     for k in chosen:
                         for at in (2 * i, 2 * i + 1):
-                            jobs.append((1, read(lists[k], 1, jnp.minimum(at, numbers[k] - 1))))
+                            jobs.append((sort, read(lists[k], sort, jnp.minimum(at, numbers[k] - 1))))
                     put_all(jobs)
                     return 0
 
@@ -281,25 +281,23 @@
                 lax.fori_loop(0, jnp.where(both, 0, lax.div(numbers[k] + 1, 2)), some((k,)), 0)
 
         if name != "far_rest":
-            diagonals()
-        for other in range(2):
-            for sort in (0, 2):
-                which = list_of(other, sort)
-                if sort == 2 and (other == 1 or name == "rows" or not PIECES[name][1]):
-                    continue
-                if sort == 0 and name != "rows" and not PIECES[name][2]:
-                    continue
-                number = count_ref[which]
-
-                def two(i, _):
-                    put_all([(sort, read(which, sort, 2 * i)), (sort, read(which, sort, 2 * i + 1))])
-                    return 0
-
-                lax.fori_loop(0, lax.div(number, 2), two, 0)
-
-                @pl.when(lax.rem(number, 2) == 1)
-                def _():
-                    put_all([(sort, read(which, sort, number - 1))])
+            by_fours(1)
+        if name == "rows" or PIECES[name][2]:
+            by_fours(0)
+        if name == "rows" or not PIECES[name][1]:
+            return
+        which = list_of(0, 2)
+        number = count_ref[which]
+
+        def two(i, _):
+            put_all([(2, read(which, 2, 2 * i)), (2, read(which, 2, 2 * i + 1))])
+            return 0
+
+        lax.fori_loop(0, lax.div(number, 2), two, 0)
+
+        @pl.when(lax.rem(number, 2) == 1)
+        def _():
+            put_all([(2, read(which, 2, number - 1))])
 
     at = 0
     for names in sets:
@@ -523,14 +521,14 @@
     copy_rows(rest_ref, 0, far_ref, far)
 
 
-def turn_3(inner, side_last_ref, rest_ref, rest_outer_ref, held_ref):
-    row = copy_rows(held_ref, 0, side_last_ref)
-
-    def take(ref):
-        copy_rows(held_ref, row, ref)
-
-    pl.when(inner)(lambda: take(rest_ref))
-    pl.when(jnp.logical_not(inner))(lambda: take(rest_outer_ref))
+def turn_3(inner, rest_ref, rest_outer_ref, held_ref):
+    pl.when(inner)(lambda: copy_rows(held_ref, 0, rest_ref) and None)
+    pl.when(jnp.logical_not(inner))(lambda: copy_rows(held_ref, 0, rest_outer_ref) and None)
+
+
+def hold(value, after):
+    out = pltpu.VMEM(value.shape, value.dtype)
+    return call(lambda *refs: None, "hold", [("vmem", value)], out, VMEM, after, input_output_aliases={0: 0})
 
 
 def planned(sep_inv, factor, widths, patterns, dinv):
@@ -556,8 +554,10 @@
 
     side_last, rest_outer = swap(part, 2), move(rest, outward)
     *blocks, marg, out = do(blocks, ROUNDS[1:2], (held, swap(held, 1)), 1, factors, marg, (out,))
-    (held,) = turn("turn_3", turn_3, me, (side_last, rest, rest_outer), (piece_rows(*ROUNDS[2]),), (), (marg,))
-    *_, marg, out = do(blocks, ROUNDS[2:], (held, swap(held, 1)), 2, factors, marg, (out,), last=True)
+    side_last = hold(side_last, (marg,))
+    (rest,) = turn("turn_3", turn_3, me, (rest, rest_outer), (piece_rows("far_rest"),), (), (marg, side_last))
+    sets, sources = (ROUNDS[2][:2], ROUNDS[2][2:]), (side_last, swap(side_last, 1), rest, swap(rest, 1))
+    *_, marg, out = do(blocks, sets, sources, 2, factors, marg, (out,), last=True)
     return out, marg
 
 

time: 66.5 us -> 66 us (level)
  Pallas kernels: 33.9 us -> 32.5 us
  waiting for transfers between devices: 7.25 us -> 7.97 us
    pallas_call x11 -> x12, Pallas kernels: 33.9 us -> 32.5 us  [call(): pl.pallas_call(body, out_shape=out_shape, in_specs=[pl.BlockSpec(memory_s...]
    ppermute x5, waiting for transfers between devices: 0.5 us -> 1.23 us  [move(): return lax.ppermute(value, 'pr', pairs)]
    ppermute x8 -> x9, starting transfers between devices: 7.33 us -> 7.35 us  [swap(): return lax.ppermute(value, 'pr', [(i, i ^ mask) for i in range(DEVICES)])]
    ppermute x8 -> x9, waiting for transfers between devices: 6.75 us -> 6.74 us  [swap(): return lax.ppermute(value, 'pr', [(i, i ^ mask) for i in range(DEVICES)])]
  transfers between devices with their start and end apart: 13 -> 14, of which waited for: 5 -> 6; matrix products, arithmetic and copies ran while one was open for 1% -> 1% of each run, Pallas kernels for 39% -> 37%
where the time goes in v9:
time: 66 us; the launch traced here: 65.5 us
  Pallas kernels  32.5 us (49%)
  starting transfers between devices  16.8 us (25%)
  waiting for transfers between devices  7.97 us (12%)
  local copies, waits for them, and re-layouts  7.19 us (11%)
  between operations  1.07 us (2%)
    pallas_call x12, Pallas kernels, call(): pl.pallas_call(body, out_shape=out_shape, in_specs=[pl.BlockSpec(memory_s...  32.5 us
    ppermute x5, starting transfers between devices, move(): return lax.ppermute(value, 'pr', pairs)  9.44 us
    ppermute x9, starting transfers between devices, swap(): return lax.ppermute(value, 'pr', [(i, i ^ mask) for i in range(DEVICES)])  7.35 us
    unnamed x17, local copies, waits for them, and re-layouts  7.19 us
    ppermute x9, waiting for transfers between devices, swap(): return lax.ppermute(value, 'pr', [(i, i ^ mask) for i in range(DEVICES)])  6.74 us
  transfers between devices with their start and end apart: 14, of which 6 were waited for; matrix products, arithmetic and copies ran while one was open for 1% of the time, Pallas kernels for 37%

profile of v9, /device:TPU:0, one launch (start us, length us, event | category | flops | bytes accessed | tf_op | source)
XLA Modules:
  0.0 65.5 jit_solution(16329830426258250782)
XLA Ops:
  1.1 1.2 %copy-done = f32[128,2048]{1,0:T(8,128)S(1)} copy-done((f32[128,2048]{1,0:T(8,128)S(1)}, f32[128,2048]{1,0:T(8,128)}, u32[]{:S(2)}) %copy-start) | copy-done | bytes 1048600
  2.4 1.4 %pack_near.1 = (f32[1696,128]{1,0:T(8,128)}, f32[1440,128]{1,0:T(8,128)}) custom-call(s32[1]{0:T(128)} %bitcast.refs_0_, f32[128,2048]{1,0:T(8,128)S(1)} %copy-done), custom_call_target="tpu_custom_call" | custom-call | tf_op jit(solution)/shard_map/pack_near/pallas_call | solution.py:81
  3.7 2.7 %collective-permute-start.1 = (f32[1696,128]{1,0:T(8,128)}, f32[1696,128]{1,0:T(8,128)S(1)}, u32[]{:S(2)}, u32[]{:S(2)}) collective-permute-start(f32[1696,128]{1,0:T(8,128)} %get-tuple-element.33.refs_2_), channel_id=1, source_target_pairs={{0,4},{1,5},{2,6},{3,7},{4,0},{5,1},{6,2},{7,3},{8,12},{9,13},{10,... | collective-permute-start | bytes 2605064 | tf_op jit(solution)/shard_map/ppermute | solution.py:463
  6.4 1.5 %collective-permute-start.2 = (f32[1440,128]{1,0:T(8,128)}, f32[1440,128]{1,0:T(8,128)S(1)}, u32[]{:S(2)}, u32[]{:S(2)}) collective-permute-start(f32[1440,128]{1,0:T(8,128)} %get-tuple-element.34), channel_id=1, source_target_pairs={{0,2},{1,3},{2,0},{3,1},{4,6},{5,7},{6,4},{7,5},{8,10},{9,11},{10,... | collective-permute-start | bytes 2211848 | tf_op jit(solution)/shard_map/ppermute | solution.py:463
  7.9 1.2 %copy-done.3 = f32[1696,128]{1,0:T(8,128)S(1)} copy-done((f32[1696,128]{1,0:T(8,128)S(1)}, f32[1696,128]{1,0:T(8,128)}, u32[]{:S(2)}) %copy-start.3) | copy-done | bytes 868376
  9.1 0.9 %pack_mid.1 = (f32[928,128]{1,0:T(8,128)}, f32[160,128]{1,0:T(8,128)}) custom-call(s32[1]{0:T(128)} %bitcast.refs_0_, f32[128,2048]{1,0:T(8,128)S(1)} %copy-done, f32[1696,128]{1,0:T(8,128)S(1)} %copy-done.3), custom_call_target="tpu_custom_call" | custom-call | tf_op jit(solution)/shard_map/pack_mid/pallas_call | solution.py:81
  10.0 0.7 %collective-permute-start.3 = (f32[928,128]{1,0:T(8,128)}, f32[928,128]{1,0:T(8,128)S(1)}, u32[]{:S(2)}, u32[]{:S(2)}) collective-permute-start(f32[928,128]{1,0:T(8,128)} %get-tuple-element.35), channel_id=1, source_target_pairs={{4,8},{5,9},{6,10},{7,11},{8,4},{9,5},{10,6},{11,7},{20,24},{21,25... | collective-permute-start | bytes 1425416 | tf_op jit(solution)/shard_map/ppermute | solution.py:468
  10.7 0.8 %copy.18.refs_2_ = s32[8,4]{1,0:T(8,128)S(1)} copy(s32[8,4]{0,1:T(4,128)} %param.9) | data formatting | bytes 256 | tf_op args[3]
  12.1 3.7 %plan_jobs.1 = (s32[54,32]{1,0:T(8,128)S(1)}, s32[54]{0:T(128)S(1)}, s32[5,32]{1,0:T(8,128)S(1)}) custom-call(s32[1]{0:T(128)} %bitcast.refs_0_, s32[64]{0:T(128)S(1)} %copy-done.6, s32[8,4]{1,0:T(8,128)S(1)} %copy.18.refs_2_, f32[128,2048]{1,0:T(8,128)S(1)} %collective-permute-done.refs_3_.refs_6_), custom_call_target="tpu_custom_call" | custom-call | tf_op jit(solution)/shard_map/plan_jobs/pallas_call | solution.py:81
  15.8 3.4 %copy-done.2 = f32[512,4096]{1,0:T(8,128)S(1)} copy-done((f32[512,4096]{1,0:T(8,128)S(1)}, f32[512,4096]{1,0:T(8,128)}, u32[]{:S(2)}) %copy-start.2) | copy-done | bytes 8388632
  19.2 1.3 %factor_halves.1 = (bf16[512,4096]{1,0:T(8,128)(2,1)S(1)}, bf16[512,4096]{1,0:T(8,128)(2,1)S(1)}) custom-call(f32[512,4096]{1,0:T(8,128)S(1)} %copy-done.2, s32[54]{0:T(128)S(1)} %get-tuple-element.31.refs_1_.refs_2_), custom_call_target="tpu_custom_call" | custom-call | tf_op jit(solution)/shard_map/factor_halves/pallas_call | solution.py:81
  20.5 1.8 %put_rows.1 = (bf16[8,512,512]{2,1,0:T(8,128)(2,1)S(1)}, bf16[8,512,512]{2,1,0:T(8,128)(2,1)S(1)}) custom-call(s32[1]{0:T(128)} %bitcast.refs_0_, s32[54,32]{1,0:T(8,128)S(1)} %get-tuple-element.30.refs_1_, s32[54]{0:T(128)S(1)} %get-tuple-element.31.refs_1_.refs_2_, s32[5,32]{1,0:T(8,128)S(1)} %get-tuple-element.32.refs_3_, s32[1,8]{1,0:T(1,128)S(1)} %copy-done.5, ...), custom_call_target="tpu_custom_call" | custom-call | tf_op jit(solution)/shard_map/put_rows/pallas_call | solution.py:81
  22.4 2.8 %collective-permute-done.2.refs_2_ = f32[1440,128]{1,0:T(8,128)S(1)} collective-permute-done((f32[1440,128]{1,0:T(8,128)}, f32[1440,128]{1,0:T(8,128)S(1)}, u32[]{:S(2)}, u32[]{:S(2)}) %collective-permute-start.2) | collective-permute-done | bytes 737312 | tf_op jit(solution)/shard_map/ppermute | solution.py:463
  25.2 1.3 %collective-permute-done.1.refs_1_ = f32[1696,128]{1,0:T(8,128)S(1)} collective-permute-done((f32[1696,128]{1,0:T(8,128)}, f32[1696,128]{1,0:T(8,128)S(1)}, u32[]{:S(2)}, u32[]{:S(2)}) %collective-permute-start.1) | collective-permute-done | bytes 868384 | tf_op jit(solution)/shard_map/ppermute | solution.py:463
  26.8 1.7 %collective-permute-start.7 = (f32[1184,128]{1,0:T(8,128)S(1)}, f32[1184,128]{1,0:T(8,128)S(1)}, u32[]{:S(2)}, u32[]{:S(2)}) collective-permute-start(f32[1184,128]{1,0:T(8,128)S(1)} %get-tuple-element.41), channel_id=1, source_target_pairs={{0,2},{1,3},{2,0},{3,1},{4,6},{5,7},{6,4},{7,5},{8,10},{9,11},{10,... | collective-permute-start | bytes 1818632 | tf_op jit(solution)/shard_map/ppermute | solution.py:463
  28.6 1.3 %collective-permute-start.4 = (f32[928,128]{1,0:T(8,128)S(1)}, f32[928,128]{1,0:T(8,128)S(1)}, u32[]{:S(2)}, u32[]{:S(2)}) collective-permute-start(f32[928,128]{1,0:T(8,128)S(1)} %get-tuple-element.38.refs_1_), channel_id=1, source_target_pairs={{4,0},{5,1},{6,2},{7,3},{8,12},{9,13},{10,14},{11,15},{20,16},{21,... | collective-permute-start | bytes 1425416 | tf_op jit(solution)/shard_map/ppermute | solution.py:468
  30.5 5.5 %collective-permute-start.6 = (f32[160,128]{1,0:T(8,128)S(1)}, f32[160,128]{1,0:T(8,128)S(1)}, u32[]{:S(2)}, u32[]{:S(2)}) collective-permute-start(f32[160,128]{1,0:T(8,128)S(1)} %copy-done.7), channel_id=1, source_target_pairs={{0,12},{1,13},{2,14},{3,15},{12,0},{13,1},{14,2},{15,3},{16,28},{1... | collective-permute-start | bytes 245768 | tf_op jit(solution)/shard_map/ppermute | solution.py:468
  36.1 8.1 %put_near_multiply_0.1 = (bf16[8,512,512]{2,1,0:T(8,128)(2,1)S(1)}, bf16[8,512,512]{2,1,0:T(8,128)(2,1)S(1)}, f32[32,128]{1,0:T(8,128)S(1)}, f32[512,4096]{1,0:T(8,128)}) custom-call(s32[1]{0:T(128)} %bitcast.refs_0_, s32[54,32]{1,0:T(8,128)S(1)} %get-tuple-element.30.refs_1_, ...), custom_call_target="tpu_custom_call", output_to_operand_aliasing={{0}: (10, {}), {1}: (11, {})} | custom-call | tf_op jit(solution)/shard_map/put_near_multiply_0/pallas_call | solution.py:81
  44.2 0.9 %collective-permute-done.4.refs_2_ = f32[928,128]{1,0:T(8,128)S(1)} collective-permute-done((f32[928,128]{1,0:T(8,128)S(1)}, f32[928,128]{1,0:T(8,128)S(1)}, u32[]{:S(2)}, u32[]{:S(2)}) %collective-permute-start.4) | collective-permute-done | bytes 475168 | tf_op jit(solution)/shard_map/ppermute | solution.py:468
  45.8 1.3 %collective-permute-start.12 = (f32[512,128]{1,0:T(8,128)S(1)}, f32[512,128]{1,0:T(8,128)S(1)}, u32[]{:S(2)}, u32[]{:S(2)}) collective-permute-start(f32[512,128]{1,0:T(8,128)S(1)} %get-tuple-element.52.refs_1_), channel_id=1, source_target_pairs={{4,0},{5,1},{6,2},{7,3},{8,12},{9,13},{10,14},{11,15},{20,16},{21,... | collective-permute-start | bytes 786440 | tf_op jit(solution)/shard_map/ppermute | solution.py:468
  47.1 1.1 %collective-permute-done.10.refs_6_ = f32[2272,128]{1,0:T(8,128)S(1)} collective-permute-done((f32[2272,128]{1,0:T(8,128)S(1)}, f32[2272,128]{1,0:T(8,128)S(1)}, u32[]{:S(2)}, u32[]{:S(2)}) %collective-permute-start.10) | collective-permute-done | bytes 1163296 | tf_op jit(solution)/shard_map/ppermute | solution.py:463
  48.2 7.3 %put_mid_multiply_1.1 = (bf16[8,512,512]{2,1,0:T(8,128)(2,1)S(1)}, bf16[8,512,512]{2,1,0:T(8,128)(2,1)S(1)}, f32[32,128]{1,0:T(8,128)S(1)}, f32[512,4096]{1,0:T(8,128)}) custom-call(s32[1]{0:T(128)} %bitcast.refs_0_, s32[54,32]{1,0:T(8,128)S(1)} %get-tuple-element.30.refs_1_, ...), custom_call_target="tpu_custom_call", output_to_operand_aliasing={{0}: (10, {}), {1}: (11, {}), {3}: (12, {})} | custom-call | tf_op jit(solution)/shard_map/put_mid_multiply_1/pallas_call | solution.py:81
  56.2 1.5 %collective-permute-done.13.refs_8_ = f32[512,128]{1,0:T(8,128)S(1)} collective-permute-done((f32[512,128]{1,0:T(8,128)S(1)}, f32[512,128]{1,0:T(8,128)S(1)}, u32[]{:S(2)}, u32[]{:S(2)}) %collective-permute-start.13) | collective-permute-done | bytes 262176 | tf_op jit(solution)/shard_map/ppermute | solution.py:463
  57.7 7.6 %put_side_mid_multiply_2.1 = (bf16[8,512,512]{2,1,0:T(8,128)(2,1)S(1)}, bf16[8,512,512]{2,1,0:T(8,128)(2,1)S(1)}, f32[32,128]{1,0:T(8,128)}, f32[512,4096]{1,0:T(8,128)}) custom-call(s32[1]{0:T(128)} %bitcast.refs_0_, s32[54,32]{1,0:T(8,128)S(1)} %get-tuple-element.30.refs_1_, ...), custom_call_target="tpu_custom_call", output_to_operand_aliasing={{0}: (12, {}), {1}: (13, {}), {3}: (14, {})} | custom-call | tf_op jit(solution)/shard_map/put_side_mid_multiply_2/pallas_call | solution.py:81
  (33 shorter events, 3.5 us)
Async XLA Ops:
  0.6 10.8 %collective-permute-start = (f32[128,2048]{1,0:T(8,128)}, f32[128,2048]{1,0:T(8,128)S(1)}, u32[]{:S(2)}, u32[]{:S(2)}) collective-permute-start(f32[128,2048]{1,0:T(8,128)} %refs_5_.1), channel_id=1, source_target_pairs={{0,1},{1,0},{2,3},{3,2},{4,5},{5,4},{6,7},{7,6},{8,9},{9,8},{10,11... | collective-permute-start | bytes 3145736 | tf_op jit(solution)/shard_map/ppermute | solution.py:463
  1.1 1.2 %copy-start = (f32[128,2048]{1,0:T(8,128)S(1)}, f32[128,2048]{1,0:T(8,128)}, u32[]{:S(2)}) copy-start(f32[128,2048]{1,0:T(8,128)} %refs_5_.1) | copy-start | bytes 3145732
  3.7 22.8 %collective-permute-start.1 = (f32[1696,128]{1,0:T(8,128)}, f32[1696,128]{1,0:T(8,128)S(1)}, u32[]{:S(2)}, u32[]{:S(2)}) collective-permute-start(f32[1696,128]{1,0:T(8,128)} %get-tuple-element.33.refs_2_), channel_id=1, source_target_pairs={{0,4},{1,5},{2,6},{3,7},{4,0},{5,1},{6,2},{7,3},{8,12},{9,13},{10,... | collective-permute-start | bytes 2605064 | tf_op jit(solution)/shard_map/ppermute | solution.py:463
  6.4 18.8 %collective-permute-start.2 = (f32[1440,128]{1,0:T(8,128)}, f32[1440,128]{1,0:T(8,128)S(1)}, u32[]{:S(2)}, u32[]{:S(2)}) collective-permute-start(f32[1440,128]{1,0:T(8,128)} %get-tuple-element.34), channel_id=1, source_target_pairs={{0,2},{1,3},{2,0},{3,1},{4,6},{5,7},{6,4},{7,5},{8,10},{9,11},{10,... | collective-permute-start | bytes 2211848 | tf_op jit(solution)/shard_map/ppermute | solution.py:463
  7.9 1.2 %copy-start.3 = (f32[1696,128]{1,0:T(8,128)S(1)}, f32[1696,128]{1,0:T(8,128)}, u32[]{:S(2)}) copy-start(f32[1696,128]{1,0:T(8,128)} %get-tuple-element.33.refs_2_) | copy-start | bytes 2605060
  10.0 12.4 %collective-permute-start.3 = (f32[928,128]{1,0:T(8,128)}, f32[928,128]{1,0:T(8,128)S(1)}, u32[]{:S(2)}, u32[]{:S(2)}) collective-permute-start(f32[928,128]{1,0:T(8,128)} %get-tuple-element.35), channel_id=1, source_target_pairs={{4,8},{5,9},{6,10},{7,11},{8,4},{9,5},{10,6},{11,7},{20,24},{21,25... | collective-permute-start | bytes 1425416 | tf_op jit(solution)/shard_map/ppermute | solution.py:468
  11.5 0.7 %copy-start.6 = (s32[64]{0:T(128)S(1)}, s32[64]{0:T(128)}, u32[]{:S(2)}) copy-start(s32[64]{0:T(128)} %constant.6.clone.refs_1_) | copy-start | bytes 772
  15.8 3.4 %copy-start.2 = (f32[512,4096]{1,0:T(8,128)S(1)}, f32[512,4096]{1,0:T(8,128)}, u32[]{:S(2)}) copy-start(f32[512,4096]{1,0:T(8,128)} %refs_0_.1) | copy-start | bytes 25165828
  19.2 1.3 %copy-start.1 = (f32[128,2048]{1,0:T(8,128)S(1)}, f32[128,2048]{1,0:T(8,128)}, u32[]{:S(2)}) copy-start(f32[128,2048]{1,0:T(8,128)} %refs_5_.1) | copy-start | bytes 3145732
  19.2 1.3 %copy-start.5 = (s32[1,8]{1,0:T(1,128)S(1)}, s32[1,8]{1,0:T(1,128)}, u32[]{:S(2)}) copy-start(s32[1,8]{1,0:T(1,128)} %refs_4_.7) | copy-start | bytes 100
  22.4 8.1 %copy-start.7 = (f32[160,128]{1,0:T(8,128)S(1)}, f32[160,128]{1,0:T(8,128)}, u32[]{:S(2)}) copy-start(f32[160,128]{1,0:T(8,128)} %get-tuple-element.40) | copy-start | bytes 245764
  22.4 13.7 %copy-start.4 = (f32[4096]{0:T(1024)S(1)}, f32[4096]{0:T(1024)}, u32[]{:S(2)}) copy-start(f32[4096]{0:T(1024)} %param.10) | copy-start | bytes 49156
  26.7 9.3 %collective-permute-start.8 = (f32[3136,128]{1,0:T(8,128)S(1)}, f32[3136,128]{1,0:T(8,128)S(1)}, u32[]{:S(2)}, u32[]{:S(2)}) collective-permute-start(f32[3136,128]{1,0:T(8,128)S(1)} %get-tuple-element.42.refs_5_), channel_id=1, source_target_pairs={{0,1},{1,0},{2,3},{3,2},{4,5},{5,4},{6,7},{7,6},{8,9},{9,8},{10,11... | collective-permute-start | bytes 4816904 | tf_op jit(solution)/shard_map/ppermute | solution.py:463
  26.8 18.3 %collective-permute-start.7 = (f32[1184,128]{1,0:T(8,128)S(1)}, f32[1184,128]{1,0:T(8,128)S(1)}, u32[]{:S(2)}, u32[]{:S(2)}) collective-permute-start(f32[1184,128]{1,0:T(8,128)S(1)} %get-tuple-element.41), channel_id=1, source_target_pairs={{0,2},{1,3},{2,0},{3,1},{4,6},{5,7},{6,4},{7,5},{8,10},{9,11},{10,... | collective-permute-start | bytes 1818632 | tf_op jit(solution)/shard_map/ppermute | solution.py:463
  28.6 16.6 %collective-permute-start.4 = (f32[928,128]{1,0:T(8,128)S(1)}, f32[928,128]{1,0:T(8,128)S(1)}, u32[]{:S(2)}, u32[]{:S(2)}) collective-permute-start(f32[928,128]{1,0:T(8,128)S(1)} %get-tuple-element.38.refs_1_), channel_id=1, source_target_pairs={{4,0},{5,1},{6,2},{7,3},{8,12},{9,13},{10,14},{11,15},{20,16},{21,... | collective-permute-start | bytes 1425416 | tf_op jit(solution)/shard_map/ppermute | solution.py:468
  29.8 14.3 %collective-permute-start.5 = (f32[672,128]{1,0:T(8,128)S(1)}, f32[672,128]{1,0:T(8,128)S(1)}, u32[]{:S(2)}, u32[]{:S(2)}) collective-permute-start(f32[672,128]{1,0:T(8,128)S(1)} %get-tuple-element.39), channel_id=1, source_target_pairs={{4,8},{5,9},{6,10},{7,11},{8,4},{9,5},{10,6},{11,7},{20,24},{21,25... | collective-permute-start | bytes 1032200 | tf_op jit(solution)/shard_map/ppermute | solution.py:468
  30.5 13.6 %collective-permute-start.6 = (f32[160,128]{1,0:T(8,128)S(1)}, f32[160,128]{1,0:T(8,128)S(1)}, u32[]{:S(2)}, u32[]{:S(2)}) collective-permute-start(f32[160,128]{1,0:T(8,128)S(1)} %copy-done.7), channel_id=1, source_target_pairs={{0,12},{1,13},{2,14},{3,15},{12,0},{13,1},{14,2},{15,3},{16,28},{1... | collective-permute-start | bytes 245768 | tf_op jit(solution)/shard_map/ppermute | solution.py:468
  45.4 2.9 %collective-permute-start.10 = (f32[2272,128]{1,0:T(8,128)S(1)}, f32[2272,128]{1,0:T(8,128)S(1)}, u32[]{:S(2)}, u32[]{:S(2)}) collective-permute-start(f32[2272,128]{1,0:T(8,128)S(1)} %get-tuple-element.47.refs_5_), channel_id=1, source_target_pairs={{0,1},{1,0},{2,3},{3,2},{4,5},{5,4},{6,7},{7,6},{8,9},{9,8},{10,11... | collective-permute-start | bytes 3489800 | tf_op jit(solution)/shard_map/ppermute | solution.py:463
  45.4 10.1 %collective-permute-start.9 = (f32[640,128]{1,0:T(8,128)S(1)}, f32[640,128]{1,0:T(8,128)S(1)}, u32[]{:S(2)}, u32[]{:S(2)}) collective-permute-start(f32[640,128]{1,0:T(8,128)S(1)} %get-tuple-element.46), channel_id=1, source_target_pairs={{0,2},{1,3},{2,0},{3,1},{4,6},{5,7},{6,4},{7,5},{8,10},{9,11},{10,... | collective-permute-start | bytes 983048 | tf_op jit(solution)/shard_map/ppermute | solution.py:463
  45.8 10.3 %collective-permute-start.12 = (f32[512,128]{1,0:T(8,128)S(1)}, f32[512,128]{1,0:T(8,128)S(1)}, u32[]{:S(2)}, u32[]{:S(2)}) collective-permute-start(f32[512,128]{1,0:T(8,128)S(1)} %get-tuple-element.52.refs_1_), channel_id=1, source_target_pairs={{4,0},{5,1},{6,2},{7,3},{8,12},{9,13},{10,14},{11,15},{20,16},{21,... | collective-permute-start | bytes 786440 | tf_op jit(solution)/shard_map/ppermute | solution.py:468
  55.6 2.1 %collective-permute-start.11 = (f32[640,128]{1,0:T(8,128)S(1)}, f32[640,128]{1,0:T(8,128)S(1)}, u32[]{:S(2)}, u32[]{:S(2)}) collective-permute-start(f32[640,128]{1,0:T(8,128)S(1)} %hold.1.refs_4_.refs_5_), channel_id=1, source_target_pairs={{0,1},{1,0},{2,3},{3,2},{4,5},{5,4},{6,7},{7,6},{8,9},{9,8},{10,11... | collective-permute-start | bytes 983048 | tf_op jit(solution)/shard_map/ppermute | solution.py:463
  56.1 1.6 %collective-permute-start.13 = (f32[512,128]{1,0:T(8,128)S(1)}, f32[512,128]{1,0:T(8,128)S(1)}, u32[]{:S(2)}, u32[]{:S(2)}) collective-permute-start(f32[512,128]{1,0:T(8,128)S(1)} %turn_3.1.refs_7_), channel_id=1, source_target_pairs={{0,1},{1,0},{2,3},{3,2},{4,5},{5,4},{6,7},{7,6},{8,9},{9,8},{10,11... | collective-permute-start | bytes 786440 | tf_op jit(solution)/shard_map/ppermute | solution.py:463

commit v10 on v9

--- a/solution.py
+++ b/solution.py
@@ -536,7 +536,7 @@
     between_inner, between_outer, outward = {1: 2, 2: 1}, {0: 3, 3: 0}, {1: 0, 2: 3}
 
     near, side = pack((("near",), ("side",)), me, sep_inv)
-    mid, first = pack((("mid",), ("far",)), me, sep_inv, (near,))
+    mid, first = pack((("mid",), ("far",)), me, sep_inv, (side,))
     rows_other = swap(sep_inv, 1)
     near, side, mid = swap(near, 4), swap(side, 2), move(mid, between_inner)
     plan = plan_jobs(me, patterns, (rows_other,))

time: 66 us -> 66 us (level)
  no operation moved by 1% of the time
where the time goes in v10:
time: 66 us; the launch traced here: 65.6 us
  Pallas kernels  32.4 us (49%)
  starting transfers between devices  16.7 us (25%)
  waiting for transfers between devices  8.26 us (13%)
  local copies, waits for them, and re-layouts  7.18 us (11%)
  between operations  1.06 us (2%)
    pallas_call x12, Pallas kernels, call(): pl.pallas_call(body, out_shape=out_shape, in_specs=[pl.BlockSpec(memory_s...  32.4 us
    ppermute x5, starting transfers between devices, move(): return lax.ppermute(value, 'pr', pairs)  9.44 us
    ppermute x9, starting transfers between devices, swap(): return lax.ppermute(value, 'pr', [(i, i ^ mask) for i in range(DEVICES)])  7.26 us
    unnamed x17, local copies, waits for them, and re-layouts  7.18 us
    ppermute x9, waiting for transfers between devices, swap(): return lax.ppermute(value, 'pr', [(i, i ^ mask) for i in range(DEVICES)])  6.81 us
    ppermute x5, waiting for transfers between devices, move(): return lax.ppermute(value, 'pr', pairs)  1.45 us
  transfers between devices with their start and end apart: 14, of which 6 were waited for; matrix products, arithmetic and copies ran while one was open for 1% of the time, Pallas kernels for 37%

profile of v10, /device:TPU:0, one launch (start us, length us, event | category | flops | bytes accessed | tf_op | source)
XLA Modules:
  0.0 65.6 jit_solution(5928262810822240192)
XLA Ops:
  1.1 1.2 %copy-done = f32[128,2048]{1,0:T(8,128)S(1)} copy-done((f32[128,2048]{1,0:T(8,128)S(1)}, f32[128,2048]{1,0:T(8,128)}, u32[]{:S(2)}) %copy-start) | copy-done | bytes 1048600
  2.4 1.4 %pack_near.1 = (f32[1696,128]{1,0:T(8,128)}, f32[1440,128]{1,0:T(8,128)}) custom-call(s32[1]{0:T(128)} %bitcast.refs_0_, f32[128,2048]{1,0:T(8,128)S(1)} %copy-done), custom_call_target="tpu_custom_call" | custom-call | tf_op jit(solution)/shard_map/pack_near/pallas_call | solution.py:81
  3.7 2.7 %collective-permute-start.1 = (f32[1696,128]{1,0:T(8,128)}, f32[1696,128]{1,0:T(8,128)S(1)}, u32[]{:S(2)}, u32[]{:S(2)}) collective-permute-start(f32[1696,128]{1,0:T(8,128)} %get-tuple-element.33), channel_id=1, source_target_pairs={{0,4},{1,5},{2,6},{3,7},{4,0},{5,1},{6,2},{7,3},{8,12},{9,13},{10,... | collective-permute-start | bytes 2605064 | tf_op jit(solution)/shard_map/ppermute | solution.py:463
  6.4 1.5 %collective-permute-start.2 = (f32[1440,128]{1,0:T(8,128)}, f32[1440,128]{1,0:T(8,128)S(1)}, u32[]{:S(2)}, u32[]{:S(2)}) collective-permute-start(f32[1440,128]{1,0:T(8,128)} %get-tuple-element.34.refs_2_), channel_id=1, source_target_pairs={{0,2},{1,3},{2,0},{3,1},{4,6},{5,7},{6,4},{7,5},{8,10},{9,11},{10,... | collective-permute-start | bytes 2211848 | tf_op jit(solution)/shard_map/ppermute | solution.py:463
  7.9 1.1 %copy-done.3 = f32[1440,128]{1,0:T(8,128)S(1)} copy-done((f32[1440,128]{1,0:T(8,128)S(1)}, f32[1440,128]{1,0:T(8,128)}, u32[]{:S(2)}) %copy-start.3) | copy-done | bytes 737304
  9.1 0.9 %pack_mid.1 = (f32[928,128]{1,0:T(8,128)}, f32[160,128]{1,0:T(8,128)}) custom-call(s32[1]{0:T(128)} %bitcast.refs_0_, f32[128,2048]{1,0:T(8,128)S(1)} %copy-done, f32[1440,128]{1,0:T(8,128)S(1)} %copy-done.3), custom_call_target="tpu_custom_call" | custom-call | tf_op jit(solution)/shard_map/pack_mid/pallas_call | solution.py:81
  10.0 0.7 %collective-permute-start.3 = (f32[928,128]{1,0:T(8,128)}, f32[928,128]{1,0:T(8,128)S(1)}, u32[]{:S(2)}, u32[]{:S(2)}) collective-permute-start(f32[928,128]{1,0:T(8,128)} %get-tuple-element.35), channel_id=1, source_target_pairs={{4,8},{5,9},{6,10},{7,11},{8,4},{9,5},{10,6},{11,7},{20,24},{21,25... | collective-permute-start | bytes 1425416 | tf_op jit(solution)/shard_map/ppermute | solution.py:468
  10.7 0.8 %copy.18.refs_2_ = s32[8,4]{1,0:T(8,128)S(1)} copy(s32[8,4]{0,1:T(4,128)} %param.9) | data formatting | bytes 256 | tf_op args[3]
  12.1 3.7 %plan_jobs.1 = (s32[54,32]{1,0:T(8,128)S(1)}, s32[54]{0:T(128)S(1)}, s32[5,32]{1,0:T(8,128)S(1)}) custom-call(s32[1]{0:T(128)} %bitcast.refs_0_, s32[64]{0:T(128)S(1)} %copy-done.6, s32[8,4]{1,0:T(8,128)S(1)} %copy.18.refs_2_, f32[128,2048]{1,0:T(8,128)S(1)} %collective-permute-done.refs_3_.refs_6_), custom_call_target="tpu_custom_call" | custom-call | tf_op jit(solution)/shard_map/plan_jobs/pallas_call | solution.py:81
  15.8 3.4 %copy-done.2 = f32[512,4096]{1,0:T(8,128)S(1)} copy-done((f32[512,4096]{1,0:T(8,128)S(1)}, f32[512,4096]{1,0:T(8,128)}, u32[]{:S(2)}) %copy-start.2) | copy-done | bytes 8388632
  19.2 1.3 %factor_halves.1 = (bf16[512,4096]{1,0:T(8,128)(2,1)S(1)}, bf16[512,4096]{1,0:T(8,128)(2,1)S(1)}) custom-call(f32[512,4096]{1,0:T(8,128)S(1)} %copy-done.2, s32[54]{0:T(128)S(1)} %get-tuple-element.31.refs_1_.refs_2_), custom_call_target="tpu_custom_call" | custom-call | tf_op jit(solution)/shard_map/factor_halves/pallas_call | solution.py:81
  20.5 1.8 %put_rows.1 = (bf16[8,512,512]{2,1,0:T(8,128)(2,1)S(1)}, bf16[8,512,512]{2,1,0:T(8,128)(2,1)S(1)}) custom-call(s32[1]{0:T(128)} %bitcast.refs_0_, s32[54,32]{1,0:T(8,128)S(1)} %get-tuple-element.30.refs_1_, s32[54]{0:T(128)S(1)} %get-tuple-element.31.refs_1_.refs_2_, s32[5,32]{1,0:T(8,128)S(1)} %get-tuple-element.32.refs_3_, s32[1,8]{1,0:T(1,128)S(1)} %copy-done.5, ...), custom_call_target="tpu_custom_call" | custom-call | tf_op jit(solution)/shard_map/put_rows/pallas_call | solution.py:81
  22.4 2.8 %collective-permute-done.2.refs_2_ = f32[1440,128]{1,0:T(8,128)S(1)} collective-permute-done((f32[1440,128]{1,0:T(8,128)}, f32[1440,128]{1,0:T(8,128)S(1)}, u32[]{:S(2)}, u32[]{:S(2)}) %collective-permute-start.2) | collective-permute-done | bytes 737312 | tf_op jit(solution)/shard_map/ppermute | solution.py:463
  25.2 1.3 %collective-permute-done.1.refs_1_ = f32[1696,128]{1,0:T(8,128)S(1)} collective-permute-done((f32[1696,128]{1,0:T(8,128)}, f32[1696,128]{1,0:T(8,128)S(1)}, u32[]{:S(2)}, u32[]{:S(2)}) %collective-permute-start.1) | collective-permute-done | bytes 868384 | tf_op jit(solution)/shard_map/ppermute | solution.py:463
  26.8 1.7 %collective-permute-start.7 = (f32[1184,128]{1,0:T(8,128)S(1)}, f32[1184,128]{1,0:T(8,128)S(1)}, u32[]{:S(2)}, u32[]{:S(2)}) collective-permute-start(f32[1184,128]{1,0:T(8,128)S(1)} %get-tuple-element.41), channel_id=1, source_target_pairs={{0,2},{1,3},{2,0},{3,1},{4,6},{5,7},{6,4},{7,5},{8,10},{9,11},{10,... | collective-permute-start | bytes 1818632 | tf_op jit(solution)/shard_map/ppermute | solution.py:463
  28.6 1.3 %collective-permute-start.4 = (f32[928,128]{1,0:T(8,128)S(1)}, f32[928,128]{1,0:T(8,128)S(1)}, u32[]{:S(2)}, u32[]{:S(2)}) collective-permute-start(f32[928,128]{1,0:T(8,128)S(1)} %get-tuple-element.38.refs_1_), channel_id=1, source_target_pairs={{4,0},{5,1},{6,2},{7,3},{8,12},{9,13},{10,14},{11,15},{20,16},{21,... | collective-permute-start | bytes 1425416 | tf_op jit(solution)/shard_map/ppermute | solution.py:468
  30.5 5.5 %collective-permute-start.6 = (f32[160,128]{1,0:T(8,128)S(1)}, f32[160,128]{1,0:T(8,128)S(1)}, u32[]{:S(2)}, u32[]{:S(2)}) collective-permute-start(f32[160,128]{1,0:T(8,128)S(1)} %copy-done.7), channel_id=1, source_target_pairs={{0,12},{1,13},{2,14},{3,15},{12,0},{13,1},{14,2},{15,3},{16,28},{1... | collective-permute-start | bytes 245768 | tf_op jit(solution)/shard_map/ppermute | solution.py:468
  36.1 7.9 %put_near_multiply_0.1 = (bf16[8,512,512]{2,1,0:T(8,128)(2,1)S(1)}, bf16[8,512,512]{2,1,0:T(8,128)(2,1)S(1)}, f32[32,128]{1,0:T(8,128)S(1)}, f32[512,4096]{1,0:T(8,128)}) custom-call(s32[1]{0:T(128)} %bitcast.refs_0_, s32[54,32]{1,0:T(8,128)S(1)} %get-tuple-element.30.refs_1_, ...), custom_call_target="tpu_custom_call", output_to_operand_aliasing={{0}: (10, {}), {1}: (11, {})} | custom-call | tf_op jit(solution)/shard_map/put_near_multiply_0/pallas_call | solution.py:81
  44.1 1.1 %collective-permute-done.4.refs_2_ = f32[928,128]{1,0:T(8,128)S(1)} collective-permute-done((f32[928,128]{1,0:T(8,128)S(1)}, f32[928,128]{1,0:T(8,128)S(1)}, u32[]{:S(2)}, u32[]{:S(2)}) %collective-permute-start.4) | collective-permute-done | bytes 475168 | tf_op jit(solution)/shard_map/ppermute | solution.py:468
  45.8 1.3 %collective-permute-start.12 = (f32[512,128]{1,0:T(8,128)S(1)}, f32[512,128]{1,0:T(8,128)S(1)}, u32[]{:S(2)}, u32[]{:S(2)}) collective-permute-start(f32[512,128]{1,0:T(8,128)S(1)} %get-tuple-element.52.refs_1_), channel_id=1, source_target_pairs={{4,0},{5,1},{6,2},{7,3},{8,12},{9,13},{10,14},{11,15},{20,16},{21,... | collective-permute-start | bytes 786440 | tf_op jit(solution)/shard_map/ppermute | solution.py:468
  47.1 1.1 %collective-permute-done.10.refs_6_ = f32[2272,128]{1,0:T(8,128)S(1)} collective-permute-done((f32[2272,128]{1,0:T(8,128)S(1)}, f32[2272,128]{1,0:T(8,128)S(1)}, u32[]{:S(2)}, u32[]{:S(2)}) %collective-permute-start.10) | collective-permute-done | bytes 1163296 | tf_op jit(solution)/shard_map/ppermute | solution.py:463
  48.2 7.3 %put_mid_multiply_1.1 = (bf16[8,512,512]{2,1,0:T(8,128)(2,1)S(1)}, bf16[8,512,512]{2,1,0:T(8,128)(2,1)S(1)}, f32[32,128]{1,0:T(8,128)S(1)}, f32[512,4096]{1,0:T(8,128)}) custom-call(s32[1]{0:T(128)} %bitcast.refs_0_, s32[54,32]{1,0:T(8,128)S(1)} %get-tuple-element.30.refs_1_, ...), custom_call_target="tpu_custom_call", output_to_operand_aliasing={{0}: (10, {}), {1}: (11, {}), {3}: (12, {})} | custom-call | tf_op jit(solution)/shard_map/put_mid_multiply_1/pallas_call | solution.py:81
  56.2 1.5 %collective-permute-done.13.refs_8_ = f32[512,128]{1,0:T(8,128)S(1)} collective-permute-done((f32[512,128]{1,0:T(8,128)S(1)}, f32[512,128]{1,0:T(8,128)S(1)}, u32[]{:S(2)}, u32[]{:S(2)}) %collective-permute-start.13) | collective-permute-done | bytes 262176 | tf_op jit(solution)/shard_map/ppermute | solution.py:463
  57.7 7.7 %put_side_mid_multiply_2.1 = (bf16[8,512,512]{2,1,0:T(8,128)(2,1)S(1)}, bf16[8,512,512]{2,1,0:T(8,128)(2,1)S(1)}, f32[32,128]{1,0:T(8,128)}, f32[512,4096]{1,0:T(8,128)}) custom-call(s32[1]{0:T(128)} %bitcast.refs_0_, s32[54,32]{1,0:T(8,128)S(1)} %get-tuple-element.30.refs_1_, ...), custom_call_target="tpu_custom_call", output_to_operand_aliasing={{0}: (12, {}), {1}: (13, {}), {3}: (14, {})} | custom-call | tf_op jit(solution)/shard_map/put_side_mid_multiply_2/pallas_call | solution.py:81
  (33 shorter events, 3.5 us)
Async XLA Ops:
  0.6 10.8 %collective-permute-start = (f32[128,2048]{1,0:T(8,128)}, f32[128,2048]{1,0:T(8,128)S(1)}, u32[]{:S(2)}, u32[]{:S(2)}) collective-permute-start(f32[128,2048]{1,0:T(8,128)} %refs_5_.1), channel_id=1, source_target_pairs={{0,1},{1,0},{2,3},{3,2},{4,5},{5,4},{6,7},{7,6},{8,9},{9,8},{10,11... | collective-permute-start | bytes 3145736 | tf_op jit(solution)/shard_map/ppermute | solution.py:463
  1.1 1.2 %copy-start = (f32[128,2048]{1,0:T(8,128)S(1)}, f32[128,2048]{1,0:T(8,128)}, u32[]{:S(2)}) copy-start(f32[128,2048]{1,0:T(8,128)} %refs_5_.1) | copy-start | bytes 3145732
  3.7 22.8 %collective-permute-start.1 = (f32[1696,128]{1,0:T(8,128)}, f32[1696,128]{1,0:T(8,128)S(1)}, u32[]{:S(2)}, u32[]{:S(2)}) collective-permute-start(f32[1696,128]{1,0:T(8,128)} %get-tuple-element.33), channel_id=1, source_target_pairs={{0,4},{1,5},{2,6},{3,7},{4,0},{5,1},{6,2},{7,3},{8,12},{9,13},{10,... | collective-permute-start | bytes 2605064 | tf_op jit(solution)/shard_map/ppermute | solution.py:463
  6.4 18.8 %collective-permute-start.2 = (f32[1440,128]{1,0:T(8,128)}, f32[1440,128]{1,0:T(8,128)S(1)}, u32[]{:S(2)}, u32[]{:S(2)}) collective-permute-start(f32[1440,128]{1,0:T(8,128)} %get-tuple-element.34.refs_2_), channel_id=1, source_target_pairs={{0,2},{1,3},{2,0},{3,1},{4,6},{5,7},{6,4},{7,5},{8,10},{9,11},{10,... | collective-permute-start | bytes 2211848 | tf_op jit(solution)/shard_map/ppermute | solution.py:463
  7.9 1.1 %copy-start.3 = (f32[1440,128]{1,0:T(8,128)S(1)}, f32[1440,128]{1,0:T(8,128)}, u32[]{:S(2)}) copy-start(f32[1440,128]{1,0:T(8,128)} %get-tuple-element.34.refs_2_) | copy-start | bytes 2211844
  10.0 12.4 %collective-permute-start.3 = (f32[928,128]{1,0:T(8,128)}, f32[928,128]{1,0:T(8,128)S(1)}, u32[]{:S(2)}, u32[]{:S(2)}) collective-permute-start(f32[928,128]{1,0:T(8,128)} %get-tuple-element.35), channel_id=1, source_target_pairs={{4,8},{5,9},{6,10},{7,11},{8,4},{9,5},{10,6},{11,7},{20,24},{21,25... | collective-permute-start | bytes 1425416 | tf_op jit(solution)/shard_map/ppermute | solution.py:468
  11.5 0.7 copy-start.6
  15.8 3.4 %copy-start.2 = (f32[512,4096]{1,0:T(8,128)S(1)}, f32[512,4096]{1,0:T(8,128)}, u32[]{:S(2)}) copy-start(f32[512,4096]{1,0:T(8,128)} %refs_0_.1) | copy-start | bytes 25165828
  19.2 1.3 %copy-start.1 = (f32[128,2048]{1,0:T(8,128)S(1)}, f32[128,2048]{1,0:T(8,128)}, u32[]{:S(2)}) copy-start(f32[128,2048]{1,0:T(8,128)} %refs_5_.1) | copy-start | bytes 3145732
  19.2 1.3 %copy-start.5 = (s32[1,8]{1,0:T(1,128)S(1)}, s32[1,8]{1,0:T(1,128)}, u32[]{:S(2)}) copy-start(s32[1,8]{1,0:T(1,128)} %refs_4_.7) | copy-start | bytes 100
  22.4 8.2 %copy-start.7 = (f32[160,128]{1,0:T(8,128)S(1)}, f32[160,128]{1,0:T(8,128)}, u32[]{:S(2)}) copy-start(f32[160,128]{1,0:T(8,128)} %get-tuple-element.40) | copy-start | bytes 245764
  22.4 13.7 %copy-start.4 = (f32[4096]{0:T(1024)S(1)}, f32[4096]{0:T(1024)}, u32[]{:S(2)}) copy-start(f32[4096]{0:T(1024)} %param.10) | copy-start | bytes 49156
  26.7 9.3 %collective-permute-start.8 = (f32[3136,128]{1,0:T(8,128)S(1)}, f32[3136,128]{1,0:T(8,128)S(1)}, u32[]{:S(2)}, u32[]{:S(2)}) collective-permute-start(f32[3136,128]{1,0:T(8,128)S(1)} %get-tuple-element.42.refs_5_), channel_id=1, source_target_pairs={{0,1},{1,0},{2,3},{3,2},{4,5},{5,4},{6,7},{7,6},{8,9},{9,8},{10,11... | collective-permute-start | bytes 4816904 | tf_op jit(solution)/shard_map/ppermute | solution.py:463
  26.8 18.3 %collective-permute-start.7 = (f32[1184,128]{1,0:T(8,128)S(1)}, f32[1184,128]{1,0:T(8,128)S(1)}, u32[]{:S(2)}, u32[]{:S(2)}) collective-permute-start(f32[1184,128]{1,0:T(8,128)S(1)} %get-tuple-element.41), channel_id=1, source_target_pairs={{0,2},{1,3},{2,0},{3,1},{4,6},{5,7},{6,4},{7,5},{8,10},{9,11},{10,... | collective-permute-start | bytes 1818632 | tf_op jit(solution)/shard_map/ppermute | solution.py:463
  28.6 16.6 %collective-permute-start.4 = (f32[928,128]{1,0:T(8,128)S(1)}, f32[928,128]{1,0:T(8,128)S(1)}, u32[]{:S(2)}, u32[]{:S(2)}) collective-permute-start(f32[928,128]{1,0:T(8,128)S(1)} %get-tuple-element.38.refs_1_), channel_id=1, source_target_pairs={{4,0},{5,1},{6,2},{7,3},{8,12},{9,13},{10,14},{11,15},{20,16},{21,... | collective-permute-start | bytes 1425416 | tf_op jit(solution)/shard_map/ppermute | solution.py:468
  29.8 14.2 %collective-permute-start.5 = (f32[672,128]{1,0:T(8,128)S(1)}, f32[672,128]{1,0:T(8,128)S(1)}, u32[]{:S(2)}, u32[]{:S(2)}) collective-permute-start(f32[672,128]{1,0:T(8,128)S(1)} %get-tuple-element.39), channel_id=1, source_target_pairs={{4,8},{5,9},{6,10},{7,11},{8,4},{9,5},{10,6},{11,7},{20,24},{21,25... | collective-permute-start | bytes 1032200 | tf_op jit(solution)/shard_map/ppermute | solution.py:468
  30.5 13.5 %collective-permute-start.6 = (f32[160,128]{1,0:T(8,128)S(1)}, f32[160,128]{1,0:T(8,128)S(1)}, u32[]{:S(2)}, u32[]{:S(2)}) collective-permute-start(f32[160,128]{1,0:T(8,128)S(1)} %copy-done.7), channel_id=1, source_target_pairs={{0,12},{1,13},{2,14},{3,15},{12,0},{13,1},{14,2},{15,3},{16,28},{1... | collective-permute-start | bytes 245768 | tf_op jit(solution)/shard_map/ppermute | solution.py:468
  45.4 2.9 %collective-permute-start.10 = (f32[2272,128]{1,0:T(8,128)S(1)}, f32[2272,128]{1,0:T(8,128)S(1)}, u32[]{:S(2)}, u32[]{:S(2)}) collective-permute-start(f32[2272,128]{1,0:T(8,128)S(1)} %get-tuple-element.47.refs_5_), channel_id=1, source_target_pairs={{0,1},{1,0},{2,3},{3,2},{4,5},{5,4},{6,7},{7,6},{8,9},{9,8},{10,11... | collective-permute-start | bytes 3489800 | tf_op jit(solution)/shard_map/ppermute | solution.py:463
  45.4 10.1 %collective-permute-start.9 = (f32[640,128]{1,0:T(8,128)S(1)}, f32[640,128]{1,0:T(8,128)S(1)}, u32[]{:S(2)}, u32[]{:S(2)}) collective-permute-start(f32[640,128]{1,0:T(8,128)S(1)} %get-tuple-element.46), channel_id=1, source_target_pairs={{0,2},{1,3},{2,0},{3,1},{4,6},{5,7},{6,4},{7,5},{8,10},{9,11},{10,... | collective-permute-start | bytes 983048 | tf_op jit(solution)/shard_map/ppermute | solution.py:463
  45.8 10.3 %collective-permute-start.12 = (f32[512,128]{1,0:T(8,128)S(1)}, f32[512,128]{1,0:T(8,128)S(1)}, u32[]{:S(2)}, u32[]{:S(2)}) collective-permute-start(f32[512,128]{1,0:T(8,128)S(1)} %get-tuple-element.52.refs_1_), channel_id=1, source_target_pairs={{4,0},{5,1},{6,2},{7,3},{8,12},{9,13},{10,14},{11,15},{20,16},{21,... | collective-permute-start | bytes 786440 | tf_op jit(solution)/shard_map/ppermute | solution.py:468
  55.6 2.2 %collective-permute-start.11 = (f32[640,128]{1,0:T(8,128)S(1)}, f32[640,128]{1,0:T(8,128)S(1)}, u32[]{:S(2)}, u32[]{:S(2)}) collective-permute-start(f32[640,128]{1,0:T(8,128)S(1)} %hold.1.refs_4_.refs_5_), channel_id=1, source_target_pairs={{0,1},{1,0},{2,3},{3,2},{4,5},{5,4},{6,7},{7,6},{8,9},{9,8},{10,11... | collective-permute-start | bytes 983048 | tf_op jit(solution)/shard_map/ppermute | solution.py:463
  56.1 1.6 %collective-permute-start.13 = (f32[512,128]{1,0:T(8,128)S(1)}, f32[512,128]{1,0:T(8,128)S(1)}, u32[]{:S(2)}, u32[]{:S(2)}) collective-permute-start(f32[512,128]{1,0:T(8,128)S(1)} %turn_3.1.refs_7_), channel_id=1, source_target_pairs={{0,1},{1,0},{2,3},{3,2},{4,5},{5,4},{6,7},{7,6},{8,9},{9,8},{10,11... | collective-permute-start | bytes 786440 | tf_op jit(solution)/shard_map/ppermute | solution.py:463
